TPU v7x, 128 devices: a whole 4x4x4 slice. The times are simulated.
128 devices in a mesh: group: 8 (over y, core), dev: 16 (over z, x).
Axes of the slice: x: 4, y: 4, z: 4, core: 2. Of those that a mesh axis runs over, the one named last changes fastest.
Arguments:
- queries: bfloat16 [3072, 1024], P(('group', 'dev')), may hold values from -12 to 12
- keys: bfloat16 [512, 256, 1024], P(('group', 'dev')), may hold values from -12 to 12
- values: bfloat16 [512, 256, 1024], P(('group', 'dev')), may hold values from -6 to 6
- frame_slot: int32 [512], replicated, may hold values from 0 to 511, each once
- covisible: int32 [12, 160], replicated, may hold values from 0 to 511, as said below
- counts: int32 [12], replicated, may hold values from 16 to 160
- out_weight: bfloat16 [1024, 1024], replicated, may hold values from -0.1875 to 0.1875
Outputs:
- projected: bfloat16 [3072, 1024], P(('group', 'dev'))
Inputs may be any that keep to these rules, and one draw needn't show every extreme that they name: `covisible`: each row lists 160 different frame numbers; query frame q attends to the first counts[q] of them. `frame_slot`: every frame is held at exactly one storage row.
All inputs are finite; a program needn't handle non-finite values.
Results may differ from a plain program's by a relative error of at most 0.02.
Values may be sent and summed in bfloat16 or wider, within the bound.
No kernel may reach another device: no remote copies, remote signals or barrier semaphores. Data moves between devices by JAX's collectives and lax.ppermute only.
A program may use at most 192 MiB of HBM per device.

v0:
```python
import itertools

import jax
import jax.numpy as jnp
from jax import lax
from jax.experimental import pallas as pl
from jax.experimental.pallas import tpu as pltpu
from jax.sharding import Mesh, PartitionSpec as P

HD = 64
LOG2E = 1.4426950408889634
TOP_STEP = 16.0
NO_TOP = -32768.0
CHIPS = ("y", "z", "x")
ALL = ("y", "core", "z", "x")
F32 = jnp.float32
BF16 = jnp.bfloat16


def attend_kernel(
    me, cnt, lst, q0, q1, q2, q3, k0, k1, v0, v1, out, pq, pj, k, vt, qm, acc, sa, sb, ta, tb, ha, hb, yb, sem
):
    copies = [
        pltpu.make_async_copy(src, dst, sem.at[i])
        for i, (src, dst) in enumerate(
            [(k0, k.at[pl.ds(0, 4)]), (k1, k.at[pl.ds(4, 4)]), (v0, vt.at[pl.ds(0, 4)]), (v1, vt.at[pl.ds(4, 4)])]
        )
    ]
    for copy in copies:
        copy.start()
    my_y, my_core, my_z, my_x = me[0], me[1], me[2], me[3]
    scale = HD ** -0.5 * LOG2E
    ones = jnp.ones((16, 256), BF16)

    def list_frame(qi, at):
        n = cnt[qi]

        def put(i, at):
            pj[at] = lst[qi * 8 + i]
            pq[at] = qi
            return at + 1

        return lax.fori_loop(0, n, put, at)

    total = lax.fori_loop(0, 12, list_frame, 0)
    for u in range(3):
        pq[total + u] = 12
        pj[total + u] = 0

    for r3, q in enumerate((q0, q1, q2, q3)):

        def load(r2, _, q=q, r3=r3):
            y = (my_y + 4 - jnp.where(my_core == 0, r2, r3)) % 4
            x = (my_x + 4 - jnp.where(my_core == 0, r3, r2)) % 4
            for rz in range(4):
                z = (my_z + 4 - rz) % 4
                block = q[r2 * 4 + rz].astype(F32)
                for c in range(2):
                    row = pl.multiple_of(y * 768 + (c * 16 + z * 4 + x) * 24, 8)
                    yb[pl.ds(row, 24), :512] = block[c * 24:(c + 1) * 24]
            return 0

        lax.fori_loop(0, 4, load, 0)

    def turn(qi, _):
        rows = pl.ds(pl.multiple_of(qi * 256, 256), 256)
        for hp in range(4):
            turned = yb[rows, hp * 128:(hp + 1) * 128].T.astype(BF16)
            zero = jnp.zeros((64, 256), BF16)
            qm[qi, 2 * hp] = jnp.concatenate([turned[:64], zero], axis=0)
            qm[qi, 2 * hp + 1] = jnp.concatenate([zero, turned[64:]], axis=0)

        @pl.when(cnt[qi] == 0)
        def _():
            yb[rows, 0:512] = jnp.zeros((256, 512), F32)
            lane = lax.broadcasted_iota(jnp.int32, (256, 128), 1)
            yb[rows, 512:640] = jnp.where(lane < 8, NO_TOP, 0.0)

        return 0

    lax.fori_loop(0, 12, turn, 0)
    for copy in copies:
        copy.wait()
    acc[...] = jnp.zeros_like(acc)
    ta[...] = jnp.full_like(ta, NO_TOP)
    tb[...] = jnp.full_like(tb, NO_TOP)
    qm[12] = jnp.zeros((8, 128, 256), BF16)

    def score(t, h, s_ref):
        qi, j = pq[t], pj[t]
        hp = h // 2
        keys = k[j, :, hp * 128:(hp + 1) * 128]
        s = jnp.dot(keys, qm[qi, h], preferred_element_type=F32) * scale
        s_ref[h] = s
        return jnp.max(s, axis=0, keepdims=True)

    def settle(t, highs, old_ref, new_ref, shrink_ref):
        first = pq[t] != pq[jnp.maximum(t - 1, 0)]
        old = jnp.where(first, NO_TOP, old_ref[...])
        high = jnp.concatenate(highs, axis=0)
        new = jnp.maximum(old, jnp.ceil(high * (1.0 / TOP_STEP)) * TOP_STEP)
        new_ref[...] = new
        shrink_ref[...] = jnp.exp2(old - new)

    def weigh(t, h, s_ref, top, shrink):
        j = pj[t]
        weights = jnp.exp2(s_ref[h] - top[h:h + 1]).astype(BF16)
        vals = jnp.concatenate([vt[j, h * 64:(h + 1) * 64, :], ones], axis=0)
        part = jnp.dot(vals, weights, preferred_element_type=F32)
        acc[h] = acc[h] * shrink[h:h + 1] + part

    def finish(t, top_ref):
        qi = pq[t]

        @pl.when((qi < 12) & (pq[t + 1] != qi))
        def _():
            rows = pl.ds(pl.multiple_of(qi * 256, 256), 256)
            totals = jnp.concatenate([acc[h, 64:65, :] for h in range(8)], axis=0)
            hi = totals.astype(BF16).astype(F32)
            extra = jnp.concatenate([top_ref[...], hi, totals - hi, jnp.zeros((104, 256), F32)], axis=0)
            for hp in range(4):
                both = jnp.concatenate([acc[2 * hp, :64, :], acc[2 * hp + 1, :64, :]], axis=0)
                yb[rows, hp * 128:(hp + 1) * 128] = both.T
            yb[rows, 512:640] = extra.T

    def half(t, s_now, s_next, t_now, t_next, h_now, h_next):
        top, shrink = t_now[...], h_now[...]
        highs = []
        for h in range(8):
            highs.append(score(t + 1, h, s_next))
            weigh(t, h, s_now, top, shrink)
        settle(t + 1, highs, t_now, t_next, h_next)
        finish(t, t_now)

    settle(0, [score(0, h, sa) for h in range(8)], tb, ta, ha)

    def two(u, _):
        half(2 * u, sa, sb, ta, tb, ha, hb)
        half(2 * u + 1, sb, sa, tb, ta, hb, ha)
        return 0

    lax.fori_loop(0, (total + 1) // 2, two, 0)

    def emit(y, _):
        for zx in range(16):
            data, packed = [], [jnp.zeros((8, 128), F32)] * 2
            for c in range(2):
                row = pl.multiple_of(y * 768 + (c * 16 + zx) * 24, 8)
                block = yb[pl.ds(row, 24), :]
                data.append(block[:, :512])
                for p in range(3):
                    g = c * 3 + p
                    piece = block[p * 8:(p + 1) * 8, 512:640]
                    if g % 4:
                        piece = pltpu.roll(piece, 32 * (g % 4), 1)
                    packed[g // 4] = packed[g // 4] + piece
            tail = jnp.concatenate(packed + [jnp.zeros((8, 256), F32)], axis=1)
            out[y * 16 + zx] = jnp.concatenate(data + [tail], axis=0).astype(BF16)
        return 0

    lax.fori_loop(0, 4, emit, 0)


def attend(me, cnt, lst, q, k0, k1, v0, v1):
    vmem = pl.BlockSpec(memory_space=pltpu.VMEM)
    smem = pl.BlockSpec(memory_space=pltpu.SMEM)
    whole = pl.BlockSpec(memory_space=pl.ANY)
    return pl.pallas_call(
        attend_kernel,
        out_shape=jax.ShapeDtypeStruct((64, 56, 512), BF16),
        in_specs=[smem] * 3 + [vmem] * 4 + [whole] * 4,
        out_specs=vmem,
        scratch_shapes=[
            pltpu.SMEM((104,), jnp.int32),
            pltpu.SMEM((104,), jnp.int32),
            pltpu.VMEM((8, 256, 512), BF16),
            pltpu.VMEM((8, 512, 256), BF16),
            pltpu.VMEM((13, 8, 128, 256), BF16),
            pltpu.VMEM((8, 80, 256), F32),
            pltpu.VMEM((8, 256, 256), F32),
            pltpu.VMEM((8, 256, 256), F32),
            pltpu.VMEM((8, 256), F32),
            pltpu.VMEM((8, 256), F32),
            pltpu.VMEM((8, 256), F32),
            pltpu.VMEM((8, 256), F32),
            pltpu.VMEM((3072, 640), F32),
            pltpu.SemaphoreType.DMA((4,)),
        ],
        compiler_params=pltpu.CompilerParams(vmem_limit_bytes=52 * 2**20),
        name="attend",
    )(me, cnt, lst, *q, k0, k1, v0, v1)


def combine_kernel(r, out, fs):
    n = r.shape[0]

    def find(s, best):
        for u in range(16):
            best = jnp.maximum(best, r[s * 16 + u, 48:56, 0:256].astype(F32))
        return best

    best = lax.fori_loop(0, n // 16, find, jnp.full((8, 256), NO_TOP, F32))

    def weigh(s, total):
        for u in range(16):
            e = r[s * 16 + u, 48:56, 0:256].astype(F32)
            f = jnp.exp2(jnp.minimum(e - best, 0.0))
            fs[pl.ds(pl.multiple_of((s * 16 + u) * 8, 8), 8), :] = f
            hl = [
                pltpu.roll(e[:, t * 128:(t + 1) * 128], 120, 1) + pltpu.roll(e[:, t * 128:(t + 1) * 128], 112, 1)
                for t in range(2)
            ]
            total = total + f * jnp.concatenate(hl, axis=1)
        return total

    total = lax.fori_loop(0, n // 16, weigh, jnp.zeros((8, 256), F32))
    src = lax.broadcasted_iota(jnp.int32, (128, 512), 0)
    dst = lax.broadcasted_iota(jnp.int32, (128, 512), 1) // 64
    spreads = [(src - 32 * g == dst).astype(BF16) for g in range(4)]

    def add(s8, numer):
        f = fs[pl.ds(pl.multiple_of(s8 * 64, 64), 64), :].astype(BF16)
        numer = list(numer)
        for g in range(6):
            t = g // 4
            wide = jnp.dot(f[:, t * 128:(t + 1) * 128], spreads[g % 4], preferred_element_type=F32)
            for u in range(8):
                numer[g] = numer[g] + wide[u * 8:(u + 1) * 8] * r[s8 * 8 + u, g * 8:(g + 1) * 8, :].astype(F32)
        return tuple(numer)

    numer = lax.fori_loop(0, n // 8, add, tuple(jnp.zeros((8, 512), F32) for _ in range(6)))
    for g in range(6):
        t = g // 4
        wide = jnp.dot(
            total[:, t * 128:(t + 1) * 128],
            spreads[g % 4].astype(F32),
            precision=lax.Precision.HIGHEST,
            preferred_element_type=F32,
        )
        out[g * 8:(g + 1) * 8, :] = numer[g] / wide


def combine(r):
    vmem = pl.BlockSpec(memory_space=pltpu.VMEM)
    return pl.pallas_call(
        combine_kernel,
        out_shape=jax.ShapeDtypeStruct((48, 512), F32),
        in_specs=[vmem],
        out_specs=vmem,
        scratch_shapes=[pltpu.VMEM((r.shape[0] * 8, 256), F32)],
        compiler_params=pltpu.CompilerParams(vmem_limit_bytes=32 * 2**20),
        name="combine",
    )(r)


def swap(x):
    return lax.ppermute(x, "core", [(0, 1), (1, 0)])


def shift(x, axes, by):
    pairs = []
    for y, c, z, w in itertools.product(range(4), range(2), range(4), range(4)):
        to = {"y": y, "z": z, "x": w}
        to[axes[c]] = (to[axes[c]] + by) % 4
        pairs.append((((y * 2 + c) * 4 + z) * 4 + w, ((to["y"] * 2 + c) * 4 + to["z"]) * 4 + to["x"]))
    return lax.ppermute(x, ALL, pairs)


def ring(x, axes):
    return [x] + [shift(x, axes, by) for by in (1, 2, 3)]


def body(queries, keys, values, frame_slot, covisible, counts, out_weight):
    core = lax.axis_index("core")
    device = lax.axis_index(ALL)
    partner = device + 16 - 32 * core
    own_col = core * 512
    other_col = 512 - own_col

    mine = lax.dynamic_slice_in_dim(queries, own_col, 512, 1)
    theirs = swap(lax.dynamic_slice_in_dim(queries, other_col, 512, 1))
    first = core == 0
    pair = jnp.concatenate([jnp.where(first, mine, theirs), jnp.where(first, theirs, mine)], axis=0)
    along_z = jnp.concatenate(ring(pair[None], "zz"), axis=0)
    plane = jnp.concatenate(ring(along_z, "yx"), axis=0)
    q_all = ring(plane, "xy")

    k_mine = lax.dynamic_slice_in_dim(keys, own_col, 512, 2)
    k_theirs = swap(lax.dynamic_slice_in_dim(keys, other_col, 512, 2))
    v_turned = jnp.swapaxes(values, 1, 2)
    v_mine = lax.dynamic_slice_in_dim(v_turned, own_col, 512, 1)
    v_theirs = swap(lax.dynamic_slice_in_dim(v_turned, other_col, 512, 1))

    four = jnp.arange(4, dtype=jnp.int32)
    slots = jnp.concatenate([device * 4 + four, partner * 4 + four])
    frame_ids = jnp.arange(frame_slot.shape[0], dtype=jnp.int32)
    local = jnp.sum(jnp.where(frame_slot[None, :] == slots[:, None], frame_ids[None, :], 0), axis=1)
    used = jnp.arange(covisible.shape[1], dtype=jnp.int32)[None, :] < counts[:, None]
    need = jnp.any((covisible[:, None, :] == local[None, :, None]) & used[:, None, :], axis=2)
    need_i = need.astype(jnp.int32)
    place = jnp.cumsum(need_i, axis=1) - need_i
    eight = jnp.arange(8, dtype=jnp.int32)
    hit = need[:, None, :] & (place[:, None, :] == eight[None, :, None])
    lst = jnp.sum(jnp.where(hit, eight[None, None, :], 0), axis=2).reshape(96)
    cnt = jnp.sum(need_i, axis=1)

    me = jnp.stack([lax.axis_index(a) for a in ALL]).astype(jnp.int32)
    sent = attend(me, cnt, lst, q_all, k_mine, k_theirs, v_mine, v_theirs)
    got = lax.all_to_all(sent, CHIPS, 0, 0)
    attended = combine(got).astype(BF16)

    keep = lax.dynamic_slice_in_dim(attended, core * 24, 24, 0)
    give = swap(lax.dynamic_slice_in_dim(attended, 24 - core * 24, 24, 0))
    rows = jnp.concatenate([jnp.where(first, keep, give), jnp.where(first, give, keep)], axis=1)
    return jnp.dot(rows, out_weight, preferred_element_type=F32).astype(BF16)


def solution(mesh):
    fine = Mesh(mesh.devices.reshape(4, 2, 4, 4), ALL)
    return jax.shard_map(
        body,
        mesh=fine,
        in_specs=(P(ALL, None), P(ALL, None, None), P(ALL, None, None), P(), P(), P(), P()),
        out_specs=P(ALL, None),
        check_vma=False,
    )
```

profile of v0, /device:TPU:1, one launch (start us, length us, event | category | flops | bytes accessed | tf_op | source)
XLA Modules:
  0.0 138.0 jit_solution(10642313752177583367)
XLA Ops:
  0.9 1.4 %collective-permute-start = (bf16[24,512]{1,0:T(8,128)(2,1)S(1)}, bf16[24,512]{1,0:T(8,128)(2,1)S(1)}, u32[]{:S(2)}, u32[]{:S(2)}) collective-permute-start(bf16[24,512]{1,0:T(8,128)(2,1)S(1)} %constant_dynamic-slice_fusion.5), channel_id=1, source_target_pairs={{0,16},{16,0},{1,17},{17,1},{2,18},{18,2},{3,19},{19,3},{4,20},{20... | collective-permute-start | bytes 73736 | tf_op jit(solution)/shard_map/ppermute | solution.py:257
  2.3 2.7 %constant_dynamic-slice_fusion.1 = (bf16[4,256,512]{2,1,0:T(8,128)(2,1)S(1)}, bf16[4,256,512]{2,1,0:T(8,128)(2,1)}) fusion(bf16[4,256,1024]{2,1,0:T(8,128)(2,1)} %param.9, s32[]{:T(128)S(6)} %select_n.48, s32[]{:T(128)S(6)} %select_n.47), kind=kLoop, calls=%fused_computation.26 | loop fusion | bytes 4194312 | tf_op jit(solution)/shard_map/dynamic-slice.1
  5.0 1.3 copy.20
  6.3 3.1 %constant_dynamic-slice_fusion.3 = (bf16[4,256,512]{2,1,0:T(8,128)(2,1)}, bf16[4,256,512]{2,1,0:T(8,128)(2,1)}) fusion(bf16[4,256,1024]{2,1,0:T(8,128)(2,1)} %param.8, s32[]{:T(128)S(6)} %select_n.48, s32[]{:T(128)S(6)} %select_n.47), kind=kLoop, calls=%fused_computation.28 | loop fusion | bytes 4194312 | tf_op jit(solution)/shard_map/dynamic_slice | solution.py:289
  10.2 1.8 %collective-permute-start.1 = (bf16[1,48,512]{2,1,0:T(8,128)(2,1)S(1)}, bf16[1,48,512]{2,1,0:T(8,128)(2,1)S(1)}, u32[]{:S(2)}, u32[]{:S(2)}) collective-permute-start(bf16[1,48,512]{2,1,0:T(8,128)(2,1)S(1)} %maximum_bitcast_fusion), channel_id=1, source_target_pairs={{0,4},{1,5},{2,6},{3,7},{4,8},{5,9},{6,10},{7,11},{8,12},{9,13},{1... | collective-permute-start | bytes 147464 | tf_op jit(solution)/shard_map/ppermute | solution.py:266
  12.0 3.3 %collective-permute-start.2 = (bf16[1,48,512]{2,1,0:T(8,128)(2,1)S(1)}, bf16[1,48,512]{2,1,0:T(8,128)(2,1)S(1)}, u32[]{:S(2)}, u32[]{:S(2)}) collective-permute-start(bf16[1,48,512]{2,1,0:T(8,128)(2,1)S(1)} %maximum_bitcast_fusion), channel_id=1, source_target_pairs={{0,8},{1,9},{2,10},{3,11},{4,12},{5,13},{6,14},{7,15},{8,0},{9,1},... | collective-permute-start | bytes 147464 | tf_op jit(solution)/shard_map/ppermute | solution.py:266
  16.2 2.0 %collective-permute-done.2 = bf16[1,48,512]{2,1,0:T(8,128)(2,1)S(1)} collective-permute-done((bf16[1,48,512]{2,1,0:T(8,128)(2,1)S(1)}, bf16[1,48,512]{2,1,0:T(8,128)(2,1)S(1)}, u32[]{:S(2)}, u32[]{:S(2)}) %collective-permute-start.2) | collective-permute-done | bytes 49184 | tf_op jit(solution)/shard_map/ppermute | solution.py:266
  18.6 1.3 collective-permute-start.4
  19.8 2.5 %collective-permute-start.5 = (bf16[4,48,512]{2,1,0:T(8,128)(2,1)S(1)}, bf16[4,48,512]{2,1,0:T(8,128)(2,1)S(1)}, u32[]{:S(2)}, u32[]{:S(2)}) collective-permute-start(bf16[4,48,512]{2,1,0:T(8,128)(2,1)S(1)} %pad_maximum_fusion), channel_id=1, source_target_pairs={{0,64},{1,65},{2,66},{3,67},{4,68},{5,69},{6,70},{7,71},{8,72},{9,... | collective-permute-start | bytes 589832 | tf_op jit(solution)/shard_map/ppermute | solution.py:266
  22.3 1.2 collective-permute-start.6
  23.5 1.2 collective-permute-done.4
  24.7 2.8 %collective-permute-done.5 = bf16[4,48,512]{2,1,0:T(8,128)(2,1)S(1)} collective-permute-done((bf16[4,48,512]{2,1,0:T(8,128)(2,1)S(1)}, bf16[4,48,512]{2,1,0:T(8,128)(2,1)S(1)}, u32[]{:S(2)}, u32[]{:S(2)}) %collective-permute-start.5) | collective-permute-done | bytes 196640 | tf_op jit(solution)/shard_map/ppermute | solution.py:266
  27.5 1.4 collective-permute-start.7
  28.9 2.6 %collective-permute-start.8 = (bf16[16,48,512]{2,1,0:T(8,128)(2,1)S(1)}, bf16[16,48,512]{2,1,0:T(8,128)(2,1)}, u32[]{:S(2)}, u32[]{:S(2)}) collective-permute-start(bf16[16,48,512]{2,1,0:T(8,128)(2,1)S(1)} %constant_dynamic-update-slice_fusion.q0), channel_id=1, source_target_pairs={{0,2},{1,3},{2,0},{3,1},{4,6},{5,7},{6,4},{7,5},{8,10},{9,11},{10,... | collective-permute-start | bytes 2359304 | tf_op jit(solution)/shard_map/ppermute | solution.py:266
  31.5 1.1 collective-permute-start.9
  33.7 2.3 %copy.19 = bf16[4,256,512]{1,2,0:T(8,128)(2,1)} copy(bf16[4,256,512]{2,1,0:T(8,128)(2,1)} %get-tuple-element.6) | data formatting | bytes 2097152
  36.0 4.1 %collective-permute-done.7.q1 = bf16[16,48,512]{2,1,0:T(8,128)(2,1)} collective-permute-done((bf16[16,48,512]{2,1,0:T(8,128)(2,1)S(1)}, bf16[16,48,512]{2,1,0:T(8,128)(2,1)}, u32[]{:S(2)}, u32[]{:S(2)}) %collective-permute-start.7) | collective-permute-done | bytes 786464 | tf_op jit(solution)/shard_map/ppermute | solution.py:266
  40.1 9.6 %collective-permute-done.8.q2 = bf16[16,48,512]{2,1,0:T(8,128)(2,1)} collective-permute-done((bf16[16,48,512]{2,1,0:T(8,128)(2,1)S(1)}, bf16[16,48,512]{2,1,0:T(8,128)(2,1)}, u32[]{:S(2)}, u32[]{:S(2)}) %collective-permute-start.8) | collective-permute-done | bytes 786464 | tf_op jit(solution)/shard_map/ppermute | solution.py:266
  49.7 26.7 %attend.1 = bf16[64,56,512]{2,1,0:T(8,128)(2,1)} custom-call(s32[4]{0:T(128)S(1)} %pad_add_fusion.me, s32[12]{0:T(128)S(1)} %get-tuple-element.14.cnt, s32[96]{0:T(128)S(1)} %reshape.37.lst, bf16[16,48,512]{2,1,0:T(8,128)(2,1)S(1)} %constant_dynamic-update-slice_fusion.q0, bf16[16,48,512]{2,1,0:T(8,128)(2,1)} %collective-permute-done.7.q1, ...), custom_call_target="tpu_custom_call" | custom-call | tf_op jit(solution)/shard_map/attend/pallas_call | solution.py:168
  76.4 5.6 %all-to-all-start = ((bf16[64,56,512]{2,1,0:T(8,128)(2,1)}), bf16[64,56,512]{2,1,0:T(8,128)(2,1)}, u32[]{:S(2)}, u32[]{:S(2)}) async-start(bf16[64,56,512]{2,1,0:T(8,128)(2,1)} %attend.1), calls=%async_computation | async-start | bytes 7340032 | tf_op jit(solution)/shard_map/all_to_all | solution.py:309
  82.0 42.5 %all-to-all-done.r = bf16[64,56,512]{2,1,0:T(8,128)(2,1)} async-done(((bf16[64,56,512]{2,1,0:T(8,128)(2,1)}), bf16[64,56,512]{2,1,0:T(8,128)(2,1)}, u32[]{:S(2)}, u32[]{:S(2)}) %all-to-all-start) | async-done | bytes 3670048 | tf_op jit(solution)/shard_map/all_to_all | solution.py:309
  124.5 5.3 %combine.1 = f32[48,512]{1,0:T(8,128)S(1)} custom-call(bf16[64,56,512]{2,1,0:T(8,128)(2,1)} %all-to-all-done.r), custom_call_target="tpu_custom_call" | custom-call | tf_op jit(solution)/shard_map/combine/pallas_call | solution.py:245
  129.8 6.3 %collective-permute-start.12 = (bf16[24,512]{1,0:T(8,128)(2,1)S(1)}, bf16[24,512]{1,0:T(8,128)(2,1)S(1)}, u32[]{:S(2)}, u32[]{:S(2)}) collective-permute-start(bf16[24,512]{1,0:T(8,128)(2,1)S(1)} %constant_dynamic-slice_fusion), channel_id=1, source_target_pairs={{0,16},{16,0},{1,17},{17,1},{2,18},{18,2},{3,19},{19,3},{4,20},{20... | collective-permute-start | bytes 73736 | tf_op jit(solution)/shard_map/ppermute | solution.py:257
  137.0 1.0 convolution_convert_fusion
  (49 shorter events, 5.0 us)
Async XLA Ops:
  0.0 137.0 %copy-start = (bf16[1024,1024]{1,0:T(8,128)(2,1)S(1)}, bf16[1024,1024]{1,0:T(8,128)(2,1)}, u32[]{:S(2)}) copy-start(bf16[1024,1024]{1,0:T(8,128)(2,1)} %param.13) | copy-start | bytes 6291460
  0.9 9.3 %collective-permute-start = (bf16[24,512]{1,0:T(8,128)(2,1)S(1)}, bf16[24,512]{1,0:T(8,128)(2,1)S(1)}, u32[]{:S(2)}, u32[]{:S(2)}) collective-permute-start(bf16[24,512]{1,0:T(8,128)(2,1)S(1)} %constant_dynamic-slice_fusion.5), channel_id=1, source_target_pairs={{0,16},{16,0},{1,17},{17,1},{2,18},{18,2},{3,19},{19,3},{4,20},{20... | collective-permute-start | bytes 73736 | tf_op jit(solution)/shard_map/ppermute | solution.py:257
  6.3 3.6 %copy-start.3 = (s32[512]{0:T(512)S(1)}, s32[512]{0:T(512)}, u32[]{:S(2)}) copy-start(s32[512]{0:T(512)} %param.10) | copy-start | bytes 6148
  6.3 3.8 %copy-start.1 = (bf16[24,1024]{1,0:T(8,128)(2,1)S(1)}, bf16[24,1024]{1,0:T(8,128)(2,1)}, u32[]{:S(2)}) copy-start(bf16[24,1024]{1,0:T(8,128)(2,1)} %param.7) | copy-start | bytes 147460
  6.3 29.7 %collective-permute-start.11 = (bf16[4,512,256]{2,1,0:T(8,128)(2,1)}, bf16[4,512,256]{2,1,0:T(8,128)(2,1)}, u32[]{:S(2)}, u32[]{:S(2)}) collective-permute-start(bf16[4,512,256]{2,1,0:T(8,128)(2,1)} %bitcast.12), channel_id=1, source_target_pairs={{0,16},{16,0},{1,17},{17,1},{2,18},{18,2},{3,19},{19,3},{4,20},{20... | collective-permute-start | bytes 3145736 | tf_op jit(solution)/shard_map/ppermute | solution.py:257
  9.4 23.2 %copy-start.4 = (s32[12]{0:T(128)S(1)}, s32[12]{0:T(128)}, u32[]{:S(2)}) copy-start(s32[12]{0:T(128)} %param.12) | copy-start | bytes 148
  9.4 23.2 %copy-start.2 = (s32[12,160]{1,0:T(8,128)S(1)}, s32[12,160]{1,0:T(8,128)}, u32[]{:S(2)}) copy-start(s32[12,160]{1,0:T(8,128)} %param.11) | copy-start | bytes 23044
  9.4 26.6 %collective-permute-start.10 = (bf16[4,256,512]{2,1,0:T(8,128)(2,1)}, bf16[4,256,512]{2,1,0:T(8,128)(2,1)}, u32[]{:S(2)}, u32[]{:S(2)}) collective-permute-start(bf16[4,256,512]{2,1,0:T(8,128)(2,1)} %get-tuple-element.7), channel_id=1, source_target_pairs={{0,16},{16,0},{1,17},{17,1},{2,18},{18,2},{3,19},{19,3},{4,20},{20... | collective-permute-start | bytes 3145736 | tf_op jit(solution)/shard_map/ppermute | solution.py:257
  10.2 6.0 %collective-permute-start.1 = (bf16[1,48,512]{2,1,0:T(8,128)(2,1)S(1)}, bf16[1,48,512]{2,1,0:T(8,128)(2,1)S(1)}, u32[]{:S(2)}, u32[]{:S(2)}) collective-permute-start(bf16[1,48,512]{2,1,0:T(8,128)(2,1)S(1)} %maximum_bitcast_fusion), channel_id=1, source_target_pairs={{0,4},{1,5},{2,6},{3,7},{4,8},{5,9},{6,10},{7,11},{8,12},{9,13},{1... | collective-permute-start | bytes 147464 | tf_op jit(solution)/shard_map/ppermute | solution.py:266
  12.0 6.2 %collective-permute-start.2 = (bf16[1,48,512]{2,1,0:T(8,128)(2,1)S(1)}, bf16[1,48,512]{2,1,0:T(8,128)(2,1)S(1)}, u32[]{:S(2)}, u32[]{:S(2)}) collective-permute-start(bf16[1,48,512]{2,1,0:T(8,128)(2,1)S(1)} %maximum_bitcast_fusion), channel_id=1, source_target_pairs={{0,8},{1,9},{2,10},{3,11},{4,12},{5,13},{6,14},{7,15},{8,0},{9,1},... | collective-permute-start | bytes 147464 | tf_op jit(solution)/shard_map/ppermute | solution.py:266
  15.3 3.2 %collective-permute-start.3 = (bf16[1,48,512]{2,1,0:T(8,128)(2,1)S(1)}, bf16[1,48,512]{2,1,0:T(8,128)(2,1)S(1)}, u32[]{:S(2)}, u32[]{:S(2)}) collective-permute-start(bf16[1,48,512]{2,1,0:T(8,128)(2,1)S(1)} %maximum_bitcast_fusion), channel_id=1, source_target_pairs={{0,12},{1,13},{2,14},{3,15},{4,0},{5,1},{6,2},{7,3},{8,4},{9,5},{1... | collective-permute-start | bytes 147464 | tf_op jit(solution)/shard_map/ppermute | solution.py:266
  18.6 6.1 %collective-permute-start.4 = (bf16[4,48,512]{2,1,0:T(8,128)(2,1)S(1)}, bf16[4,48,512]{2,1,0:T(8,128)(2,1)S(1)}, u32[]{:S(2)}, u32[]{:S(2)}) collective-permute-start(bf16[4,48,512]{2,1,0:T(8,128)(2,1)S(1)} %pad_maximum_fusion), channel_id=1, source_target_pairs={{0,32},{1,33},{2,34},{3,35},{4,36},{5,37},{6,38},{7,39},{8,40},{9,... | collective-permute-start | bytes 589832 | tf_op jit(solution)/shard_map/ppermute | solution.py:266
  19.8 7.6 %collective-permute-start.5 = (bf16[4,48,512]{2,1,0:T(8,128)(2,1)S(1)}, bf16[4,48,512]{2,1,0:T(8,128)(2,1)S(1)}, u32[]{:S(2)}, u32[]{:S(2)}) collective-permute-start(bf16[4,48,512]{2,1,0:T(8,128)(2,1)S(1)} %pad_maximum_fusion), channel_id=1, source_target_pairs={{0,64},{1,65},{2,66},{3,67},{4,68},{5,69},{6,70},{7,71},{8,72},{9,... | collective-permute-start | bytes 589832 | tf_op jit(solution)/shard_map/ppermute | solution.py:266
  22.3 5.2 %collective-permute-start.6 = (bf16[4,48,512]{2,1,0:T(8,128)(2,1)S(1)}, bf16[4,48,512]{2,1,0:T(8,128)(2,1)S(1)}, u32[]{:S(2)}, u32[]{:S(2)}) collective-permute-start(bf16[4,48,512]{2,1,0:T(8,128)(2,1)S(1)} %pad_maximum_fusion), channel_id=1, source_target_pairs={{0,96},{1,97},{2,98},{3,99},{4,100},{5,101},{6,102},{7,103},{8,104... | collective-permute-start | bytes 589832 | tf_op jit(solution)/shard_map/ppermute | solution.py:266
  27.5 12.6 %collective-permute-start.7 = (bf16[16,48,512]{2,1,0:T(8,128)(2,1)S(1)}, bf16[16,48,512]{2,1,0:T(8,128)(2,1)}, u32[]{:S(2)}, u32[]{:S(2)}) collective-permute-start(bf16[16,48,512]{2,1,0:T(8,128)(2,1)S(1)} %constant_dynamic-update-slice_fusion.q0), channel_id=1, source_target_pairs={{0,1},{1,2},{2,3},{3,0},{4,5},{5,6},{6,7},{7,4},{8,9},{9,10},{10,1... | collective-permute-start | bytes 2359304 | tf_op jit(solution)/shard_map/ppermute | solution.py:266
  28.9 20.8 %collective-permute-start.8 = (bf16[16,48,512]{2,1,0:T(8,128)(2,1)S(1)}, bf16[16,48,512]{2,1,0:T(8,128)(2,1)}, u32[]{:S(2)}, u32[]{:S(2)}) collective-permute-start(bf16[16,48,512]{2,1,0:T(8,128)(2,1)S(1)} %constant_dynamic-update-slice_fusion.q0), channel_id=1, source_target_pairs={{0,2},{1,3},{2,0},{3,1},{4,6},{5,7},{6,4},{7,5},{8,10},{9,11},{10,... | collective-permute-start | bytes 2359304 | tf_op jit(solution)/shard_map/ppermute | solution.py:266
  31.5 18.2 %collective-permute-start.9 = (bf16[16,48,512]{2,1,0:T(8,128)(2,1)S(1)}, bf16[16,48,512]{2,1,0:T(8,128)(2,1)}, u32[]{:S(2)}, u32[]{:S(2)}) collective-permute-start(bf16[16,48,512]{2,1,0:T(8,128)(2,1)S(1)} %constant_dynamic-update-slice_fusion.q0), channel_id=1, source_target_pairs={{0,3},{1,0},{2,1},{3,2},{4,7},{5,4},{6,5},{7,6},{8,11},{9,8},{10,9... | collective-permute-start | bytes 2359304 | tf_op jit(solution)/shard_map/ppermute | solution.py:266
  76.4 48.1 %all-to-all-start = ((bf16[64,56,512]{2,1,0:T(8,128)(2,1)}), bf16[64,56,512]{2,1,0:T(8,128)(2,1)}, u32[]{:S(2)}, u32[]{:S(2)}) async-start(bf16[64,56,512]{2,1,0:T(8,128)(2,1)} %attend.1), calls=%async_computation | async-start | bytes 7340032 | tf_op jit(solution)/shard_map/all_to_all | solution.py:309
  129.8 7.1 %collective-permute-start.12 = (bf16[24,512]{1,0:T(8,128)(2,1)S(1)}, bf16[24,512]{1,0:T(8,128)(2,1)S(1)}, u32[]{:S(2)}, u32[]{:S(2)}) collective-permute-start(bf16[24,512]{1,0:T(8,128)(2,1)S(1)} %constant_dynamic-slice_fusion), channel_id=1, source_target_pairs={{0,16},{16,0},{1,17},{17,1},{2,18},{18,2},{3,19},{19,3},{4,20},{20... | collective-permute-start | bytes 73736 | tf_op jit(solution)/shard_map/ppermute | solution.py:257
where the time goes:
time: 140 us; the launch traced here: 138 us
  waiting for transfers between devices  63.5 us (45%)
  Pallas kernels  32 us (23%)
  starting transfers between devices  29.6 us (21%)
  local copies, waits for them, and re-layouts  10.7 us (8%)
    all_to_all x1, waiting for transfers between devices, body(): got = lax.all_to_all(sent, CHIPS, 0, 0)  42.5 us
    pallas_call x1, Pallas kernels, attend(): pl.pallas_call(attend_kernel, out_shape=jax.ShapeDtypeStruct((64, 56, 512...  26.7 us
    ppermute x9, waiting for transfers between devices, shift(): return lax.ppermute(x, ALL, pairs)  20.2 us
    ppermute x9, starting transfers between devices, shift(): return lax.ppermute(x, ALL, pairs)  15.8 us
    ppermute x4, starting transfers between devices, swap(): return lax.ppermute(x, 'core', [(0, 1), (1, 0)])  8.18 us
    all_to_all x1, starting transfers between devices, body(): got = lax.all_to_all(sent, CHIPS, 0, 0)  5.62 us
    pallas_call x1, Pallas kernels, combine(): pl.pallas_call(combine_kernel, out_shape=jax.ShapeDtypeStruct((48, 512),...  5.27 us
    unnamed x17, local copies, waits for them, and re-layouts  3.61 us
  transfers between devices with their start and end apart: 14, of which 9 were waited for; matrix products, arithmetic and copies ran while one was open for 8% of the time, Pallas kernels for 0%

commit v1 on v0

v1 whole, which is shorter than its diff:
```python
import functools
import itertools

import jax
import jax.numpy as jnp
from jax import lax
from jax.experimental import pallas as pl
from jax.experimental.pallas import tpu as pltpu
from jax.sharding import Mesh, PartitionSpec as P

HD = 64
LOG2E = 1.4426950408889634
TOP_STEP = 16.0
NO_TOP = -32768.0
NH = 4
WIDE = NH * HD
ALL = ("y", "core", "z", "x")
F32 = jnp.float32
BF16 = jnp.bfloat16


def attend_kernel(
    me, cnt, lst, q0, q1, q2, q3, k0, k1, v0, v1, o0, o1, o2, o3,
    pq, pj, k, vt, qm, acc, sa, sb, ta, tb, ha, hb, yb, sem, *, part,
):
    my_y, my_core, my_z, my_x = me[0], me[1], me[2], me[3]
    col = pl.multiple_of(my_core * 512 + part * WIDE, WIDE)
    copies = [
        pltpu.make_async_copy(src, dst, sem.at[i])
        for i, (src, dst) in enumerate(
            [
                (k0.at[:, :, pl.ds(col, WIDE)], k.at[pl.ds(0, 4)]),
                (k1.at[:, :, pl.ds(col, WIDE)], k.at[pl.ds(4, 4)]),
                (v0.at[:, pl.ds(col, WIDE), :], vt.at[pl.ds(0, 4)]),
                (v1.at[:, pl.ds(col, WIDE), :], vt.at[pl.ds(4, 4)]),
            ]
        )
    ]
    for copy in copies:
        copy.start()
    scale = HD ** -0.5 * LOG2E
    ones = jnp.ones((16, 256), BF16)

    def list_frame(qi, at):
        def put(i, at):
            pj[at] = lst[qi * 8 + i]
            pq[at] = qi
            return at + 1

        return lax.fori_loop(0, cnt[qi], put, at)

    total = lax.fori_loop(0, 12, list_frame, 0)
    for u in range(3):
        pq[total + u] = 12
        pj[total + u] = 0

    def place(r2, r3, rz):
        y = lax.rem(my_y + 4 - jnp.where(my_core == 0, r2, r3), 4)
        x = lax.rem(my_x + 4 - jnp.where(my_core == 0, r3, r2), 4)
        z = lax.rem(my_z + 4 - rz, 4)
        return [pl.multiple_of(y * 768 + (c * 16 + z * 4 + x) * 24, 8) for c in range(2)]

    for r3, q in enumerate((q0, q1, q2, q3)):

        def load(r2, _, q=q, r3=r3):
            for rz in range(4):
                block = q[r2 * 4 + rz].astype(F32)
                for c, row in enumerate(place(r2, r3, rz)):
                    yb[pl.ds(row, 24), :WIDE] = block[c * 24:(c + 1) * 24]
            return 0

        lax.fori_loop(0, 4, load, 0)

    def turn(qi, _):
        rows = pl.ds(pl.multiple_of(qi * 256, 256), 256)
        zero = jnp.zeros((64, 256), BF16)
        for hp in range(NH // 2):
            turned = yb[rows, hp * 128:(hp + 1) * 128].T.astype(BF16)
            qm[qi, 2 * hp] = jnp.concatenate([turned[:64], zero], axis=0)
            qm[qi, 2 * hp + 1] = jnp.concatenate([zero, turned[64:]], axis=0)

        @pl.when(cnt[qi] == 0)
        def _():
            yb[rows, :WIDE] = jnp.zeros((256, WIDE), F32)
            lane = lax.broadcasted_iota(jnp.int32, (256, 128), 1)
            yb[rows, WIDE:] = jnp.where(lane < NH, NO_TOP, 0.0)

        return 0

    lax.fori_loop(0, 12, turn, 0)
    for copy in copies:
        copy.wait()
    acc[...] = jnp.zeros_like(acc)
    ta[...] = jnp.full_like(ta, NO_TOP)
    tb[...] = jnp.full_like(tb, NO_TOP)
    qm[12] = jnp.zeros((NH, 128, 256), BF16)

    def score(t, h, s_ref):
        hp = h // 2
        keys = k[pj[t], :, hp * 128:(hp + 1) * 128]
        s = jnp.dot(keys, qm[pq[t], h], preferred_element_type=F32) * scale
        s_ref[h] = s
        return jnp.max(s, axis=0, keepdims=True)

    def settle(t, highs, old_ref, new_ref, shrink_ref):
        first = pq[t] != pq[jnp.maximum(t - 1, 0)]
        old = jnp.where(first, NO_TOP, old_ref[...])
        high = jnp.concatenate(highs, axis=0)
        new = jnp.maximum(old, jnp.ceil(high * (1.0 / TOP_STEP)) * TOP_STEP)
        new_ref[...] = new
        shrink_ref[...] = jnp.exp2(old - new)

    def weigh(t, h, s_ref, top, shrink):
        weights = jnp.exp2(s_ref[h] - top[h:h + 1]).astype(BF16)
        vals = jnp.concatenate([vt[pj[t], h * 64:(h + 1) * 64, :], ones], axis=0)
        part = jnp.dot(vals, weights, preferred_element_type=F32)
        acc[h] = acc[h] * shrink[h:h + 1] + part

    def finish(t, top_ref):
        qi = pq[t]

        @pl.when((qi < 12) & (pq[t + 1] != qi))
        def _():
            rows = pl.ds(pl.multiple_of(qi * 256, 256), 256)
            totals = jnp.concatenate([acc[h, 64:65, :] for h in range(NH)], axis=0)
            hi = totals.astype(BF16).astype(F32)
            extra = [top_ref[...], hi, totals - hi, jnp.zeros((128 - 3 * NH, 256), F32)]
            for hp in range(NH // 2):
                both = jnp.concatenate([acc[2 * hp, :64, :], acc[2 * hp + 1, :64, :]], axis=0)
                yb[rows, hp * 128:(hp + 1) * 128] = both.T
            yb[rows, WIDE:] = jnp.concatenate(extra, axis=0).T

    def half(t, s_now, s_next, t_now, t_next, h_now, h_next):
        top, shrink = t_now[...], h_now[...]
        highs = []
        for h in range(NH):
            highs.append(score(t + 1, h, s_next))
            weigh(t, h, s_now, top, shrink)
        settle(t + 1, highs, t_now, t_next, h_next)
        finish(t, t_now)

    settle(0, [score(0, h, sa) for h in range(NH)], tb, ta, ha)

    def two(u, _):
        half(2 * u, sa, sb, ta, tb, ha, hb)
        half(2 * u + 1, sb, sa, tb, ta, hb, ha)
        return 0

    lax.fori_loop(0, (total + 1) // 2, two, 0)

    for r3, o in enumerate((o0, o1, o2, o3)):

        def emit(r2, _, o=o, r3=r3):
            for rz in range(4):
                data, tail = [], jnp.zeros((8, 128), F32)
                for c, row in enumerate(place(r2, r3, rz)):
                    block = yb[pl.ds(row, 24), :]
                    data.append(block[:, :WIDE])
                    for p in range(3):
                        piece = block[p * 8:(p + 1) * 8, WIDE:]
                        g = c * 3 + p
                        tail = tail + (pltpu.roll(piece, 16 * g, 1) if g else piece)
                data.append(jnp.concatenate([tail, jnp.zeros((8, WIDE - 128), F32)], axis=1))
                o[r2 * 4 + rz] = jnp.concatenate(data, axis=0).astype(BF16)
            return 0

        lax.fori_loop(0, 4, emit, 0)


def attend(me, cnt, lst, q, k0, k1, v0, v1, part):
    vmem = pl.BlockSpec(memory_space=pltpu.VMEM)
    smem = pl.BlockSpec(memory_space=pltpu.SMEM)
    whole = pl.BlockSpec(memory_space=pl.ANY)
    return pl.pallas_call(
        functools.partial(attend_kernel, part=part),
        out_shape=[jax.ShapeDtypeStruct((16, 56, WIDE), BF16)] * 4,
        in_specs=[smem] * 3 + [vmem] * 4 + [whole] * 4,
        out_specs=[vmem] * 4,
        scratch_shapes=[
            pltpu.SMEM((104,), jnp.int32),
            pltpu.SMEM((104,), jnp.int32),
            pltpu.VMEM((8, 256, WIDE), BF16),
            pltpu.VMEM((8, WIDE, 256), BF16),
            pltpu.VMEM((13, NH, 128, 256), BF16),
            pltpu.VMEM((NH, 80, 256), F32),
            pltpu.VMEM((NH, 256, 256), F32),
            pltpu.VMEM((NH, 256, 256), F32),
            pltpu.VMEM((NH, 256), F32),
            pltpu.VMEM((NH, 256), F32),
            pltpu.VMEM((NH, 256), F32),
            pltpu.VMEM((NH, 256), F32),
            pltpu.VMEM((3072, WIDE + 128), F32),
            pltpu.SemaphoreType.DMA((4,)),
        ],
        compiler_params=pltpu.CompilerParams(vmem_limit_bytes=36 * 2**20),
        cost_estimate=pl.CostEstimate(flops=10**10, bytes_accessed=2**23, transcendentals=2 * 10**7),
        name="attend",
    )(me, cnt, lst, *q, k0, k1, v0, v1)


def pack_kernel(p0, p1, p2, p3, k, v, o0, o1):
    for at, p in enumerate((p0, p1, p2, p3)):
        for c, o in enumerate((o0, o1)):
            o[at * 4:at * 4 + 4] = p[:, :, c * WIDE:(c + 1) * WIDE]


def pack(parts, k, v):
    vmem = pl.BlockSpec(memory_space=pltpu.VMEM)
    whole = pl.BlockSpec(memory_space=pl.ANY)
    return pl.pallas_call(
        pack_kernel,
        out_shape=[jax.ShapeDtypeStruct((16, 48, WIDE), BF16)] * 2,
        in_specs=[vmem] * 4 + [whole] * 2,
        out_specs=[vmem] * 2,
        name="pack",
    )(*parts, k, v)


def add_up(parts, spread):
    tails = [p[48:56, :128].astype(F32) for p in parts]
    best = functools.reduce(jnp.maximum, tails)
    shares = [jnp.exp2(jnp.minimum(t - best, 0.0)) for t in tails]
    total = sum(f * (pltpu.roll(t, 128 - NH, 1) + pltpu.roll(t, 128 - 2 * NH, 1)) for f, t in zip(shares, tails))
    stack = jnp.concatenate(shares, axis=0)
    stack = jnp.concatenate([stack] + [pltpu.roll(stack, 128 - 16 * g, 1) for g in range(1, 6)], axis=0)
    wide = jnp.dot(stack.astype(BF16), spread, preferred_element_type=F32)
    numer = []
    for g in range(6):
        at = g * 8 * len(parts)
        numer.append(
            sum(wide[at + s * 8:at + s * 8 + 8] * p[g * 8:g * 8 + 8, :].astype(F32) for s, p in enumerate(parts))
        )
    return numer, best, total


def make_spread():
    src = lax.broadcasted_iota(jnp.int32, (128, WIDE), 0)
    dst = lax.broadcasted_iota(jnp.int32, (128, WIDE), 1) // HD
    return src == dst


def merge_kernel(*refs, joint, blocks):
    parts, outs = refs[:-4], refs[-4:]
    spread = make_spread().astype(BF16)
    is_top = lax.broadcasted_iota(jnp.int32, (8, 128), 1) % 16 < NH
    for r, out in enumerate(outs):

        def one(b, _, r=r, out=out):
            for c in range(2):
                if joint:
                    held = [p[(r * blocks + b) * 2 + c] for p in parts]
                else:
                    held = [p[r * blocks + b] for p in parts[c * 4:c * 4 + 4]]
                numer, best, total = add_up(held, spread)
                total = jnp.where(is_top, total, 0.0)
                hi = total.astype(BF16).astype(F32)
                tail = jnp.where(is_top, best, 0.0) + pltpu.roll(hi, NH, 1) + pltpu.roll(total - hi, 2 * NH, 1)
                tail = jnp.concatenate([tail, jnp.zeros((8, WIDE - 128), F32)], axis=1)
                out[b * 2 + c] = jnp.concatenate(numer + [tail], axis=0).astype(BF16)
            return 0

        lax.fori_loop(0, blocks, one, 0)


def merge(parts, blocks):
    vmem = pl.BlockSpec(memory_space=pltpu.VMEM)
    return pl.pallas_call(
        functools.partial(merge_kernel, joint=len(parts) == 4, blocks=blocks),
        out_shape=[jax.ShapeDtypeStruct((blocks * 2, 56, WIDE), BF16)] * 4,
        in_specs=[vmem] * len(parts),
        out_specs=[vmem] * 4,
        compiler_params=pltpu.CompilerParams(vmem_limit_bytes=32 * 2**20),
        name="merge",
    )(*parts)


def close_kernel(*refs):
    parts, out = refs[:4], refs[4]
    spread = make_spread()
    for c in range(2):
        numer, _, total = add_up([p[c] for p in parts], spread.astype(BF16))
        totals = jnp.concatenate([total] + [pltpu.roll(total, 128 - 16 * g, 1) for g in range(1, 6)], axis=0)
        wide = jnp.dot(
            totals, spread.astype(F32), precision=lax.Precision.HIGHEST, preferred_element_type=F32
        )
        out[:, c * WIDE:(c + 1) * WIDE] = jnp.concatenate(numer, axis=0) / wide


def close(parts):
    vmem = pl.BlockSpec(memory_space=pltpu.VMEM)
    return pl.pallas_call(
        close_kernel,
        out_shape=jax.ShapeDtypeStruct((48, 512), F32),
        in_specs=[vmem] * 4,
        out_specs=vmem,
        name="close",
    )(*parts)


def swap(x):
    return lax.ppermute(x, "core", [(0, 1), (1, 0)])


def shift(x, axes, by):
    pairs = []
    for y, c, z, w in itertools.product(range(4), range(2), range(4), range(4)):
        to = {"y": y, "z": z, "x": w}
        to[axes[c]] = (to[axes[c]] + by) % 4
        pairs.append((((y * 2 + c) * 4 + z) * 4 + w, ((to["y"] * 2 + c) * 4 + to["z"]) * 4 + to["x"]))
    return lax.ppermute(x, ALL, pairs)


def ring(x, axes):
    return [x] + [shift(x, axes, by) for by in (1, 2, 3)]


def deliver(parts, axes):
    return [parts[0]] + [shift(parts[by], axes, -by) for by in (1, 2, 3)]


def body(queries, keys, values, frame_slot, covisible, counts, out_weight):
    core = lax.axis_index("core")
    device = lax.axis_index(ALL)
    partner = device + 16 - 32 * core
    own_col = core * 512
    other_col = 512 - own_col

    mine = lax.dynamic_slice_in_dim(queries, own_col, 512, 1)
    theirs = swap(lax.dynamic_slice_in_dim(queries, other_col, 512, 1))
    first = core == 0
    pair = jnp.concatenate([jnp.where(first, mine, theirs), jnp.where(first, theirs, mine)], axis=0)
    along_z = jnp.concatenate(ring(pair[None], "zz"), axis=0)
    k_theirs = swap(keys)
    v_turned = jnp.swapaxes(values, 1, 2)
    v_theirs = swap(v_turned)
    planes = pack(ring(along_z, "yx"), k_theirs, v_theirs)
    q_parts = [ring(plane, "xy") for plane in planes]

    four = jnp.arange(4, dtype=jnp.int32)
    slots = jnp.concatenate([device * 4 + four, partner * 4 + four])
    frame_ids = jnp.arange(frame_slot.shape[0], dtype=jnp.int32)
    local = jnp.sum(jnp.where(frame_slot[None, :] == slots[:, None], frame_ids[None, :], 0), axis=1)
    used = jnp.arange(covisible.shape[1], dtype=jnp.int32)[None, :] < counts[:, None]
    need = jnp.any((covisible[:, None, :] == local[None, :, None]) & used[:, None, :], axis=2)
    need_i = need.astype(jnp.int32)
    place = jnp.cumsum(need_i, axis=1) - need_i
    eight = jnp.arange(8, dtype=jnp.int32)
    hit = need[:, None, :] & (place[:, None, :] == eight[None, :, None])
    lst = jnp.sum(jnp.where(hit, eight[None, None, :], 0), axis=2).reshape(96)
    cnt = jnp.sum(need_i, axis=1)

    me = jnp.stack([lax.axis_index(a) for a in ALL]).astype(jnp.int32)
    sent = []
    for c in range(2):
        sent += deliver(attend(me, cnt, lst, q_parts[c], keys, k_theirs, v_turned, v_theirs, c), "xy")
    sent = deliver(merge(sent, 4), "yx")
    sent = deliver(merge(sent, 1), "zz")
    attended = close(sent).astype(BF16)

    keep = lax.dynamic_slice_in_dim(attended, core * 24, 24, 0)
    give = swap(lax.dynamic_slice_in_dim(attended, 24 - core * 24, 24, 0))
    rows = jnp.concatenate([jnp.where(first, keep, give), jnp.where(first, give, keep)], axis=1)
    return jnp.dot(rows, out_weight, preferred_element_type=F32).astype(BF16)


def solution(mesh):
    fine = Mesh(mesh.devices.reshape(4, 2, 4, 4), ALL)
    return jax.shard_map(
        body,
        mesh=fine,
        in_specs=(P(ALL, None), P(ALL, None, None), P(ALL, None, None), P(), P(), P(), P()),
        out_specs=P(ALL, None),
        check_vma=False,
    )
```

time: 140 us -> 138 us (0.986); the launches traced: 138 us -> 139 us
  waiting for transfers between devices: 63.5 us -> 38.9 us
  starting transfers between devices: 29.6 us -> 51.1 us
  Pallas kernels: 32 us -> 35 us
    all_to_all x1 -> x0, waiting for transfers between devices: 42.5 us -> none  [body(): got = lax.all_to_all(sent, CHIPS, 0, 0)]
    ppermute x9 -> x24, starting transfers between devices: 15.8 us -> 41.2 us  [shift(): return lax.ppermute(x, ALL, pairs)]
    ppermute x9 -> x24, waiting for transfers between devices: 20.2 us -> 34.8 us  [shift(): return lax.ppermute(x, ALL, pairs)]
    unnamed x17 -> x35, local copies, waits for them, and re-layouts: 3.61 us -> 10.2 us
    all_to_all x1 -> x0, starting transfers between devices: 5.62 us -> none  [body(): got = lax.all_to_all(sent, CHIPS, 0, 0)]
    ppermute x4, waiting for transfers between devices: 0.86 us -> 4.11 us  [swap(): return lax.ppermute(x, 'core', [(0, 1), (1, 0)])]
    dynamic_slice x1 -> x0, local copies, waits for them, and re-layouts: 3.06 us -> none  [body(): k_theirs = swap(lax.dynamic_slice_in_dim(keys, other_col, 512, 2))]
    pallas_call x2 -> x6, Pallas kernels: 32 us -> 35 us  [the longest x2 26.2 us: attend(): pl.pallas_call(functools.partial(attend_kernel, part=part), out_shape=[ja...]
  transfers between devices with their start and end apart: 14 -> 28, of which waited for: 9 -> 16; matrix products, arithmetic and copies ran while one was open for 8% -> 1% of each run, Pallas kernels for 0% -> 19%
where the time goes in v1:
time: 138 us; the launch traced here: 139 us
  starting transfers between devices  51.1 us (37%)
  waiting for transfers between devices  38.9 us (28%)
  Pallas kernels  35 us (25%)
  local copies, waits for them, and re-layouts  10.6 us (8%)
  other arithmetic  2.03 us (1%)
    ppermute x24, starting transfers between devices, shift(): return lax.ppermute(x, ALL, pairs)  41.2 us
    ppermute x24, waiting for transfers between devices, shift(): return lax.ppermute(x, ALL, pairs)  34.8 us
    pallas_call x2, Pallas kernels, attend(): pl.pallas_call(functools.partial(attend_kernel, part=part), out_shape=[ja...  26.2 us
    unnamed x35, local copies, waits for them, and re-layouts  10.2 us
    ppermute x4, starting transfers between devices, swap(): return lax.ppermute(x, 'core', [(0, 1), (1, 0)])  9.83 us
    pallas_call x2, Pallas kernels, merge(): pl.pallas_call(functools.partial(merge_kernel, joint=len(parts) == 4, blo...  4.73 us
    ppermute x4, waiting for transfers between devices, swap(): return lax.ppermute(x, 'core', [(0, 1), (1, 0)])  4.11 us
  transfers between devices with their start and end apart: 28, of which 16 were waited for; matrix products, arithmetic and copies ran while one was open for 1% of the time, Pallas kernels for 19%

profile of v1, /device:TPU:1, one launch (start us, length us, event | category | flops | bytes accessed | tf_op | source)
XLA Modules:
  0.0 138.8 jit_solution(10420095887264086032)
XLA Ops:
  0.0 4.1 %copy.14 = bf16[4,256,1024]{1,2,0:T(8,128)(2,1)} copy(bf16[4,256,1024]{2,1,0:T(8,128)(2,1)} %param.9) | data formatting | bytes 4194304 | tf_op args[2]
  6.1 3.3 %collective-permute-done = bf16[24,512]{1,0:T(8,128)(2,1)S(1)} collective-permute-done((bf16[24,512]{1,0:T(8,128)(2,1)S(1)}, bf16[24,512]{1,0:T(8,128)(2,1)S(1)}, u32[]{:S(2)}, u32[]{:S(2)}) %collective-permute-start) | collective-permute-done | bytes 24608 | tf_op jit(solution)/shard_map/ppermute | solution.py:301
  9.4 1.8 %collective-permute-start.1 = (bf16[1,48,512]{2,1,0:T(8,128)(2,1)S(1)}, bf16[1,48,512]{2,1,0:T(8,128)(2,1)S(1)}, u32[]{:S(2)}, u32[]{:S(2)}) collective-permute-start(bf16[1,48,512]{2,1,0:T(8,128)(2,1)S(1)} %maximum_bitcast_fusion), channel_id=1, source_target_pairs={{0,4},{1,5},{2,6},{3,7},{4,8},{5,9},{6,10},{7,11},{8,12},{9,13},{1... | collective-permute-start | bytes 147464 | tf_op jit(solution)/shard_map/ppermute | solution.py:310
  11.2 3.3 %collective-permute-start.2 = (bf16[1,48,512]{2,1,0:T(8,128)(2,1)S(1)}, bf16[1,48,512]{2,1,0:T(8,128)(2,1)S(1)}, u32[]{:S(2)}, u32[]{:S(2)}) collective-permute-start(bf16[1,48,512]{2,1,0:T(8,128)(2,1)S(1)} %maximum_bitcast_fusion), channel_id=1, source_target_pairs={{0,8},{1,9},{2,10},{3,11},{4,12},{5,13},{6,14},{7,15},{8,0},{9,1},... | collective-permute-start | bytes 147464 | tf_op jit(solution)/shard_map/ppermute | solution.py:310
  19.1 2.5 %collective-permute-start.5 = (bf16[4,48,512]{2,1,0:T(8,128)(2,1)S(1)}, bf16[4,48,512]{2,1,0:T(8,128)(2,1)S(1)}, u32[]{:S(2)}, u32[]{:S(2)}) collective-permute-start(bf16[4,48,512]{2,1,0:T(8,128)(2,1)S(1)} %pad_maximum_fusion.p0), channel_id=1, source_target_pairs={{0,64},{1,65},{2,66},{3,67},{4,68},{5,69},{6,70},{7,71},{8,72},{9,... | collective-permute-start | bytes 589832 | tf_op jit(solution)/shard_map/ppermute | solution.py:310
  23.6 3.1 %collective-permute-done.5.p2 = bf16[4,48,512]{2,1,0:T(8,128)(2,1)S(1)} collective-permute-done((bf16[4,48,512]{2,1,0:T(8,128)(2,1)S(1)}, bf16[4,48,512]{2,1,0:T(8,128)(2,1)S(1)}, u32[]{:S(2)}, u32[]{:S(2)}) %collective-permute-start.5) | collective-permute-done | bytes 196640 | tf_op jit(solution)/shard_map/ppermute | solution.py:310
  27.5 2.1 %pack.1 = (bf16[16,48,256]{2,1,0:T(8,128)(2,1)}, bf16[16,48,256]{2,1,0:T(8,128)(2,1)}) custom-call(bf16[4,48,512]{2,1,0:T(8,128)(2,1)} %copy-done.6, bf16[4,48,512]{2,1,0:T(8,128)(2,1)} %copy-done.7, bf16[4,48,512]{2,1,0:T(8,128)(2,1)} %copy-done.8, bf16[4,48,512]{2,1,0:T(8,128)(2,1)} %copy-done.9, bf16[4,256,1024]{2,1,0:T(8,128)(2,1)} %collective-permute-done.7.k.k1, ...), custom_call_target="tpu_custom_call" | custom-call | tf_op jit(solution)/shard_map/pack/pallas_call | solution.py:210
  30.9 2.6 %collective-permute-start.16 = (bf16[16,48,256]{2,1,0:T(8,128)(2,1)}, bf16[16,48,256]{2,1,0:T(8,128)(2,1)S(1)}, u32[]{:S(2)}, u32[]{:S(2)}) collective-permute-start(bf16[16,48,256]{2,1,0:T(8,128)(2,1)} %get-tuple-element.28.q0), channel_id=1, source_target_pairs={{0,2},{1,3},{2,0},{3,1},{4,6},{5,7},{6,4},{7,5},{8,10},{9,11},{10,... | collective-permute-start | bytes 1179656 | tf_op jit(solution)/shard_map/ppermute | solution.py:310
  35.2 2.7 %collective-permute-start.11 = (bf16[16,48,256]{2,1,0:T(8,128)(2,1)}, bf16[16,48,256]{2,1,0:T(8,128)(2,1)S(1)}, u32[]{:S(2)}, u32[]{:S(2)}) collective-permute-start(bf16[16,48,256]{2,1,0:T(8,128)(2,1)} %get-tuple-element.23.q0), channel_id=1, source_target_pairs={{0,3},{1,0},{2,1},{3,2},{4,7},{5,4},{6,5},{7,6},{8,11},{9,8},{10,9... | collective-permute-start | bytes 1179656 | tf_op jit(solution)/shard_map/ppermute | solution.py:310
  38.0 5.4 %collective-permute-done.16.q2 = bf16[16,48,256]{2,1,0:T(8,128)(2,1)S(1)} collective-permute-done((bf16[16,48,256]{2,1,0:T(8,128)(2,1)}, bf16[16,48,256]{2,1,0:T(8,128)(2,1)S(1)}, u32[]{:S(2)}, u32[]{:S(2)}) %collective-permute-start.16) | collective-permute-done | bytes 393248 | tf_op jit(solution)/shard_map/ppermute | solution.py:310
  43.4 1.6 %copy-done.1 = bf16[4,256,1024]{1,2,0:T(8,128)(2,1)S(1)} copy-done((bf16[4,256,1024]{1,2,0:T(8,128)(2,1)S(1)}, bf16[4,256,1024]{1,2,0:T(8,128)(2,1)}, u32[]{:S(2)}) %copy-start.1) | copy-done | bytes 2097176
  45.0 1.6 %copy-done.3 = bf16[4,256,1024]{2,1,0:T(8,128)(2,1)S(1)} copy-done((bf16[4,256,1024]{2,1,0:T(8,128)(2,1)S(1)}, bf16[4,256,1024]{2,1,0:T(8,128)(2,1)}, u32[]{:S(2)}) %copy-start.3) | copy-done | bytes 2097176
  47.6 13.1 %attend.3 = (bf16[16,56,256]{2,1,0:T(8,128)(2,1)S(1)}, bf16[16,56,256]{2,1,0:T(8,128)(2,1)S(1)}, bf16[16,56,256]{2,1,0:T(8,128)(2,1)S(1)}, bf16[16,56,256]{2,1,0:T(8,128)(2,1)S(1)}) custom-call(s32[4]{0:T(128)S(1)} %pad_add_fusion.me, s32[12]{0:T(128)S(1)} %get-tuple-element.46.cnt, s32[96]{0:T(128)S(1)} %reshape.37.lst, bf16[16,48,256]{2,1,0:T(8,128)(2,1)S(1)} %copy-done.5, ...), custom_call_target="tpu_custom_call" | custom-call | flops 10000000000 | bytes 8388608 | tf_op jit(solution)/shard_map/attend/pallas_call | solution.py:174
  62.1 5.5 %collective-permute-start.19 = (bf16[16,56,256]{2,1,0:T(8,128)(2,1)S(1)}, bf16[16,56,256]{2,1,0:T(8,128)(2,1)S(1)}, u32[]{:S(2)}, u32[]{:S(2)}) collective-permute-start(bf16[16,56,256]{2,1,0:T(8,128)(2,1)S(1)} %get-tuple-element.31), channel_id=1, source_target_pairs={{0,2},{1,3},{2,0},{3,1},{4,6},{5,7},{6,4},{7,5},{8,10},{9,11},{10,... | collective-permute-start | bytes 1376264 | tf_op jit(solution)/shard_map/ppermute | solution.py:310
  68.5 13.1 %attend.2 = (bf16[16,56,256]{2,1,0:T(8,128)(2,1)S(1)}, bf16[16,56,256]{2,1,0:T(8,128)(2,1)S(1)}, bf16[16,56,256]{2,1,0:T(8,128)(2,1)S(1)}, bf16[16,56,256]{2,1,0:T(8,128)(2,1)S(1)}) custom-call(s32[4]{0:T(128)S(1)} %pad_add_fusion.me, s32[12]{0:T(128)S(1)} %get-tuple-element.46.cnt, s32[96]{0:T(128)S(1)} %reshape.37.lst, bf16[16,48,256]{2,1,0:T(8,128)(2,1)S(1)} %copy-done.4, ...), custom_call_target="tpu_custom_call" | custom-call | flops 10000000000 | bytes 8388608 | tf_op jit(solution)/shard_map/attend/pallas_call | solution.py:174
  85.3 8.2 %collective-permute-done.12.refs_1_ = bf16[16,56,256]{2,1,0:T(8,128)(2,1)S(1)} collective-permute-done((bf16[16,56,256]{2,1,0:T(8,128)(2,1)S(1)}, bf16[16,56,256]{2,1,0:T(8,128)(2,1)S(1)}, u32[]{:S(2)}, u32[]{:S(2)}) %collective-permute-start.12) | collective-permute-done | bytes 458784 | tf_op jit(solution)/shard_map/ppermute | solution.py:310
  93.5 3.7 %collective-permute-done.14.refs_3_ = bf16[16,56,256]{2,1,0:T(8,128)(2,1)S(1)} collective-permute-done((bf16[16,56,256]{2,1,0:T(8,128)(2,1)S(1)}, bf16[16,56,256]{2,1,0:T(8,128)(2,1)S(1)}, u32[]{:S(2)}, u32[]{:S(2)}) %collective-permute-start.14) | collective-permute-done | bytes 458784 | tf_op jit(solution)/shard_map/ppermute | solution.py:310
  97.2 4.3 %merge.2 = (bf16[8,56,256]{2,1,0:T(8,128)(2,1)S(1)}, bf16[8,56,256]{2,1,0:T(8,128)(2,1)S(1)}, bf16[8,56,256]{2,1,0:T(8,128)(2,1)S(1)}, bf16[8,56,256]{2,1,0:T(8,128)(2,1)S(1)}) custom-call(bf16[16,56,256]{2,1,0:T(8,128)(2,1)S(1)} %get-tuple-element.24.refs_0_, bf16[16,56,256]{2,1,0:T(8,128)(2,1)S(1)} %collective-permute-done.12.refs_1_, ...), custom_call_target="tpu_custom_call" | custom-call | tf_op jit(solution)/shard_map/merge/pallas_call | solution.py:267
  103.1 3.7 %collective-permute-done.21.refs_1_ = bf16[8,56,256]{2,1,0:T(8,128)(2,1)S(1)} collective-permute-done((bf16[8,56,256]{2,1,0:T(8,128)(2,1)S(1)}, bf16[8,56,256]{2,1,0:T(8,128)(2,1)S(1)}, u32[]{:S(2)}, u32[]{:S(2)}) %collective-permute-start.21) | collective-permute-done | bytes 229408 | tf_op jit(solution)/shard_map/ppermute | solution.py:310
  108.2 2.4 %collective-permute-done.23.refs_3_ = bf16[8,56,256]{2,1,0:T(8,128)(2,1)S(1)} collective-permute-done((bf16[8,56,256]{2,1,0:T(8,128)(2,1)S(1)}, bf16[8,56,256]{2,1,0:T(8,128)(2,1)S(1)}, u32[]{:S(2)}, u32[]{:S(2)}) %collective-permute-start.23) | collective-permute-done | bytes 229408 | tf_op jit(solution)/shard_map/ppermute | solution.py:310
  111.6 9.1 %collective-permute-start.24 = (bf16[2,56,256]{2,1,0:T(8,128)(2,1)S(1)}, bf16[2,56,256]{2,1,0:T(8,128)(2,1)S(1)}, u32[]{:S(2)}, u32[]{:S(2)}) collective-permute-start(bf16[2,56,256]{2,1,0:T(8,128)(2,1)S(1)} %get-tuple-element.38), channel_id=1, source_target_pairs={{0,12},{1,13},{2,14},{3,15},{4,0},{5,1},{6,2},{7,3},{8,4},{9,5},{1... | collective-permute-start | bytes 172040 | tf_op jit(solution)/shard_map/ppermute | solution.py:310
  122.4 2.9 %collective-permute-done.25.refs_2_ = bf16[2,56,256]{2,1,0:T(8,128)(2,1)S(1)} collective-permute-done((bf16[2,56,256]{2,1,0:T(8,128)(2,1)S(1)}, bf16[2,56,256]{2,1,0:T(8,128)(2,1)S(1)}, u32[]{:S(2)}, u32[]{:S(2)}) %collective-permute-start.25) | collective-permute-done | bytes 57376 | tf_op jit(solution)/shard_map/ppermute | solution.py:310
  126.2 1.9 %close.1 = f32[48,512]{1,0:T(8,128)} custom-call(bf16[2,56,256]{2,1,0:T(8,128)(2,1)} %copy-done.2, bf16[2,56,256]{2,1,0:T(8,128)(2,1)} %copy-done.10, bf16[2,56,256]{2,1,0:T(8,128)(2,1)} %copy-done.11, bf16[2,56,256]{2,1,0:T(8,128)(2,1)} %copy-done.12), custom_call_target="tpu_custom_call" | custom-call | tf_op jit(solution)/shard_map/close/pallas_call | solution.py:291
  129.0 7.9 %collective-permute-start.27 = (bf16[24,512]{1,0:T(8,128)(2,1)S(1)}, bf16[24,512]{1,0:T(8,128)(2,1)S(1)}, u32[]{:S(2)}, u32[]{:S(2)}) collective-permute-start(bf16[24,512]{1,0:T(8,128)(2,1)S(1)} %constant_dynamic-slice_fusion), channel_id=1, source_target_pairs={{0,16},{16,0},{1,17},{17,1},{2,18},{18,2},{3,19},{19,3},{4,20},{20... | collective-permute-start | bytes 73736 | tf_op jit(solution)/shard_map/ppermute | solution.py:301
  (95 shorter events, 28.8 us)
Async XLA Ops:
  4.1 22.6 %collective-permute-start.8 = (bf16[4,1024,256]{2,1,0:T(8,128)(2,1)}, bf16[4,1024,256]{2,1,0:T(8,128)(2,1)}, u32[]{:S(2)}, u32[]{:S(2)}) collective-permute-start(bf16[4,1024,256]{2,1,0:T(8,128)(2,1)} %bitcast.8), channel_id=1, source_target_pairs={{0,16},{16,0},{1,17},{17,1},{2,18},{18,2},{3,19},{19,3},{4,20},{20... | collective-permute-start | bytes 6291464 | tf_op jit(solution)/shard_map/ppermute | solution.py:301
  5.5 21.2 %collective-permute-start.7 = (bf16[4,256,1024]{2,1,0:T(8,128)(2,1)}, bf16[4,256,1024]{2,1,0:T(8,128)(2,1)}, u32[]{:S(2)}, u32[]{:S(2)}) collective-permute-start(bf16[4,256,1024]{2,1,0:T(8,128)(2,1)} %k0.3), channel_id=1, source_target_pairs={{0,16},{16,0},{1,17},{17,1},{2,18},{18,2},{3,19},{19,3},{4,20},{20... | collective-permute-start | bytes 6291464 | tf_op jit(solution)/shard_map/ppermute | solution.py:301
  9.4 5.9 %collective-permute-start.1 = (bf16[1,48,512]{2,1,0:T(8,128)(2,1)S(1)}, bf16[1,48,512]{2,1,0:T(8,128)(2,1)S(1)}, u32[]{:S(2)}, u32[]{:S(2)}) collective-permute-start(bf16[1,48,512]{2,1,0:T(8,128)(2,1)S(1)} %maximum_bitcast_fusion), channel_id=1, source_target_pairs={{0,4},{1,5},{2,6},{3,7},{4,8},{5,9},{6,10},{7,11},{8,12},{9,13},{1... | collective-permute-start | bytes 147464 | tf_op jit(solution)/shard_map/ppermute | solution.py:310
  11.2 5.6 %collective-permute-start.2 = (bf16[1,48,512]{2,1,0:T(8,128)(2,1)S(1)}, bf16[1,48,512]{2,1,0:T(8,128)(2,1)S(1)}, u32[]{:S(2)}, u32[]{:S(2)}) collective-permute-start(bf16[1,48,512]{2,1,0:T(8,128)(2,1)S(1)} %maximum_bitcast_fusion), channel_id=1, source_target_pairs={{0,8},{1,9},{2,10},{3,11},{4,12},{5,13},{6,14},{7,15},{8,0},{9,1},... | collective-permute-start | bytes 147464 | tf_op jit(solution)/shard_map/ppermute | solution.py:310
  17.8 5.8 %collective-permute-start.4 = (bf16[4,48,512]{2,1,0:T(8,128)(2,1)S(1)}, bf16[4,48,512]{2,1,0:T(8,128)(2,1)S(1)}, u32[]{:S(2)}, u32[]{:S(2)}) collective-permute-start(bf16[4,48,512]{2,1,0:T(8,128)(2,1)S(1)} %pad_maximum_fusion.p0), channel_id=1, source_target_pairs={{0,32},{1,33},{2,34},{3,35},{4,36},{5,37},{6,38},{7,39},{8,40},{9,... | collective-permute-start | bytes 589832 | tf_op jit(solution)/shard_map/ppermute | solution.py:310
  19.1 7.6 %collective-permute-start.5 = (bf16[4,48,512]{2,1,0:T(8,128)(2,1)S(1)}, bf16[4,48,512]{2,1,0:T(8,128)(2,1)S(1)}, u32[]{:S(2)}, u32[]{:S(2)}) collective-permute-start(bf16[4,48,512]{2,1,0:T(8,128)(2,1)S(1)} %pad_maximum_fusion.p0), channel_id=1, source_target_pairs={{0,64},{1,65},{2,66},{3,67},{4,68},{5,69},{6,70},{7,71},{8,72},{9,... | collective-permute-start | bytes 589832 | tf_op jit(solution)/shard_map/ppermute | solution.py:310
  21.5 5.2 %collective-permute-start.6 = (bf16[4,48,512]{2,1,0:T(8,128)(2,1)S(1)}, bf16[4,48,512]{2,1,0:T(8,128)(2,1)S(1)}, u32[]{:S(2)}, u32[]{:S(2)}) collective-permute-start(bf16[4,48,512]{2,1,0:T(8,128)(2,1)S(1)} %pad_maximum_fusion.p0), channel_id=1, source_target_pairs={{0,96},{1,97},{2,98},{3,99},{4,100},{5,101},{6,102},{7,103},{8,104... | collective-permute-start | bytes 589832 | tf_op jit(solution)/shard_map/ppermute | solution.py:310
  29.6 8.4 %collective-permute-start.15 = (bf16[16,48,256]{2,1,0:T(8,128)(2,1)}, bf16[16,48,256]{2,1,0:T(8,128)(2,1)S(1)}, u32[]{:S(2)}, u32[]{:S(2)}) collective-permute-start(bf16[16,48,256]{2,1,0:T(8,128)(2,1)} %get-tuple-element.28.q0), channel_id=1, source_target_pairs={{0,1},{1,2},{2,3},{3,0},{4,5},{5,6},{6,7},{7,4},{8,9},{9,10},{10,1... | collective-permute-start | bytes 1179656 | tf_op jit(solution)/shard_map/ppermute | solution.py:310
  30.9 12.5 %collective-permute-start.16 = (bf16[16,48,256]{2,1,0:T(8,128)(2,1)}, bf16[16,48,256]{2,1,0:T(8,128)(2,1)S(1)}, u32[]{:S(2)}, u32[]{:S(2)}) collective-permute-start(bf16[16,48,256]{2,1,0:T(8,128)(2,1)} %get-tuple-element.28.q0), channel_id=1, source_target_pairs={{0,2},{1,3},{2,0},{3,1},{4,6},{5,7},{6,4},{7,5},{8,10},{9,11},{10,... | collective-permute-start | bytes 1179656 | tf_op jit(solution)/shard_map/ppermute | solution.py:310
  33.5 9.9 %collective-permute-start.17 = (bf16[16,48,256]{2,1,0:T(8,128)(2,1)}, bf16[16,48,256]{2,1,0:T(8,128)(2,1)S(1)}, u32[]{:S(2)}, u32[]{:S(2)}) collective-permute-start(bf16[16,48,256]{2,1,0:T(8,128)(2,1)} %get-tuple-element.28.q0), channel_id=1, source_target_pairs={{0,3},{1,0},{2,1},{3,2},{4,7},{5,4},{6,5},{7,6},{8,11},{9,8},{10,9... | collective-permute-start | bytes 1179656 | tf_op jit(solution)/shard_map/ppermute | solution.py:310
  35.1 32.6 %collective-permute-start.10 = (bf16[16,48,256]{2,1,0:T(8,128)(2,1)}, bf16[16,48,256]{2,1,0:T(8,128)(2,1)S(1)}, u32[]{:S(2)}, u32[]{:S(2)}) collective-permute-start(bf16[16,48,256]{2,1,0:T(8,128)(2,1)} %get-tuple-element.23.q0), channel_id=1, source_target_pairs={{0,2},{1,3},{2,0},{3,1},{4,6},{5,7},{6,4},{7,5},{8,10},{9,11},{10,... | collective-permute-start | bytes 1179656 | tf_op jit(solution)/shard_map/ppermute | solution.py:310
  35.2 33.3 %collective-permute-start.11 = (bf16[16,48,256]{2,1,0:T(8,128)(2,1)}, bf16[16,48,256]{2,1,0:T(8,128)(2,1)S(1)}, u32[]{:S(2)}, u32[]{:S(2)}) collective-permute-start(bf16[16,48,256]{2,1,0:T(8,128)(2,1)} %get-tuple-element.23.q0), channel_id=1, source_target_pairs={{0,3},{1,0},{2,1},{3,2},{4,7},{5,4},{6,5},{7,6},{8,11},{9,8},{10,9... | collective-permute-start | bytes 1179656 | tf_op jit(solution)/shard_map/ppermute | solution.py:310
  38.0 30.5 %collective-permute-start.9 = (bf16[16,48,256]{2,1,0:T(8,128)(2,1)}, bf16[16,48,256]{2,1,0:T(8,128)(2,1)S(1)}, u32[]{:S(2)}, u32[]{:S(2)}) collective-permute-start(bf16[16,48,256]{2,1,0:T(8,128)(2,1)} %get-tuple-element.23.q0), channel_id=1, source_target_pairs={{0,1},{1,2},{2,3},{3,0},{4,5},{5,6},{6,7},{7,4},{8,9},{9,10},{10,1... | collective-permute-start | bytes 1179656 | tf_op jit(solution)/shard_map/ppermute | solution.py:310
  60.7 23.8 %collective-permute-start.18 = (bf16[16,56,256]{2,1,0:T(8,128)(2,1)S(1)}, bf16[16,56,256]{2,1,0:T(8,128)(2,1)S(1)}, u32[]{:S(2)}, u32[]{:S(2)}) collective-permute-start(bf16[16,56,256]{2,1,0:T(8,128)(2,1)S(1)} %get-tuple-element.30), channel_id=1, source_target_pairs={{0,3},{1,0},{2,1},{3,2},{4,7},{5,4},{6,5},{7,6},{8,11},{9,8},{10,9... | collective-permute-start | bytes 1376264 | tf_op jit(solution)/shard_map/ppermute | solution.py:310
  62.1 23.2 %collective-permute-start.19 = (bf16[16,56,256]{2,1,0:T(8,128)(2,1)S(1)}, bf16[16,56,256]{2,1,0:T(8,128)(2,1)S(1)}, u32[]{:S(2)}, u32[]{:S(2)}) collective-permute-start(bf16[16,56,256]{2,1,0:T(8,128)(2,1)S(1)} %get-tuple-element.31), channel_id=1, source_target_pairs={{0,2},{1,3},{2,0},{3,1},{4,6},{5,7},{6,4},{7,5},{8,10},{9,11},{10,... | collective-permute-start | bytes 1376264 | tf_op jit(solution)/shard_map/ppermute | solution.py:310
  67.7 17.6 %collective-permute-start.20 = (bf16[16,56,256]{2,1,0:T(8,128)(2,1)S(1)}, bf16[16,56,256]{2,1,0:T(8,128)(2,1)S(1)}, u32[]{:S(2)}, u32[]{:S(2)}) collective-permute-start(bf16[16,56,256]{2,1,0:T(8,128)(2,1)S(1)} %get-tuple-element.32), channel_id=1, source_target_pairs={{0,1},{1,2},{2,3},{3,0},{4,5},{5,6},{6,7},{7,4},{8,9},{9,10},{10,1... | collective-permute-start | bytes 1376264 | tf_op jit(solution)/shard_map/ppermute | solution.py:310
  81.6 11.9 %collective-permute-start.12 = (bf16[16,56,256]{2,1,0:T(8,128)(2,1)S(1)}, bf16[16,56,256]{2,1,0:T(8,128)(2,1)S(1)}, u32[]{:S(2)}, u32[]{:S(2)}) collective-permute-start(bf16[16,56,256]{2,1,0:T(8,128)(2,1)S(1)} %get-tuple-element.25), channel_id=1, source_target_pairs={{0,3},{1,0},{2,1},{3,2},{4,7},{5,4},{6,5},{7,6},{8,11},{9,8},{10,9... | collective-permute-start | bytes 1376264 | tf_op jit(solution)/shard_map/ppermute | solution.py:310
  83.2 10.3 %collective-permute-start.13 = (bf16[16,56,256]{2,1,0:T(8,128)(2,1)S(1)}, bf16[16,56,256]{2,1,0:T(8,128)(2,1)S(1)}, u32[]{:S(2)}, u32[]{:S(2)}) collective-permute-start(bf16[16,56,256]{2,1,0:T(8,128)(2,1)S(1)} %get-tuple-element.26), channel_id=1, source_target_pairs={{0,2},{1,3},{2,0},{3,1},{4,6},{5,7},{6,4},{7,5},{8,10},{9,11},{10,... | collective-permute-start | bytes 1376264 | tf_op jit(solution)/shard_map/ppermute | solution.py:310
  84.5 12.7 %collective-permute-start.14 = (bf16[16,56,256]{2,1,0:T(8,128)(2,1)S(1)}, bf16[16,56,256]{2,1,0:T(8,128)(2,1)S(1)}, u32[]{:S(2)}, u32[]{:S(2)}) collective-permute-start(bf16[16,56,256]{2,1,0:T(8,128)(2,1)S(1)} %get-tuple-element.27), channel_id=1, source_target_pairs={{0,1},{1,2},{2,3},{3,0},{4,5},{5,6},{6,7},{7,4},{8,9},{9,10},{10,1... | collective-permute-start | bytes 1376264 | tf_op jit(solution)/shard_map/ppermute | solution.py:310
  101.5 5.2 %collective-permute-start.21 = (bf16[8,56,256]{2,1,0:T(8,128)(2,1)S(1)}, bf16[8,56,256]{2,1,0:T(8,128)(2,1)S(1)}, u32[]{:S(2)}, u32[]{:S(2)}) collective-permute-start(bf16[8,56,256]{2,1,0:T(8,128)(2,1)S(1)} %get-tuple-element.34), channel_id=1, source_target_pairs={{0,96},{1,97},{2,98},{3,99},{4,100},{5,101},{6,102},{7,103},{8,104... | collective-permute-start | bytes 688136 | tf_op jit(solution)/shard_map/ppermute | solution.py:310
  101.7 6.5 %collective-permute-start.22 = (bf16[8,56,256]{2,1,0:T(8,128)(2,1)S(1)}, bf16[8,56,256]{2,1,0:T(8,128)(2,1)S(1)}, u32[]{:S(2)}, u32[]{:S(2)}) collective-permute-start(bf16[8,56,256]{2,1,0:T(8,128)(2,1)S(1)} %get-tuple-element.35), channel_id=1, source_target_pairs={{0,64},{1,65},{2,66},{3,67},{4,68},{5,69},{6,70},{7,71},{8,72},{9,... | collective-permute-start | bytes 688136 | tf_op jit(solution)/shard_map/ppermute | solution.py:310
  102.3 8.2 %collective-permute-start.23 = (bf16[8,56,256]{2,1,0:T(8,128)(2,1)S(1)}, bf16[8,56,256]{2,1,0:T(8,128)(2,1)S(1)}, u32[]{:S(2)}, u32[]{:S(2)}) collective-permute-start(bf16[8,56,256]{2,1,0:T(8,128)(2,1)S(1)} %get-tuple-element.36), channel_id=1, source_target_pairs={{0,32},{1,33},{2,34},{3,35},{4,36},{5,37},{6,38},{7,39},{8,40},{9,... | collective-permute-start | bytes 688136 | tf_op jit(solution)/shard_map/ppermute | solution.py:310
  111.6 10.9 %collective-permute-start.24 = (bf16[2,56,256]{2,1,0:T(8,128)(2,1)S(1)}, bf16[2,56,256]{2,1,0:T(8,128)(2,1)S(1)}, u32[]{:S(2)}, u32[]{:S(2)}) collective-permute-start(bf16[2,56,256]{2,1,0:T(8,128)(2,1)S(1)} %get-tuple-element.38), channel_id=1, source_target_pairs={{0,12},{1,13},{2,14},{3,15},{4,0},{5,1},{6,2},{7,3},{8,4},{9,5},{1... | collective-permute-start | bytes 172040 | tf_op jit(solution)/shard_map/ppermute | solution.py:310
  129.0 8.8 %collective-permute-start.27 = (bf16[24,512]{1,0:T(8,128)(2,1)S(1)}, bf16[24,512]{1,0:T(8,128)(2,1)S(1)}, u32[]{:S(2)}, u32[]{:S(2)}) collective-permute-start(bf16[24,512]{1,0:T(8,128)(2,1)S(1)} %constant_dynamic-slice_fusion), channel_id=1, source_target_pairs={{0,16},{16,0},{1,17},{17,1},{2,18},{18,2},{3,19},{19,3},{4,20},{20... | collective-permute-start | bytes 73736 | tf_op jit(solution)/shard_map/ppermute | solution.py:301
  (21 other events, 255.0 us)

commit v2 on v1

--- a/solution.py
+++ b/solution.py
@@ -20,19 +20,19 @@
 
 
 def attend_kernel(
-    me, cnt, lst, q0, q1, q2, q3, k0, k1, v0, v1, o0, o1, o2, o3,
-    pq, pj, k, vt, qm, acc, sa, sb, ta, tb, ha, hb, yb, sem, *, part,
+    me, cnt, lst, q0, q1, q2, q3, k0, k1, v0, o0, o1, o2, o3,
+    pq, pj, ps, qv, k, vt, qm, acc, sb, top, shrink, yb, sem, *, part,
 ):
     my_y, my_core, my_z, my_x = me[0], me[1], me[2], me[3]
     col = pl.multiple_of(my_core * 512 + part * WIDE, WIDE)
     copies = [
         pltpu.make_async_copy(src, dst, sem.at[i])
         for i, (src, dst) in enumerate(
-            [
+            [(q, qv.at[r3]) for r3, q in enumerate((q0, q1, q2, q3))]
+            + [
                 (k0.at[:, :, pl.ds(col, WIDE)], k.at[pl.ds(0, 4)]),
                 (k1.at[:, :, pl.ds(col, WIDE)], k.at[pl.ds(4, 4)]),
-                (v0.at[:, pl.ds(col, WIDE), :], vt.at[pl.ds(0, 4)]),
-                (v1.at[:, pl.ds(col, WIDE), :], vt.at[pl.ds(4, 4)]),
+                (v0.at[:, pl.ds(part * WIDE, WIDE), :], vt),
             ]
         )
     ]
@@ -41,18 +41,23 @@
     scale = HD ** -0.5 * LOG2E
     ones = jnp.ones((16, 256), BF16)
 
-    def list_frame(qi, at):
+    def list_frame(qi, carry):
+        at, slot = carry
+
         def put(i, at):
             pj[at] = lst[qi * 8 + i]
             pq[at] = qi
+            ps[at] = slot
             return at + 1
 
-        return lax.fori_loop(0, cnt[qi], put, at)
-
-    total = lax.fori_loop(0, 12, list_frame, 0)
-    for u in range(3):
+        n = cnt[qi]
+        return lax.fori_loop(0, n, put, at), jnp.where(n > 0, 1 - slot, slot)
+
+    total, spare = lax.fori_loop(0, 12, list_frame, (jnp.int32(0), jnp.int32(0)))
+    for u in range(5):
         pq[total + u] = 12
         pj[total + u] = 0
+        ps[total + u] = spare
 
     def place(r2, r3, rz):
         y = lax.rem(my_y + 4 - jnp.where(my_core == 0, r2, r3), 4)
@@ -60,16 +65,18 @@
         z = lax.rem(my_z + 4 - rz, 4)
         return [pl.multiple_of(y * 768 + (c * 16 + z * 4 + x) * 24, 8) for c in range(2)]
 
-    for r3, q in enumerate((q0, q1, q2, q3)):
-
-        def load(r2, _, q=q, r3=r3):
+    for r3 in range(4):
+        copies[r3].wait()
+
+        def load(r2, _, r3=r3):
             for rz in range(4):
-                block = q[r2 * 4 + rz].astype(F32)
+                block = qv[r3, r2 * 4 + rz].astype(F32)
                 for c, row in enumerate(place(r2, r3, rz)):
                     yb[pl.ds(row, 24), :WIDE] = block[c * 24:(c + 1) * 24]
             return 0
 
-        lax.fori_loop(0, 4, load, 0)
+        for r2 in range(4):
+            load(r2, 0)
 
     def turn(qi, _):
         rows = pl.ds(pl.multiple_of(qi * 256, 256), 256)
@@ -88,62 +95,65 @@
         return 0
 
     lax.fori_loop(0, 12, turn, 0)
-    for copy in copies:
+    for copy in copies[4:]:
         copy.wait()
     acc[...] = jnp.zeros_like(acc)
-    ta[...] = jnp.full_like(ta, NO_TOP)
-    tb[...] = jnp.full_like(tb, NO_TOP)
     qm[12] = jnp.zeros((NH, 128, 256), BF16)
 
-    def score(t, h, s_ref):
+    def score(t, p, h):
         hp = h // 2
-        keys = k[pj[t], :, hp * 128:(hp + 1) * 128]
-        s = jnp.dot(keys, qm[pq[t], h], preferred_element_type=F32) * scale
-        s_ref[h] = s
+        keys = k[pj[t + p], :, hp * 128:(hp + 1) * 128]
+        s = jnp.dot(keys, qm[pq[t + p], h], preferred_element_type=F32) * scale
+        sb[p, h] = s
         return jnp.max(s, axis=0, keepdims=True)
 
-    def settle(t, highs, old_ref, new_ref, shrink_ref):
-        first = pq[t] != pq[jnp.maximum(t - 1, 0)]
-        old = jnp.where(first, NO_TOP, old_ref[...])
+    def settle(t, p, highs, old):
+        first = pq[t + p] != pq[jnp.maximum(t + p - 1, 0)]
+        old = jnp.where(first, NO_TOP, old)
         high = jnp.concatenate(highs, axis=0)
         new = jnp.maximum(old, jnp.ceil(high * (1.0 / TOP_STEP)) * TOP_STEP)
-        new_ref[...] = new
-        shrink_ref[...] = jnp.exp2(old - new)
-
-    def weigh(t, h, s_ref, top, shrink):
-        weights = jnp.exp2(s_ref[h] - top[h:h + 1]).astype(BF16)
-        vals = jnp.concatenate([vt[pj[t], h * 64:(h + 1) * 64, :], ones], axis=0)
+        top[p] = new
+        shrink[p] = jnp.exp2(old - new)
+        return new
+
+    def weigh(t, p, h, tops, shrinks):
+        weights = jnp.exp2(sb[p, h] - tops[h:h + 1]).astype(BF16)
+        vals = jnp.concatenate([vt[pj[t + p], h * 64:(h + 1) * 64, :], ones], axis=0)
         part = jnp.dot(vals, weights, preferred_element_type=F32)
-        acc[h] = acc[h] * shrink[h:h + 1] + part
-
-    def finish(t, top_ref):
-        qi = pq[t]
-
-        @pl.when((qi < 12) & (pq[t + 1] != qi))
+        at = ps[t + p]
+        acc[at, h] = acc[at, h] * shrinks[h:h + 1] + part
+
+    def finish(t, p, tops):
+        qi = pq[t + p]
+
+        @pl.when((qi < 12) & (pq[t + p + 1] != qi))
         def _():
+            at = ps[t + p]
             rows = pl.ds(pl.multiple_of(qi * 256, 256), 256)
-            totals = jnp.concatenate([acc[h, 64:65, :] for h in range(NH)], axis=0)
+            totals = jnp.concatenate([acc[at, h, 64:65, :] for h in range(NH)], axis=0)
             hi = totals.astype(BF16).astype(F32)
-            extra = [top_ref[...], hi, totals - hi, jnp.zeros((128 - 3 * NH, 256), F32)]
+            extra = [tops, hi, totals - hi, jnp.zeros((128 - 3 * NH, 256), F32)]
             for hp in range(NH // 2):
-                both = jnp.concatenate([acc[2 * hp, :64, :], acc[2 * hp + 1, :64, :]], axis=0)
+                both = jnp.concatenate([acc[at, 2 * hp, :64, :], acc[at, 2 * hp + 1, :64, :]], axis=0)
                 yb[rows, hp * 128:(hp + 1) * 128] = both.T
             yb[rows, WIDE:] = jnp.concatenate(extra, axis=0).T
 
-    def half(t, s_now, s_next, t_now, t_next, h_now, h_next):
-        top, shrink = t_now[...], h_now[...]
-        highs = []
-        for h in range(NH):
-            highs.append(score(t + 1, h, s_next))
-            weigh(t, h, s_now, top, shrink)
-        settle(t + 1, highs, t_now, t_next, h_next)
-        finish(t, t_now)
-
-    settle(0, [score(0, h, sa) for h in range(NH)], tb, ta, ha)
+    old = jnp.full((NH, 256), NO_TOP, F32)
+    for p in range(2):
+        old = settle(0, p, [score(0, p, h) for h in range(NH)], old)
 
     def two(u, _):
-        half(2 * u, sa, sb, ta, tb, ha, hb)
-        half(2 * u + 1, sb, sa, tb, ta, hb, ha)
+        t = u * 2
+        tops, shrinks = [top[0], top[1]], [shrink[0], shrink[1]]
+        highs = [[], []]
+        for p in range(2):
+            for h in range(NH):
+                weigh(t, p, h, tops[p], shrinks[p])
+                highs[p].append(score(t + 2, p, h))
+        old = settle(t + 2, 0, highs[0], tops[1])
+        settle(t + 2, 1, highs[1], old)
+        for p in range(2):
+            finish(t, p, tops[p])
         return 0
 
     lax.fori_loop(0, (total + 1) // 2, two, 0)
@@ -164,38 +174,73 @@
                 o[r2 * 4 + rz] = jnp.concatenate(data, axis=0).astype(BF16)
             return 0
 
-        lax.fori_loop(0, 4, emit, 0)
-
-
-def attend(me, cnt, lst, q, k0, k1, v0, v1, part):
+        for r2 in range(4):
+            emit(r2, 0)
+
+
+def attend(me, cnt, lst, q, k0, k1, v0, part):
     vmem = pl.BlockSpec(memory_space=pltpu.VMEM)
     smem = pl.BlockSpec(memory_space=pltpu.SMEM)
     whole = pl.BlockSpec(memory_space=pl.ANY)
     return pl.pallas_call(
         functools.partial(attend_kernel, part=part),
         out_shape=[jax.ShapeDtypeStruct((16, 56, WIDE), BF16)] * 4,
-        in_specs=[smem] * 3 + [vmem] * 4 + [whole] * 4,
+        in_specs=[smem] * 3 + [whole] * 7,
         out_specs=[vmem] * 4,
         scratch_shapes=[
             pltpu.SMEM((104,), jnp.int32),
             pltpu.SMEM((104,), jnp.int32),
+            pltpu.SMEM((104,), jnp.int32),
+            pltpu.VMEM((4, 16, 48, WIDE), BF16),
             pltpu.VMEM((8, 256, WIDE), BF16),
             pltpu.VMEM((8, WIDE, 256), BF16),
             pltpu.VMEM((13, NH, 128, 256), BF16),
-            pltpu.VMEM((NH, 80, 256), F32),
-            pltpu.VMEM((NH, 256, 256), F32),
-            pltpu.VMEM((NH, 256, 256), F32),
-            pltpu.VMEM((NH, 256), F32),
-            pltpu.VMEM((NH, 256), F32),
-            pltpu.VMEM((NH, 256), F32),
-            pltpu.VMEM((NH, 256), F32),
+            pltpu.VMEM((2, NH, 80, 256), F32),
+            pltpu.VMEM((2, NH, 256, 256), F32),
+            pltpu.VMEM((2, NH, 256), F32),
+            pltpu.VMEM((2, NH, 256), F32),
             pltpu.VMEM((3072, WIDE + 128), F32),
-            pltpu.SemaphoreType.DMA((4,)),
+            pltpu.SemaphoreType.DMA((7,)),
         ],
         compiler_params=pltpu.CompilerParams(vmem_limit_bytes=36 * 2**20),
         cost_estimate=pl.CostEstimate(flops=10**10, bytes_accessed=2**23, transcendentals=2 * 10**7),
         name="attend",
-    )(me, cnt, lst, *q, k0, k1, v0, v1)
+    )(me, cnt, lst, *q, k0, k1, v0)
+
+
+def turn_kernel(me, v0, v1, q, out, held, sem):
+    col = pl.multiple_of(me[1] * 512, 512)
+    copies = [
+        pltpu.make_async_copy(v.at[:, :, pl.ds(col, 512)], held.at[pl.ds(i * 4, 4)], sem.at[i])
+        for i, v in enumerate((v0, v1))
+    ]
+    for copy in copies:
+        copy.start()
+    for copy in copies:
+        copy.wait()
+
+    def one(j, _):
+        for at in range(0, 512, 128):
+            out[j, at:at + 128, :] = held[j, :, at:at + 128].astype(F32).T.astype(BF16)
+        return 0
+
+    lax.fori_loop(0, 8, one, 0)
+
+
+def turn_values(me, v0, v1, q):
+    vmem = pl.BlockSpec(memory_space=pltpu.VMEM)
+    smem = pl.BlockSpec(memory_space=pltpu.SMEM)
+    whole = pl.BlockSpec(memory_space=pl.ANY)
+    return pl.pallas_call(
+        turn_kernel,
+        out_shape=jax.ShapeDtypeStruct((8, 512, 256), BF16),
+        in_specs=[smem] + [whole] * 3,
+        out_specs=vmem,
+        scratch_shapes=[pltpu.VMEM((8, 256, 512), BF16), pltpu.SemaphoreType.DMA((2,))],
+        cost_estimate=pl.CostEstimate(flops=10**6, bytes_accessed=2**23, transcendentals=0),
+        compiler_params=pltpu.CompilerParams(vmem_limit_bytes=16 * 2**20),
+        name="turn",
+    )(me, v0, v1, q)
 
 
 def pack_kernel(p0, p1, p2, p3, k, v, o0, o1):
@@ -259,7 +304,8 @@
                 out[b * 2 + c] = jnp.concatenate(numer + [tail], axis=0).astype(BF16)
             return 0
 
-        lax.fori_loop(0, blocks, one, 0)
+        for b in range(blocks):
+            one(b, 0)
 
 
 def merge(parts, blocks):
@@ -274,8 +320,8 @@
     )(*parts)
 
 
-def close_kernel(*refs):
-    parts, out = refs[:4], refs[4]
+def close_kernel(me, p0, p1, p2, p3, keep, give, both):
+    parts = (p0, p1, p2, p3)
     spread = make_spread()
     for c in range(2):
         numer, _, total = add_up([p[c] for p in parts], spread.astype(BF16))
@@ -283,18 +329,23 @@
         wide = jnp.dot(
             totals, spread.astype(F32), precision=lax.Precision.HIGHEST, preferred_element_type=F32
         )
-        out[:, c * WIDE:(c + 1) * WIDE] = jnp.concatenate(numer, axis=0) / wide
-
-
-def close(parts):
+        both[:, c * WIDE:(c + 1) * WIDE] = jnp.concatenate(numer, axis=0) / wide
+    row = pl.multiple_of(me[1] * 24, 8)
+    keep[...] = both[pl.ds(row, 24), :].astype(BF16)
+    give[...] = both[pl.ds(24 - row, 24), :].astype(BF16)
+
+
+def close(me, parts):
     vmem = pl.BlockSpec(memory_space=pltpu.VMEM)
+    smem = pl.BlockSpec(memory_space=pltpu.SMEM)
     return pl.pallas_call(
         close_kernel,
-        out_shape=jax.ShapeDtypeStruct((48, 512), F32),
-        in_specs=[vmem] * 4,
-        out_specs=vmem,
+        out_shape=[jax.ShapeDtypeStruct((24, 512), BF16)] * 2,
+        in_specs=[smem] + [vmem] * 4,
+        out_specs=[vmem] * 2,
+        scratch_shapes=[pltpu.VMEM((48, 512), F32)],
         name="close",
-    )(*parts)
+    )(me, *parts)
 
 
 def swap(x):
@@ -330,10 +381,10 @@
     first = core == 0
     pair = jnp.concatenate([jnp.where(first, mine, theirs), jnp.where(first, theirs, mine)], axis=0)
     along_z = jnp.concatenate(ring(pair[None], "zz"), axis=0)
-    k_theirs = swap(keys)
-    v_turned = jnp.swapaxes(values, 1, 2)
-    v_theirs = swap(v_turned)
+    k_theirs, v_theirs = swap(keys), swap(values)
     planes = pack(ring(along_z, "yx"), k_theirs, v_theirs)
+    me = jnp.stack([lax.axis_index(a) for a in ALL]).astype(jnp.int32)
+    v_turned = turn_values(me, values, v_theirs, planes[0])
     q_parts = [ring(plane, "xy") for plane in planes]
 
     four = jnp.arange(4, dtype=jnp.int32)
@@ -349,16 +400,13 @@
     lst = jnp.sum(jnp.where(hit, eight[None, None, :], 0), axis=2).reshape(96)
     cnt = jnp.sum(need_i, axis=1)
 
-    me = jnp.stack([lax.axis_index(a) for a in ALL]).astype(jnp.int32)
     sent = []
     for c in range(2):
-        sent += deliver(attend(me, cnt, lst, q_parts[c], keys, k_theirs, v_turned, v_theirs, c), "xy")
+        sent += deliver(attend(me, cnt, lst, q_parts[c], keys, k_theirs, v_turned, c), "xy")
     sent = deliver(merge(sent, 4), "yx")
     sent = deliver(merge(sent, 1), "zz")
-    attended = close(sent).astype(BF16)
-
-    keep = lax.dynamic_slice_in_dim(attended, core * 24, 24, 0)
-    give = swap(lax.dynamic_slice_in_dim(attended, 24 - core * 24, 24, 0))
+    keep, give = close(me, sent)
+    give = swap(give)
     rows = jnp.concatenate([jnp.where(first, keep, give), jnp.where(first, give, keep)], axis=1)
     return jnp.dot(rows, out_weight, preferred_element_type=F32).astype(BF16)
 

time: 138 us -> 120 us (0.87); the launches traced: 139 us -> 119 us
  starting transfers between devices: 51.1 us -> 34.2 us
  local copies, waits for them, and re-layouts: 10.6 us -> 5.6 us
  other arithmetic: 2.03 us -> 4.65 us
    ppermute x24, starting transfers between devices: 41.2 us -> 23.5 us  [shift(): return lax.ppermute(x, ALL, pairs)]
    unnamed x35 -> x30, local copies, waits for them, and re-layouts: 10.2 us -> 4.52 us
    pallas_call x1 -> x2, Pallas kernels: 1.94 us -> 5.15 us  [the longest x1 3.21 us: turn_values(): pl.pallas_call(turn_kernel, out_shape=jax.ShapeDtypeStruct((8, 512, 256),...]
    pallas_call x2, Pallas kernels: 4.73 us -> 2.67 us  [merge(): pl.pallas_call(functools.partial(merge_kernel, joint=len(parts) == 4, blo...]
    pallas_call x2, Pallas kernels: 26.2 us -> 24.8 us  [attend(): pl.pallas_call(functools.partial(attend_kernel, part=part), out_shape=[ja...]
  transfers between devices with their start and end apart: 28 -> 28, of which waited for: 16 -> 17; matrix products, arithmetic and copies ran while one was open for 1% -> 4% of each run, Pallas kernels for 19% -> 23%
where the time goes in v2:
time: 120 us; the launch traced here: 119 us
  waiting for transfers between devices  38.8 us (32%)
  Pallas kernels  34.8 us (29%)
  starting transfers between devices  34.2 us (29%)
  local copies, waits for them, and re-layouts  5.6 us (5%)
  other arithmetic  4.65 us (4%)
    ppermute x24, waiting for transfers between devices, shift(): return lax.ppermute(x, ALL, pairs)  36 us
    pallas_call x2, Pallas kernels, attend(): pl.pallas_call(functools.partial(attend_kernel, part=part), out_shape=[ja...  24.8 us
    ppermute x24, starting transfers between devices, shift(): return lax.ppermute(x, ALL, pairs)  23.5 us
    ppermute x4, starting transfers between devices, swap(): return lax.ppermute(x, 'core', [(0, 1), (1, 0)])  10.7 us
    unnamed x30, local copies, waits for them, and re-layouts  4.52 us
    pallas_call x1, Pallas kernels, turn_values(): pl.pallas_call(turn_kernel, out_shape=jax.ShapeDtypeStruct((8, 512, 256),...  3.21 us
    ppermute x4, waiting for transfers between devices, swap(): return lax.ppermute(x, 'core', [(0, 1), (1, 0)])  2.82 us
    pallas_call x2, Pallas kernels, merge(): pl.pallas_call(functools.partial(merge_kernel, joint=len(parts) == 4, blo...  2.67 us
  transfers between devices with their start and end apart: 28, of which 17 were waited for; matrix products, arithmetic and copies ran while one was open for 4% of the time, Pallas kernels for 23%

profile of v2, /device:TPU:1, one launch (start us, length us, event | category | flops | bytes accessed | tf_op | source)
XLA Modules:
  0.0 119.3 jit_solution(2891501026635623562)
XLA Ops:
  3.5 1.8 %collective-permute-done = bf16[24,512]{1,0:T(8,128)(2,1)S(1)} collective-permute-done((bf16[24,512]{1,0:T(8,128)(2,1)S(1)}, bf16[24,512]{1,0:T(8,128)(2,1)S(1)}, u32[]{:S(2)}, u32[]{:S(2)}) %collective-permute-start) | collective-permute-done | bytes 24608 | tf_op jit(solution)/shard_map/ppermute | solution.py:352
  6.0 3.9 %collective-permute-start.3 = (bf16[1,48,512]{2,1,0:T(8,128)(2,1)S(1)}, bf16[1,48,512]{2,1,0:T(8,128)(2,1)S(1)}, u32[]{:S(2)}, u32[]{:S(2)}) collective-permute-start(bf16[1,48,512]{2,1,0:T(8,128)(2,1)S(1)} %maximum_bitcast_fusion), channel_id=1, source_target_pairs={{0,12},{1,13},{2,14},{3,15},{4,0},{5,1},{6,2},{7,3},{8,4},{9,5},{1... | collective-permute-start | bytes 147464 | tf_op jit(solution)/shard_map/ppermute | solution.py:361
  11.1 3.4 %collective-permute-done.2 = bf16[1,48,512]{2,1,0:T(8,128)(2,1)S(1)} collective-permute-done((bf16[1,48,512]{2,1,0:T(8,128)(2,1)S(1)}, bf16[1,48,512]{2,1,0:T(8,128)(2,1)S(1)}, u32[]{:S(2)}, u32[]{:S(2)}) %collective-permute-start.2) | collective-permute-done | bytes 49184 | tf_op jit(solution)/shard_map/ppermute | solution.py:361
  14.7 2.5 %collective-permute-start.6 = (bf16[4,48,512]{2,1,0:T(8,128)(2,1)S(1)}, bf16[4,48,512]{2,1,0:T(8,128)(2,1)S(1)}, u32[]{:S(2)}, u32[]{:S(2)}) collective-permute-start(bf16[4,48,512]{2,1,0:T(8,128)(2,1)S(1)} %pad_maximum_fusion.p0), channel_id=1, source_target_pairs={{0,96},{1,97},{2,98},{3,99},{4,100},{5,101},{6,102},{7,103},{8,104... | collective-permute-start | bytes 589832 | tf_op jit(solution)/shard_map/ppermute | solution.py:361
  23.4 2.3 %collective-permute-done.4.p1 = bf16[4,48,512]{2,1,0:T(8,128)(2,1)S(1)} collective-permute-done((bf16[4,48,512]{2,1,0:T(8,128)(2,1)S(1)}, bf16[4,48,512]{2,1,0:T(8,128)(2,1)S(1)}, u32[]{:S(2)}, u32[]{:S(2)}) %collective-permute-start.4) | collective-permute-done | bytes 196640 | tf_op jit(solution)/shard_map/ppermute | solution.py:361
  26.3 2.2 %pack.1 = (bf16[16,48,256]{2,1,0:T(8,128)(2,1)}, bf16[16,48,256]{2,1,0:T(8,128)(2,1)}) custom-call(bf16[4,48,512]{2,1,0:T(8,128)(2,1)} %copy-done.8, bf16[4,48,512]{2,1,0:T(8,128)(2,1)} %copy-done.11, bf16[4,48,512]{2,1,0:T(8,128)(2,1)} %copy-done.10, bf16[4,48,512]{2,1,0:T(8,128)(2,1)} %copy-done.9, bf16[4,256,1024]{2,1,0:T(8,128)(2,1)} %collective-permute-done.7.k.k1, ...), custom_call_target="tpu_custom_call" | custom-call | tf_op jit(solution)/shard_map/pack/pallas_call | solution.py:255
  28.5 2.4 %collective-permute-start.11 = (bf16[16,48,256]{2,1,0:T(8,128)(2,1)}, bf16[16,48,256]{2,1,0:T(8,128)(2,1)S(1)}, u32[]{:S(2)}, u32[]{:S(2)}) collective-permute-start(bf16[16,48,256]{2,1,0:T(8,128)(2,1)} %get-tuple-element.25.q.q0), channel_id=1, source_target_pairs={{0,3},{1,0},{2,1},{3,2},{4,7},{5,4},{6,5},{7,6},{8,11},{9,8},{10,9... | collective-permute-start | bytes 1179656 | tf_op jit(solution)/shard_map/ppermute | solution.py:361
  32.5 2.0 %collective-permute-start.17 = (bf16[16,48,256]{2,1,0:T(8,128)(2,1)}, bf16[16,48,256]{2,1,0:T(8,128)(2,1)S(1)}, u32[]{:S(2)}, u32[]{:S(2)}) collective-permute-start(bf16[16,48,256]{2,1,0:T(8,128)(2,1)} %get-tuple-element.30.q0), channel_id=1, source_target_pairs={{0,3},{1,0},{2,1},{3,2},{4,7},{5,4},{6,5},{7,6},{8,11},{9,8},{10,9... | collective-permute-start | bytes 1179656 | tf_op jit(solution)/shard_map/ppermute | solution.py:361
  35.9 1.6 %copy-done.1 = bf16[4,256,1024]{2,1,0:T(8,128)(2,1)S(1)} copy-done((bf16[4,256,1024]{2,1,0:T(8,128)(2,1)S(1)}, bf16[4,256,1024]{2,1,0:T(8,128)(2,1)}, u32[]{:S(2)}) %copy-start.1) | copy-done | bytes 2097176
  38.5 3.2 %turn.1.v0 = bf16[8,512,256]{2,1,0:T(8,128)(2,1)S(1)} custom-call(s32[4]{0:T(128)S(1)} %pad_add_fusion.me, bf16[4,256,1024]{2,1,0:T(8,128)(2,1)S(1)} %copy-done.1, bf16[4,256,1024]{2,1,0:T(8,128)(2,1)} %collective-permute-done.8.v.v1, bf16[16,48,256]{2,1,0:T(8,128)(2,1)S(1)} %copy-done.2), custom_call_target="tpu_custom_call" | custom-call | flops 1000000 | bytes 8388608 | tf_op jit(solution)/shard_map/turn/pallas_call | solution.py:234
  41.8 2.0 %collective-permute-done.9.q1 = bf16[16,48,256]{2,1,0:T(8,128)(2,1)S(1)} collective-permute-done((bf16[16,48,256]{2,1,0:T(8,128)(2,1)}, bf16[16,48,256]{2,1,0:T(8,128)(2,1)S(1)}, u32[]{:S(2)}, u32[]{:S(2)}) %collective-permute-start.9) | collective-permute-done | bytes 393248 | tf_op jit(solution)/shard_map/ppermute | solution.py:361
  43.8 12.4 %attend.2 = (bf16[16,56,256]{2,1,0:T(8,128)(2,1)S(1)}, bf16[16,56,256]{2,1,0:T(8,128)(2,1)S(1)}, bf16[16,56,256]{2,1,0:T(8,128)(2,1)S(1)}, bf16[16,56,256]{2,1,0:T(8,128)(2,1)S(1)}) custom-call(s32[4]{0:T(128)S(1)} %pad_add_fusion.me, s32[12]{0:T(128)S(1)} %get-tuple-element.50.cnt, s32[96]{0:T(128)S(1)} %reshape.37.lst, bf16[16,48,256]{2,1,0:T(8,128)(2,1)S(1)} %copy-done.3, ...), custom_call_target="tpu_custom_call" | custom-call | flops 10000000000 | bytes 8388608 | tf_op jit(solution)/shard_map/attend/pallas_call | solution.py:185
  58.1 12.4 %attend.3 = (bf16[16,56,256]{2,1,0:T(8,128)(2,1)S(1)}, bf16[16,56,256]{2,1,0:T(8,128)(2,1)S(1)}, bf16[16,56,256]{2,1,0:T(8,128)(2,1)S(1)}, bf16[16,56,256]{2,1,0:T(8,128)(2,1)S(1)}) custom-call(s32[4]{0:T(128)S(1)} %pad_add_fusion.me, s32[12]{0:T(128)S(1)} %get-tuple-element.50.cnt, s32[96]{0:T(128)S(1)} %reshape.37.lst, bf16[16,48,256]{2,1,0:T(8,128)(2,1)S(1)} %copy-done.7, ...), custom_call_target="tpu_custom_call" | custom-call | flops 10000000000 | bytes 8388608 | tf_op jit(solution)/shard_map/attend/pallas_call | solution.py:185
  70.5 2.8 %collective-permute-start.18 = (bf16[16,56,256]{2,1,0:T(8,128)(2,1)S(1)}, bf16[16,56,256]{2,1,0:T(8,128)(2,1)S(1)}, u32[]{:S(2)}, u32[]{:S(2)}) collective-permute-start(bf16[16,56,256]{2,1,0:T(8,128)(2,1)S(1)} %get-tuple-element.32), channel_id=1, source_target_pairs={{0,3},{1,0},{2,1},{3,2},{4,7},{5,4},{6,5},{7,6},{8,11},{9,8},{10,9... | collective-permute-start | bytes 1376264 | tf_op jit(solution)/shard_map/ppermute | solution.py:361
  74.0 9.7 %collective-permute-done.18.refs_5_ = bf16[16,56,256]{2,1,0:T(8,128)(2,1)S(1)} collective-permute-done((bf16[16,56,256]{2,1,0:T(8,128)(2,1)S(1)}, bf16[16,56,256]{2,1,0:T(8,128)(2,1)S(1)}, u32[]{:S(2)}, u32[]{:S(2)}) %collective-permute-start.18) | collective-permute-done | bytes 458784 | tf_op jit(solution)/shard_map/ppermute | solution.py:361
  83.6 3.4 %collective-permute-done.20.refs_7_ = bf16[16,56,256]{2,1,0:T(8,128)(2,1)S(1)} collective-permute-done((bf16[16,56,256]{2,1,0:T(8,128)(2,1)S(1)}, bf16[16,56,256]{2,1,0:T(8,128)(2,1)S(1)}, u32[]{:S(2)}, u32[]{:S(2)}) %collective-permute-start.20) | collective-permute-done | bytes 458784 | tf_op jit(solution)/shard_map/ppermute | solution.py:361
  87.0 2.2 %merge.2 = (bf16[8,56,256]{2,1,0:T(8,128)(2,1)S(1)}, bf16[8,56,256]{2,1,0:T(8,128)(2,1)S(1)}, bf16[8,56,256]{2,1,0:T(8,128)(2,1)S(1)}, bf16[8,56,256]{2,1,0:T(8,128)(2,1)S(1)}) custom-call(bf16[16,56,256]{2,1,0:T(8,128)(2,1)S(1)} %get-tuple-element.26.refs_0_, bf16[16,56,256]{2,1,0:T(8,128)(2,1)S(1)} %collective-permute-done.12.refs_1_, ...), custom_call_target="tpu_custom_call" | custom-call | tf_op jit(solution)/shard_map/merge/pallas_call | solution.py:313
  90.8 3.4 %collective-permute-done.21.refs_1_ = bf16[8,56,256]{2,1,0:T(8,128)(2,1)S(1)} collective-permute-done((bf16[8,56,256]{2,1,0:T(8,128)(2,1)S(1)}, bf16[8,56,256]{2,1,0:T(8,128)(2,1)S(1)}, u32[]{:S(2)}, u32[]{:S(2)}) %collective-permute-start.21) | collective-permute-done | bytes 229408 | tf_op jit(solution)/shard_map/ppermute | solution.py:361
  94.2 1.7 %collective-permute-done.22.refs_2_ = bf16[8,56,256]{2,1,0:T(8,128)(2,1)S(1)} collective-permute-done((bf16[8,56,256]{2,1,0:T(8,128)(2,1)S(1)}, bf16[8,56,256]{2,1,0:T(8,128)(2,1)S(1)}, u32[]{:S(2)}, u32[]{:S(2)}) %collective-permute-start.22) | collective-permute-done | bytes 229408 | tf_op jit(solution)/shard_map/ppermute | solution.py:361
  95.9 2.4 %collective-permute-done.23.refs_3_ = bf16[8,56,256]{2,1,0:T(8,128)(2,1)S(1)} collective-permute-done((bf16[8,56,256]{2,1,0:T(8,128)(2,1)S(1)}, bf16[8,56,256]{2,1,0:T(8,128)(2,1)S(1)}, u32[]{:S(2)}, u32[]{:S(2)}) %collective-permute-start.23) | collective-permute-done | bytes 229408 | tf_op jit(solution)/shard_map/ppermute | solution.py:361
  100.8 1.9 %collective-permute-done.24.p1 = bf16[2,56,256]{2,1,0:T(8,128)(2,1)S(1)} collective-permute-done((bf16[2,56,256]{2,1,0:T(8,128)(2,1)S(1)}, bf16[2,56,256]{2,1,0:T(8,128)(2,1)S(1)}, u32[]{:S(2)}, u32[]{:S(2)}) %collective-permute-start.24) | collective-permute-done | bytes 57376 | tf_op jit(solution)/shard_map/ppermute | solution.py:361
  102.7 2.0 %collective-permute-done.25.p2 = bf16[2,56,256]{2,1,0:T(8,128)(2,1)S(1)} collective-permute-done((bf16[2,56,256]{2,1,0:T(8,128)(2,1)S(1)}, bf16[2,56,256]{2,1,0:T(8,128)(2,1)S(1)}, u32[]{:S(2)}, u32[]{:S(2)}) %collective-permute-start.25) | collective-permute-done | bytes 57376 | tf_op jit(solution)/shard_map/ppermute | solution.py:361
  105.8 1.9 %close.1 = (bf16[24,512]{1,0:T(8,128)(2,1)}, bf16[24,512]{1,0:T(8,128)(2,1)}) custom-call(s32[4]{0:T(128)} %copy-done.5, bf16[2,56,256]{2,1,0:T(8,128)(2,1)} %copy-done.4, bf16[2,56,256]{2,1,0:T(8,128)(2,1)} %copy-done.12, bf16[2,56,256]{2,1,0:T(8,128)(2,1)} %copy-done.13, bf16[2,56,256]{2,1,0:T(8,128)(2,1)} %copy-done.14), custom_call_target="tpu_custom_call" | custom-call | tf_op jit(solution)/shard_map/close/pallas_call | solution.py:341
  107.8 8.7 %collective-permute-start.27 = (bf16[24,512]{1,0:T(8,128)(2,1)}, bf16[24,512]{1,0:T(8,128)(2,1)S(1)}, u32[]{:S(2)}, u32[]{:S(2)}) collective-permute-start(bf16[24,512]{1,0:T(8,128)(2,1)} %get-tuple-element.44), channel_id=1, source_target_pairs={{0,16},{16,0},{1,17},{17,1},{2,18},{18,2},{3,19},{19,3},{4,20},{20... | collective-permute-start | bytes 73736 | tf_op jit(solution)/shard_map/ppermute | solution.py:352
  (89 shorter events, 27.0 us)
Async XLA Ops:
  0.0 25.7 %collective-permute-start.8 = (bf16[4,256,1024]{2,1,0:T(8,128)(2,1)}, bf16[4,256,1024]{2,1,0:T(8,128)(2,1)}, u32[]{:S(2)}, u32[]{:S(2)}) collective-permute-start(bf16[4,256,1024]{2,1,0:T(8,128)(2,1)} %v0.1), channel_id=1, source_target_pairs={{0,16},{16,0},{1,17},{17,1},{2,18},{18,2},{3,19},{19,3},{4,20},{20... | collective-permute-start | bytes 6291464 | tf_op jit(solution)/shard_map/ppermute | solution.py:352
  1.4 24.2 %collective-permute-start.7 = (bf16[4,256,1024]{2,1,0:T(8,128)(2,1)}, bf16[4,256,1024]{2,1,0:T(8,128)(2,1)}, u32[]{:S(2)}, u32[]{:S(2)}) collective-permute-start(bf16[4,256,1024]{2,1,0:T(8,128)(2,1)} %k0.3), channel_id=1, source_target_pairs={{0,16},{16,0},{1,17},{17,1},{2,18},{18,2},{3,19},{19,3},{4,20},{20... | collective-permute-start | bytes 6291464 | tf_op jit(solution)/shard_map/ppermute | solution.py:352
  6.0 5.1 %collective-permute-start.3 = (bf16[1,48,512]{2,1,0:T(8,128)(2,1)S(1)}, bf16[1,48,512]{2,1,0:T(8,128)(2,1)S(1)}, u32[]{:S(2)}, u32[]{:S(2)}) collective-permute-start(bf16[1,48,512]{2,1,0:T(8,128)(2,1)S(1)} %maximum_bitcast_fusion), channel_id=1, source_target_pairs={{0,12},{1,13},{2,14},{3,15},{4,0},{5,1},{6,2},{7,3},{8,4},{9,5},{1... | collective-permute-start | bytes 147464 | tf_op jit(solution)/shard_map/ppermute | solution.py:361
  10.0 4.7 %collective-permute-start.1 = (bf16[1,48,512]{2,1,0:T(8,128)(2,1)S(1)}, bf16[1,48,512]{2,1,0:T(8,128)(2,1)S(1)}, u32[]{:S(2)}, u32[]{:S(2)}) collective-permute-start(bf16[1,48,512]{2,1,0:T(8,128)(2,1)S(1)} %maximum_bitcast_fusion), channel_id=1, source_target_pairs={{0,4},{1,5},{2,6},{3,7},{4,8},{5,9},{6,10},{7,11},{8,12},{9,13},{1... | collective-permute-start | bytes 147464 | tf_op jit(solution)/shard_map/ppermute | solution.py:361
  14.7 7.3 %collective-permute-start.6 = (bf16[4,48,512]{2,1,0:T(8,128)(2,1)S(1)}, bf16[4,48,512]{2,1,0:T(8,128)(2,1)S(1)}, u32[]{:S(2)}, u32[]{:S(2)}) collective-permute-start(bf16[4,48,512]{2,1,0:T(8,128)(2,1)S(1)} %pad_maximum_fusion.p0), channel_id=1, source_target_pairs={{0,96},{1,97},{2,98},{3,99},{4,100},{5,101},{6,102},{7,103},{8,104... | collective-permute-start | bytes 589832 | tf_op jit(solution)/shard_map/ppermute | solution.py:361
  17.2 6.1 %collective-permute-start.5 = (bf16[4,48,512]{2,1,0:T(8,128)(2,1)S(1)}, bf16[4,48,512]{2,1,0:T(8,128)(2,1)S(1)}, u32[]{:S(2)}, u32[]{:S(2)}) collective-permute-start(bf16[4,48,512]{2,1,0:T(8,128)(2,1)S(1)} %pad_maximum_fusion.p0), channel_id=1, source_target_pairs={{0,64},{1,65},{2,66},{3,67},{4,68},{5,69},{6,70},{7,71},{8,72},{9,... | collective-permute-start | bytes 589832 | tf_op jit(solution)/shard_map/ppermute | solution.py:361
  17.7 7.9 %collective-permute-start.4 = (bf16[4,48,512]{2,1,0:T(8,128)(2,1)S(1)}, bf16[4,48,512]{2,1,0:T(8,128)(2,1)S(1)}, u32[]{:S(2)}, u32[]{:S(2)}) collective-permute-start(bf16[4,48,512]{2,1,0:T(8,128)(2,1)S(1)} %pad_maximum_fusion.p0), channel_id=1, source_target_pairs={{0,32},{1,33},{2,34},{3,35},{4,36},{5,37},{6,38},{7,39},{8,40},{9,... | collective-permute-start | bytes 589832 | tf_op jit(solution)/shard_map/ppermute | solution.py:361
  28.5 13.2 %collective-permute-start.11 = (bf16[16,48,256]{2,1,0:T(8,128)(2,1)}, bf16[16,48,256]{2,1,0:T(8,128)(2,1)S(1)}, u32[]{:S(2)}, u32[]{:S(2)}) collective-permute-start(bf16[16,48,256]{2,1,0:T(8,128)(2,1)} %get-tuple-element.25.q.q0), channel_id=1, source_target_pairs={{0,3},{1,0},{2,1},{3,2},{4,7},{5,4},{6,5},{7,6},{8,11},{9,8},{10,9... | collective-permute-start | bytes 1179656 | tf_op jit(solution)/shard_map/ppermute | solution.py:361
  31.0 10.8 %collective-permute-start.10 = (bf16[16,48,256]{2,1,0:T(8,128)(2,1)}, bf16[16,48,256]{2,1,0:T(8,128)(2,1)S(1)}, u32[]{:S(2)}, u32[]{:S(2)}) collective-permute-start(bf16[16,48,256]{2,1,0:T(8,128)(2,1)} %get-tuple-element.25.q.q0), channel_id=1, source_target_pairs={{0,2},{1,3},{2,0},{3,1},{4,6},{5,7},{6,4},{7,5},{8,10},{9,11},{10,... | collective-permute-start | bytes 1179656 | tf_op jit(solution)/shard_map/ppermute | solution.py:361
  31.3 12.5 %collective-permute-start.9 = (bf16[16,48,256]{2,1,0:T(8,128)(2,1)}, bf16[16,48,256]{2,1,0:T(8,128)(2,1)S(1)}, u32[]{:S(2)}, u32[]{:S(2)}) collective-permute-start(bf16[16,48,256]{2,1,0:T(8,128)(2,1)} %get-tuple-element.25.q.q0), channel_id=1, source_target_pairs={{0,1},{1,2},{2,3},{3,0},{4,5},{5,6},{6,7},{7,4},{8,9},{9,10},{10,1... | collective-permute-start | bytes 1179656 | tf_op jit(solution)/shard_map/ppermute | solution.py:361
  32.5 24.9 %collective-permute-start.17 = (bf16[16,48,256]{2,1,0:T(8,128)(2,1)}, bf16[16,48,256]{2,1,0:T(8,128)(2,1)S(1)}, u32[]{:S(2)}, u32[]{:S(2)}) collective-permute-start(bf16[16,48,256]{2,1,0:T(8,128)(2,1)} %get-tuple-element.30.q0), channel_id=1, source_target_pairs={{0,3},{1,0},{2,1},{3,2},{4,7},{5,4},{6,5},{7,6},{8,11},{9,8},{10,9... | collective-permute-start | bytes 1179656 | tf_op jit(solution)/shard_map/ppermute | solution.py:361
  34.5 23.6 %collective-permute-start.16 = (bf16[16,48,256]{2,1,0:T(8,128)(2,1)}, bf16[16,48,256]{2,1,0:T(8,128)(2,1)S(1)}, u32[]{:S(2)}, u32[]{:S(2)}) collective-permute-start(bf16[16,48,256]{2,1,0:T(8,128)(2,1)} %get-tuple-element.30.q0), channel_id=1, source_target_pairs={{0,2},{1,3},{2,0},{3,1},{4,6},{5,7},{6,4},{7,5},{8,10},{9,11},{10,... | collective-permute-start | bytes 1179656 | tf_op jit(solution)/shard_map/ppermute | solution.py:361
  41.7 16.4 %collective-permute-start.15 = (bf16[16,48,256]{2,1,0:T(8,128)(2,1)S(1)}, bf16[16,48,256]{2,1,0:T(8,128)(2,1)S(1)}, u32[]{:S(2)}, u32[]{:S(2)}) collective-permute-start(bf16[16,48,256]{2,1,0:T(8,128)(2,1)S(1)} %copy-done.7), channel_id=1, source_target_pairs={{0,1},{1,2},{2,3},{3,0},{4,5},{5,6},{6,7},{7,4},{8,9},{9,10},{10,1... | collective-permute-start | bytes 1179656 | tf_op jit(solution)/shard_map/ppermute | solution.py:361
  56.2 17.1 %collective-permute-start.12 = (bf16[16,56,256]{2,1,0:T(8,128)(2,1)S(1)}, bf16[16,56,256]{2,1,0:T(8,128)(2,1)S(1)}, u32[]{:S(2)}, u32[]{:S(2)}) collective-permute-start(bf16[16,56,256]{2,1,0:T(8,128)(2,1)S(1)} %get-tuple-element.27), channel_id=1, source_target_pairs={{0,3},{1,0},{2,1},{3,2},{4,7},{5,4},{6,5},{7,6},{8,11},{9,8},{10,9... | collective-permute-start | bytes 1376264 | tf_op jit(solution)/shard_map/ppermute | solution.py:361
  57.4 16.6 %collective-permute-start.13 = (bf16[16,56,256]{2,1,0:T(8,128)(2,1)S(1)}, bf16[16,56,256]{2,1,0:T(8,128)(2,1)S(1)}, u32[]{:S(2)}, u32[]{:S(2)}) collective-permute-start(bf16[16,56,256]{2,1,0:T(8,128)(2,1)S(1)} %get-tuple-element.28), channel_id=1, source_target_pairs={{0,2},{1,3},{2,0},{3,1},{4,6},{5,7},{6,4},{7,5},{8,10},{9,11},{10,... | collective-permute-start | bytes 1376264 | tf_op jit(solution)/shard_map/ppermute | solution.py:361
  57.4 16.6 %collective-permute-start.14 = (bf16[16,56,256]{2,1,0:T(8,128)(2,1)S(1)}, bf16[16,56,256]{2,1,0:T(8,128)(2,1)S(1)}, u32[]{:S(2)}, u32[]{:S(2)}) collective-permute-start(bf16[16,56,256]{2,1,0:T(8,128)(2,1)S(1)} %get-tuple-element.29), channel_id=1, source_target_pairs={{0,1},{1,2},{2,3},{3,0},{4,5},{5,6},{6,7},{7,4},{8,9},{9,10},{10,1... | collective-permute-start | bytes 1376264 | tf_op jit(solution)/shard_map/ppermute | solution.py:361
  70.5 13.1 %collective-permute-start.18 = (bf16[16,56,256]{2,1,0:T(8,128)(2,1)S(1)}, bf16[16,56,256]{2,1,0:T(8,128)(2,1)S(1)}, u32[]{:S(2)}, u32[]{:S(2)}) collective-permute-start(bf16[16,56,256]{2,1,0:T(8,128)(2,1)S(1)} %get-tuple-element.32), channel_id=1, source_target_pairs={{0,3},{1,0},{2,1},{3,2},{4,7},{5,4},{6,5},{7,6},{8,11},{9,8},{10,9... | collective-permute-start | bytes 1376264 | tf_op jit(solution)/shard_map/ppermute | solution.py:361
  73.3 10.3 %collective-permute-start.19 = (bf16[16,56,256]{2,1,0:T(8,128)(2,1)S(1)}, bf16[16,56,256]{2,1,0:T(8,128)(2,1)S(1)}, u32[]{:S(2)}, u32[]{:S(2)}) collective-permute-start(bf16[16,56,256]{2,1,0:T(8,128)(2,1)S(1)} %get-tuple-element.33), channel_id=1, source_target_pairs={{0,2},{1,3},{2,0},{3,1},{4,6},{5,7},{6,4},{7,5},{8,10},{9,11},{10,... | collective-permute-start | bytes 1376264 | tf_op jit(solution)/shard_map/ppermute | solution.py:361
  73.3 13.8 %collective-permute-start.20 = (bf16[16,56,256]{2,1,0:T(8,128)(2,1)S(1)}, bf16[16,56,256]{2,1,0:T(8,128)(2,1)S(1)}, u32[]{:S(2)}, u32[]{:S(2)}) collective-permute-start(bf16[16,56,256]{2,1,0:T(8,128)(2,1)S(1)} %get-tuple-element.34), channel_id=1, source_target_pairs={{0,1},{1,2},{2,3},{3,0},{4,5},{5,6},{6,7},{7,4},{8,9},{9,10},{10,1... | collective-permute-start | bytes 1376264 | tf_op jit(solution)/shard_map/ppermute | solution.py:361
  89.3 4.9 %collective-permute-start.21 = (bf16[8,56,256]{2,1,0:T(8,128)(2,1)S(1)}, bf16[8,56,256]{2,1,0:T(8,128)(2,1)S(1)}, u32[]{:S(2)}, u32[]{:S(2)}) collective-permute-start(bf16[8,56,256]{2,1,0:T(8,128)(2,1)S(1)} %get-tuple-element.36), channel_id=1, source_target_pairs={{0,96},{1,97},{2,98},{3,99},{4,100},{5,101},{6,102},{7,103},{8,104... | collective-permute-start | bytes 688136 | tf_op jit(solution)/shard_map/ppermute | solution.py:361
  89.3 6.6 %collective-permute-start.22 = (bf16[8,56,256]{2,1,0:T(8,128)(2,1)S(1)}, bf16[8,56,256]{2,1,0:T(8,128)(2,1)S(1)}, u32[]{:S(2)}, u32[]{:S(2)}) collective-permute-start(bf16[8,56,256]{2,1,0:T(8,128)(2,1)S(1)} %get-tuple-element.37), channel_id=1, source_target_pairs={{0,64},{1,65},{2,66},{3,67},{4,68},{5,69},{6,70},{7,71},{8,72},{9,... | collective-permute-start | bytes 688136 | tf_op jit(solution)/shard_map/ppermute | solution.py:361
  89.4 8.8 %collective-permute-start.23 = (bf16[8,56,256]{2,1,0:T(8,128)(2,1)S(1)}, bf16[8,56,256]{2,1,0:T(8,128)(2,1)S(1)}, u32[]{:S(2)}, u32[]{:S(2)}) collective-permute-start(bf16[8,56,256]{2,1,0:T(8,128)(2,1)S(1)} %get-tuple-element.38), channel_id=1, source_target_pairs={{0,32},{1,33},{2,34},{3,35},{4,36},{5,37},{6,38},{7,39},{8,40},{9,... | collective-permute-start | bytes 688136 | tf_op jit(solution)/shard_map/ppermute | solution.py:361
  100.1 5.1 %collective-permute-start.26 = (bf16[2,56,256]{2,1,0:T(8,128)(2,1)S(1)}, bf16[2,56,256]{2,1,0:T(8,128)(2,1)S(1)}, u32[]{:S(2)}, u32[]{:S(2)}) collective-permute-start(bf16[2,56,256]{2,1,0:T(8,128)(2,1)S(1)} %get-tuple-element.42), channel_id=1, source_target_pairs={{0,4},{1,5},{2,6},{3,7},{4,8},{5,9},{6,10},{7,11},{8,12},{9,13},{1... | collective-permute-start | bytes 172040 | tf_op jit(solution)/shard_map/ppermute | solution.py:361
  107.8 9.7 %collective-permute-start.27 = (bf16[24,512]{1,0:T(8,128)(2,1)}, bf16[24,512]{1,0:T(8,128)(2,1)S(1)}, u32[]{:S(2)}, u32[]{:S(2)}) collective-permute-start(bf16[24,512]{1,0:T(8,128)(2,1)} %get-tuple-element.44), channel_id=1, source_target_pairs={{0,16},{16,0},{1,17},{17,1},{2,18},{18,2},{3,19},{19,3},{4,20},{20... | collective-permute-start | bytes 73736 | tf_op jit(solution)/shard_map/ppermute | solution.py:352
  (19 other events, 198.1 us)

commit v3 on v2

--- a/solution.py
+++ b/solution.py
@@ -23,7 +23,7 @@
     me, cnt, lst, q0, q1, q2, q3, k0, k1, v0, o0, o1, o2, o3,
     pq, pj, ps, qv, k, vt, qm, acc, sb, top, shrink, yb, sem, *, part,
 ):
-    my_y, my_core, my_z, my_x = me[0], me[1], me[2], me[3]
+    my_y, my_core, my_x = me[0], me[1], me[3]
     col = pl.multiple_of(my_core * 512 + part * WIDE, WIDE)
     copies = [
         pltpu.make_async_copy(src, dst, sem.at[i])
@@ -59,24 +59,17 @@
         pj[total + u] = 0
         ps[total + u] = spare
 
-    def place(r2, r3, rz):
+    def place(r2, r3, z):
         y = lax.rem(my_y + 4 - jnp.where(my_core == 0, r2, r3), 4)
         x = lax.rem(my_x + 4 - jnp.where(my_core == 0, r3, r2), 4)
-        z = lax.rem(my_z + 4 - rz, 4)
         return [pl.multiple_of(y * 768 + (c * 16 + z * 4 + x) * 24, 8) for c in range(2)]
 
     for r3 in range(4):
         copies[r3].wait()
-
-        def load(r2, _, r3=r3):
-            for rz in range(4):
-                block = qv[r3, r2 * 4 + rz].astype(F32)
-                for c, row in enumerate(place(r2, r3, rz)):
-                    yb[pl.ds(row, 24), :WIDE] = block[c * 24:(c + 1) * 24]
-            return 0
-
         for r2 in range(4):
-            load(r2, 0)
+            for z in range(4):
+                for c, row in enumerate(place(r2, r3, z)):
+                    yb[pl.ds(row, 24), :WIDE] = qv[r3, r2 * 8 + c * 4 + z].astype(F32)
 
     def turn(qi, _):
         rows = pl.ds(pl.multiple_of(qi * 256, 256), 256)
@@ -159,11 +152,10 @@
     lax.fori_loop(0, (total + 1) // 2, two, 0)
 
     for r3, o in enumerate((o0, o1, o2, o3)):
-
-        def emit(r2, _, o=o, r3=r3):
-            for rz in range(4):
+        for r2 in range(4):
+            for z in range(4):
                 data, tail = [], jnp.zeros((8, 128), F32)
-                for c, row in enumerate(place(r2, r3, rz)):
+                for c, row in enumerate(place(r2, r3, z)):
                     block = yb[pl.ds(row, 24), :]
                     data.append(block[:, :WIDE])
                     for p in range(3):
@@ -171,11 +163,7 @@
                         g = c * 3 + p
                         tail = tail + (pltpu.roll(piece, 16 * g, 1) if g else piece)
                 data.append(jnp.concatenate([tail, jnp.zeros((8, WIDE - 128), F32)], axis=1))
-                o[r2 * 4 + rz] = jnp.concatenate(data, axis=0).astype(BF16)
-            return 0
-
-        for r2 in range(4):
-            emit(r2, 0)
+                o[r2 * 4 + z] = jnp.concatenate(data, axis=0).astype(BF16)
 
 
 def attend(me, cnt, lst, q, k0, k1, v0, part):
@@ -191,7 +179,7 @@
             pltpu.SMEM((104,), jnp.int32),
             pltpu.SMEM((104,), jnp.int32),
             pltpu.SMEM((104,), jnp.int32),
-            pltpu.VMEM((4, 16, 48, WIDE), BF16),
+            pltpu.VMEM((4, 32, 24, WIDE), BF16),
             pltpu.VMEM((8, 256, WIDE), BF16),
             pltpu.VMEM((8, WIDE, 256), BF16),
             pltpu.VMEM((13, NH, 128, 256), BF16),
@@ -243,37 +231,47 @@
     )(me, v0, v1, q)
 
 
-def pack_kernel(p0, p1, p2, p3, k, v, o0, o1):
+def pack_kernel(p0, p1, p2, p3, k, v, o0, o1, sem):
+    copies = []
     for at, p in enumerate((p0, p1, p2, p3)):
         for c, o in enumerate((o0, o1)):
-            o[at * 4:at * 4 + 4] = p[:, :, c * WIDE:(c + 1) * WIDE]
+            copies.append(
+                pltpu.make_async_copy(
+                    p.at[:, :, pl.ds(c * WIDE, WIDE)], o.at[pl.ds(at * 8, 8)], sem.at[at * 2 + c]
+                )
+            )
+    for copy in copies:
+        copy.start()
+    for copy in copies:
+        copy.wait()
 
 
 def pack(parts, k, v):
-    vmem = pl.BlockSpec(memory_space=pltpu.VMEM)
     whole = pl.BlockSpec(memory_space=pl.ANY)
     return pl.pallas_call(
         pack_kernel,
-        out_shape=[jax.ShapeDtypeStruct((16, 48, WIDE), BF16)] * 2,
-        in_specs=[vmem] * 4 + [whole] * 2,
-        out_specs=[vmem] * 2,
+        out_shape=[jax.ShapeDtypeStruct((32, 24, WIDE), BF16)] * 2,
+        in_specs=[whole] * 6,
+        out_specs=[whole] * 2,
+        scratch_shapes=[pltpu.SemaphoreType.DMA((8,))],
         name="pack",
     )(*parts, k, v)
 
 
-def add_up(parts, spread):
-    tails = [p[48:56, :128].astype(F32) for p in parts]
+def add_up(data, tails, spread):
+    n = len(data)
     best = functools.reduce(jnp.maximum, tails)
     shares = [jnp.exp2(jnp.minimum(t - best, 0.0)) for t in tails]
     total = sum(f * (pltpu.roll(t, 128 - NH, 1) + pltpu.roll(t, 128 - 2 * NH, 1)) for f, t in zip(shares, tails))
     stack = jnp.concatenate(shares, axis=0)
-    stack = jnp.concatenate([stack] + [pltpu.roll(stack, 128 - 16 * g, 1) for g in range(1, 6)], axis=0)
+    groups = data[0].shape[0] // 8
+    stack = jnp.concatenate([stack] + [pltpu.roll(stack, 128 - 16 * g, 1) for g in range(1, groups)], axis=0)
     wide = jnp.dot(stack.astype(BF16), spread, preferred_element_type=F32)
     numer = []
-    for g in range(6):
-        at = g * 8 * len(parts)
+    for g in range(groups):
+        at = g * 8 * n
         numer.append(
-            sum(wide[at + s * 8:at + s * 8 + 8] * p[g * 8:g * 8 + 8, :].astype(F32) for s, p in enumerate(parts))
+            sum(wide[at + s * 8:at + s * 8 + 8] * d[g * 8:g * 8 + 8, :].astype(F32) for s, d in enumerate(data))
         )
     return numer, best, total
 
@@ -284,68 +282,88 @@
     return src == dst
 
 
-def merge_kernel(*refs, joint, blocks):
-    parts, outs = refs[:-4], refs[-4:]
+def add_blocks(held, spread, is_top):
+    data, tails = [p[:48] for p in held], [p[48:56, :128].astype(F32) for p in held]
+    numer, best, total = add_up(data, tails, spread)
+    total = jnp.where(is_top, total, 0.0)
+    hi = total.astype(BF16).astype(F32)
+    tail = jnp.where(is_top, best, 0.0) + pltpu.roll(hi, NH, 1) + pltpu.roll(total - hi, 2 * NH, 1)
+    return numer, jnp.concatenate([tail, jnp.zeros((8, WIDE - 128), F32)], axis=1)
+
+
+def merge_kernel(*refs):
+    parts, outs = refs[:8], refs[8:]
     spread = make_spread().astype(BF16)
     is_top = lax.broadcasted_iota(jnp.int32, (8, 128), 1) % 16 < NH
     for r, out in enumerate(outs):
-
-        def one(b, _, r=r, out=out):
+        for z in range(4):
             for c in range(2):
-                if joint:
-                    held = [p[(r * blocks + b) * 2 + c] for p in parts]
-                else:
-                    held = [p[r * blocks + b] for p in parts[c * 4:c * 4 + 4]]
-                numer, best, total = add_up(held, spread)
-                total = jnp.where(is_top, total, 0.0)
-                hi = total.astype(BF16).astype(F32)
-                tail = jnp.where(is_top, best, 0.0) + pltpu.roll(hi, NH, 1) + pltpu.roll(total - hi, 2 * NH, 1)
-                tail = jnp.concatenate([tail, jnp.zeros((8, WIDE - 128), F32)], axis=1)
-                out[b * 2 + c] = jnp.concatenate(numer + [tail], axis=0).astype(BF16)
-            return 0
-
-        for b in range(blocks):
-            one(b, 0)
-
-
-def merge(parts, blocks):
+                numer, tail = add_blocks([p[r * 4 + z] for p in parts[c * 4:c * 4 + 4]], spread, is_top)
+                out[z * 2 + c] = jnp.concatenate(numer + [tail], axis=0).astype(BF16)
+
+
+def merge(parts):
     vmem = pl.BlockSpec(memory_space=pltpu.VMEM)
     return pl.pallas_call(
-        functools.partial(merge_kernel, joint=len(parts) == 4, blocks=blocks),
-        out_shape=[jax.ShapeDtypeStruct((blocks * 2, 56, WIDE), BF16)] * 4,
-        in_specs=[vmem] * len(parts),
+        merge_kernel,
+        out_shape=[jax.ShapeDtypeStruct((8, 56, WIDE), BF16)] * 4,
+        in_specs=[vmem] * 8,
         out_specs=[vmem] * 4,
         compiler_params=pltpu.CompilerParams(vmem_limit_bytes=32 * 2**20),
         name="merge",
     )(*parts)
 
 
-def close_kernel(me, p0, p1, p2, p3, keep, give, both):
-    parts = (p0, p1, p2, p3)
+def split_kernel(p0, p1, p2, p3, out):
+    spread = make_spread().astype(BF16)
+    is_top = lax.broadcasted_iota(jnp.int32, (8, 128), 1) % 16 < NH
+    for z in range(4):
+        for c in range(2):
+            numer, tail = add_blocks([p[z * 2 + c] for p in (p0, p1, p2, p3)], spread, is_top)
+            for core in range(2):
+                rows = jnp.concatenate(numer[core * 3:core * 3 + 3] + [tail], axis=0)
+                out[core * 4 + z, c] = rows.astype(BF16)
+
+
+def split(parts):
+    vmem = pl.BlockSpec(memory_space=pltpu.VMEM)
+    return pl.pallas_call(
+        split_kernel,
+        out_shape=jax.ShapeDtypeStruct((8, 2, 32, WIDE), BF16),
+        in_specs=[vmem] * 4,
+        out_specs=vmem,
+        name="split",
+    )(*parts)
+
+
+def close_kernel(me, got, weight, out, rows):
     spread = make_spread()
-    for c in range(2):
-        numer, _, total = add_up([p[c] for p in parts], spread.astype(BF16))
-        totals = jnp.concatenate([total] + [pltpu.roll(total, 128 - 16 * g, 1) for g in range(1, 6)], axis=0)
-        wide = jnp.dot(
-            totals, spread.astype(F32), precision=lax.Precision.HIGHEST, preferred_element_type=F32
-        )
-        both[:, c * WIDE:(c + 1) * WIDE] = jnp.concatenate(numer, axis=0) / wide
-    row = pl.multiple_of(me[1] * 24, 8)
-    keep[...] = both[pl.ds(row, 24), :].astype(BF16)
-    give[...] = both[pl.ds(24 - row, 24), :].astype(BF16)
-
-
-def close(me, parts):
+    for core in range(2):
+        for c in range(2):
+            held = [got[core * 4 + z, c] for z in range(4)]
+            tails = [p[24:32, :128].astype(F32) for p in held]
+            tails = [jnp.where(me[1] == 0, t, pltpu.roll(t, 128 - 48, 1)) for t in tails]
+            numer, _, total = add_up([p[:24] for p in held], tails, spread.astype(BF16))
+            totals = jnp.concatenate([total] + [pltpu.roll(total, 128 - 16 * g, 1) for g in range(1, 3)], axis=0)
+            wide = jnp.dot(
+                totals, spread.astype(F32), precision=lax.Precision.HIGHEST, preferred_element_type=F32
+            )
+            at = core * 512 + c * WIDE
+            rows[:, at:at + WIDE] = (jnp.concatenate(numer, axis=0) / wide).astype(BF16)
+    out[...] = jnp.dot(rows[...], weight[...], preferred_element_type=F32).astype(BF16)
+
+
+def close(me, got, weight):
     vmem = pl.BlockSpec(memory_space=pltpu.VMEM)
     smem = pl.BlockSpec(memory_space=pltpu.SMEM)
     return pl.pallas_call(
         close_kernel,
-        out_shape=[jax.ShapeDtypeStruct((24, 512), BF16)] * 2,
-        in_specs=[smem] + [vmem] * 4,
-        out_specs=[vmem] * 2,
-        scratch_shapes=[pltpu.VMEM((48, 512), F32)],
+        out_shape=jax.ShapeDtypeStruct((24, 1024), BF16),
+        in_specs=[smem, vmem, vmem],
+        out_specs=vmem,
+        scratch_shapes=[pltpu.VMEM((24, 1024), BF16)],
         name="close",
-    )(me, *parts)
+    )(me, got, weight)
 
 
 def swap(x):
@@ -373,14 +391,8 @@
     core = lax.axis_index("core")
     device = lax.axis_index(ALL)
     partner = device + 16 - 32 * core
-    own_col = core * 512
-    other_col = 512 - own_col
-
-    mine = lax.dynamic_slice_in_dim(queries, own_col, 512, 1)
-    theirs = swap(lax.dynamic_slice_in_dim(queries, other_col, 512, 1))
-    first = core == 0
-    pair = jnp.concatenate([jnp.where(first, mine, theirs), jnp.where(first, theirs, mine)], axis=0)
-    along_z = jnp.concatenate(ring(pair[None], "zz"), axis=0)
+    halves = jnp.stack([queries[:, :512]] * 4 + [queries[:, 512:]] * 4)
+    along_z = lax.all_to_all(halves, ("core", "z"), 0, 0)
     k_theirs, v_theirs = swap(keys), swap(values)
     planes = pack(ring(along_z, "yx"), k_theirs, v_theirs)
     me = jnp.stack([lax.axis_index(a) for a in ALL]).astype(jnp.int32)
@@ -403,12 +415,9 @@
     sent = []
     for c in range(2):
         sent += deliver(attend(me, cnt, lst, q_parts[c], keys, k_theirs, v_turned, c), "xy")
-    sent = deliver(merge(sent, 4), "yx")
-    sent = deliver(merge(sent, 1), "zz")
-    keep, give = close(me, sent)
-    give = swap(give)
-    rows = jnp.concatenate([jnp.where(first, keep, give), jnp.where(first, give, keep)], axis=1)
-    return jnp.dot(rows, out_weight, preferred_element_type=F32).astype(BF16)
+    sent = split(deliver(merge(sent), "yx"))
+    got = lax.all_to_all(sent, ("core", "z"), 0, 0)
+    return close(me, got, out_weight)
 
 
 def solution(mesh):

time: 120 us -> 158 us (1.32)
  Pallas kernels: 34.8 us -> 62.6 us
  blocking collectives: 0 us -> 19.4 us
  local copies, waits for them, and re-layouts: 5.6 us -> 18 us
  starting transfers between devices: 34.2 us -> 24.8 us
  waiting for transfers between devices: 38.8 us -> 30.4 us
    pallas_call x4, Pallas kernels: 6.79 us -> 32.9 us  [the longest x1 25 us: pack(): pl.pallas_call(pack_kernel, out_shape=[jax.ShapeDtypeStruct((32, 24, WIDE...]
    all_to_all x0 -> x1, blocking collectives: none -> 19.4 us  [body(): got = lax.all_to_all(sent, ('core', 'z'), 0, 0)]
    unnamed x30 -> x39, local copies, waits for them, and re-layouts: 4.52 us -> 16.3 us
    ppermute x24 -> x18, waiting for transfers between devices: 36 us -> 25.3 us  [shift(): return lax.ppermute(x, ALL, pairs)]
    ppermute x4 -> x2, starting transfers between devices: 10.7 us -> 1.42 us  [swap(): return lax.ppermute(x, 'core', [(0, 1), (1, 0)])]
    ppermute x24 -> x18, starting transfers between devices: 23.5 us -> 17.4 us  [shift(): return lax.ppermute(x, ALL, pairs)]
    all_to_all x0 -> x1, starting transfers between devices: none -> 5.9 us  [body(): along_z = lax.all_to_all(halves, ('core', 'z'), 0, 0)]
    all_to_all x0 -> x1, waiting for transfers between devices: none -> 5.08 us  [body(): along_z = lax.all_to_all(halves, ('core', 'z'), 0, 0)]
  transfers between devices with their start and end apart: 28 -> 21, of which waited for: 17 -> 11; matrix products, arithmetic and copies ran while one was open for 4% -> 9% of each run, Pallas kernels for 23% -> 19%
where the time goes in v3:
time: 158 us
  Pallas kernels  62.6 us (40%)
  waiting for transfers between devices  30.4 us (19%)
  starting transfers between devices  24.8 us (16%)
  blocking collectives  19.4 us (12%)
  local copies, waits for them, and re-layouts  18 us (11%)
  other arithmetic  3.12 us (2%)
    pallas_call x2, Pallas kernels, attend(): pl.pallas_call(functools.partial(attend_kernel, part=part), out_shape=[ja...  27.7 us
    ppermute x18, waiting for transfers between devices, shift(): return lax.ppermute(x, ALL, pairs)  25.3 us
    pallas_call x1, Pallas kernels, pack(): pl.pallas_call(pack_kernel, out_shape=[jax.ShapeDtypeStruct((32, 24, WIDE...  25 us
    all_to_all x1, blocking collectives, body(): got = lax.all_to_all(sent, ('core', 'z'), 0, 0)  19.4 us
    ppermute x18, starting transfers between devices, shift(): return lax.ppermute(x, ALL, pairs)  17.4 us
    unnamed x39, local copies, waits for them, and re-layouts  16.3 us
    all_to_all x1, starting transfers between devices, body(): along_z = lax.all_to_all(halves, ('core', 'z'), 0, 0)  5.9 us
    all_to_all x1, waiting for transfers between devices, body(): along_z = lax.all_to_all(halves, ('core', 'z'), 0, 0)  5.08 us
  transfers between devices with their start and end apart: 21, of which 11 were waited for; matrix products, arithmetic and copies ran while one was open for 9% of the time, Pallas kernels for 19%

profile of v3, /device:TPU:1, one launch (start us, length us, event | category | flops | bytes accessed | tf_op | source)
XLA Modules:
  0.0 158.4 jit_solution(12262411561437336104)
XLA Ops:
  12.2 5.9 %all-to-all-start = ((bf16[8,24,512]{2,1,0:T(8,128)(2,1)}), bf16[8,24,512]{2,1,0:T(8,128)(2,1)S(1)}, u32[]{:S(2)}, u32[]{:S(2)}) async-start(bf16[8,24,512]{2,1,0:T(8,128)(2,1)} %bitcast_dynamic-update-slice_fusion.3), calls=%async_computation | async-start | bytes 393216 | tf_op jit(solution)/shard_map/all_to_all | solution.py:395
  18.9 5.1 %all-to-all-done.p0 = bf16[8,24,512]{2,1,0:T(8,128)(2,1)S(1)} async-done(((bf16[8,24,512]{2,1,0:T(8,128)(2,1)}), bf16[8,24,512]{2,1,0:T(8,128)(2,1)S(1)}, u32[]{:S(2)}, u32[]{:S(2)}) %all-to-all-start) | async-done | bytes 196640 | tf_op jit(solution)/shard_map/all_to_all | solution.py:395
  24.0 2.5 %collective-permute-start.2 = (bf16[8,24,512]{2,1,0:T(8,128)(2,1)S(1)}, bf16[8,24,512]{2,1,0:T(8,128)(2,1)S(1)}, u32[]{:S(2)}, u32[]{:S(2)}) collective-permute-start(bf16[8,24,512]{2,1,0:T(8,128)(2,1)S(1)} %all-to-all-done.p0), channel_id=1, source_target_pairs={{0,96},{1,97},{2,98},{3,99},{4,100},{5,101},{6,102},{7,103},{8,104... | collective-permute-start | bytes 589832 | tf_op jit(solution)/shard_map/ppermute | solution.py:379
  31.2 1.6 %collective-permute-done.1.p2 = bf16[8,24,512]{2,1,0:T(8,128)(2,1)S(1)} collective-permute-done((bf16[8,24,512]{2,1,0:T(8,128)(2,1)S(1)}, bf16[8,24,512]{2,1,0:T(8,128)(2,1)S(1)}, u32[]{:S(2)}, u32[]{:S(2)}) %collective-permute-start.1) | collective-permute-done | bytes 196640 | tf_op jit(solution)/shard_map/ppermute | solution.py:379
  32.8 2.1 %collective-permute-done.p1 = bf16[8,24,512]{2,1,0:T(8,128)(2,1)S(1)} collective-permute-done((bf16[8,24,512]{2,1,0:T(8,128)(2,1)S(1)}, bf16[8,24,512]{2,1,0:T(8,128)(2,1)S(1)}, u32[]{:S(2)}, u32[]{:S(2)}) %collective-permute-start) | collective-permute-done | bytes 196640 | tf_op jit(solution)/shard_map/ppermute | solution.py:379
  36.2 25.0 %pack.1 = (bf16[32,24,256]{2,1,0:T(8,128)(2,1)}, bf16[32,24,256]{2,1,0:T(8,128)(2,1)}) custom-call(bf16[8,24,512]{2,1,0:T(8,128)(2,1)} %copy-done.9, bf16[8,24,512]{2,1,0:T(8,128)(2,1)} %copy-done.15, bf16[8,24,512]{2,1,0:T(8,128)(2,1)} %copy-done.14, bf16[8,24,512]{2,1,0:T(8,128)(2,1)} %copy-done.13, bf16[4,256,1024]{2,1,0:T(8,128)(2,1)} %collective-permute-done.3.k.k1, ...), custom_call_target="tpu_custom_call" | custom-call | tf_op jit(solution)/shard_map/pack/pallas_call | solution.py:251
  61.2 2.5 %collective-permute-start.7 = (bf16[32,24,256]{2,1,0:T(8,128)(2,1)}, bf16[32,24,256]{2,1,0:T(8,128)(2,1)S(1)}, u32[]{:S(2)}, u32[]{:S(2)}) collective-permute-start(bf16[32,24,256]{2,1,0:T(8,128)(2,1)} %get-tuple-element.19.q.q0), channel_id=1, source_target_pairs={{0,3},{1,0},{2,1},{3,2},{4,7},{5,4},{6,5},{7,6},{8,11},{9,8},{10,9... | collective-permute-start | bytes 1179656 | tf_op jit(solution)/shard_map/ppermute | solution.py:379
  65.2 2.0 %collective-permute-start.13 = (bf16[32,24,256]{2,1,0:T(8,128)(2,1)}, bf16[32,24,256]{2,1,0:T(8,128)(2,1)S(1)}, u32[]{:S(2)}, u32[]{:S(2)}) collective-permute-start(bf16[32,24,256]{2,1,0:T(8,128)(2,1)} %get-tuple-element.24.q0), channel_id=1, source_target_pairs={{0,3},{1,0},{2,1},{3,2},{4,7},{5,4},{6,5},{7,6},{8,11},{9,8},{10,9... | collective-permute-start | bytes 1179656 | tf_op jit(solution)/shard_map/ppermute | solution.py:379
  68.7 1.6 %copy-done.1 = bf16[4,256,1024]{2,1,0:T(8,128)(2,1)S(1)} copy-done((bf16[4,256,1024]{2,1,0:T(8,128)(2,1)S(1)}, bf16[4,256,1024]{2,1,0:T(8,128)(2,1)}, u32[]{:S(2)}) %copy-start.1) | copy-done | bytes 2097176
  72.8 2.0 %turn.1.v0 = bf16[8,512,256]{2,1,0:T(8,128)(2,1)S(1)} custom-call(s32[4]{0:T(128)S(1)} %pad_add_fusion.me, bf16[4,256,1024]{2,1,0:T(8,128)(2,1)S(1)} %copy-done.2, bf16[4,256,1024]{2,1,0:T(8,128)(2,1)S(1)} %copy-done.1, bf16[32,24,256]{2,1,0:T(8,128)(2,1)S(1)} %copy-done.3), custom_call_target="tpu_custom_call" | custom-call | flops 1000000 | bytes 8388608 | tf_op jit(solution)/shard_map/turn/pallas_call | solution.py:222
  74.9 1.7 %collective-permute-done.5.q1 = bf16[32,24,256]{2,1,0:T(8,128)(2,1)S(1)} collective-permute-done((bf16[32,24,256]{2,1,0:T(8,128)(2,1)}, bf16[32,24,256]{2,1,0:T(8,128)(2,1)S(1)}, u32[]{:S(2)}, u32[]{:S(2)}) %collective-permute-start.5) | collective-permute-done | bytes 393248 | tf_op jit(solution)/shard_map/ppermute | solution.py:379
  76.6 13.8 %attend.2 = (bf16[16,56,256]{2,1,0:T(8,128)(2,1)S(1)}, bf16[16,56,256]{2,1,0:T(8,128)(2,1)S(1)}, bf16[16,56,256]{2,1,0:T(8,128)(2,1)S(1)}, bf16[16,56,256]{2,1,0:T(8,128)(2,1)S(1)}) custom-call(s32[4]{0:T(128)S(1)} %pad_add_fusion.me, s32[12]{0:T(128)S(1)} %get-tuple-element.34.cnt, s32[96]{0:T(128)S(1)} %reshape.37.lst, bf16[32,24,256]{2,1,0:T(8,128)(2,1)S(1)} %copy-done.4, ...), custom_call_target="tpu_custom_call" | custom-call | flops 10000000000 | bytes 8388608 | tf_op jit(solution)/shard_map/attend/pallas_call | solution.py:173
  92.0 13.9 %attend.3 = (bf16[16,56,256]{2,1,0:T(8,128)(2,1)S(1)}, bf16[16,56,256]{2,1,0:T(8,128)(2,1)S(1)}, bf16[16,56,256]{2,1,0:T(8,128)(2,1)S(1)}, bf16[16,56,256]{2,1,0:T(8,128)(2,1)S(1)}) custom-call(s32[4]{0:T(128)S(1)} %pad_add_fusion.me, s32[12]{0:T(128)S(1)} %get-tuple-element.34.cnt, s32[96]{0:T(128)S(1)} %reshape.37.lst, bf16[32,24,256]{2,1,0:T(8,128)(2,1)S(1)} %copy-done.8, ...), custom_call_target="tpu_custom_call" | custom-call | flops 10000000000 | bytes 8388608 | tf_op jit(solution)/shard_map/attend/pallas_call | solution.py:173
  106.5 2.4 %collective-permute-start.15 = (bf16[16,56,256]{2,1,0:T(8,128)(2,1)S(1)}, bf16[16,56,256]{2,1,0:T(8,128)(2,1)S(1)}, u32[]{:S(2)}, u32[]{:S(2)}) collective-permute-start(bf16[16,56,256]{2,1,0:T(8,128)(2,1)S(1)} %get-tuple-element.27), channel_id=1, source_target_pairs={{0,2},{1,3},{2,0},{3,1},{4,6},{5,7},{6,4},{7,5},{8,10},{9,11},{10,... | collective-permute-start | bytes 1376264 | tf_op jit(solution)/shard_map/ppermute | solution.py:379
  109.7 3.9 %collective-permute-done.14.refs_5_ = bf16[16,56,256]{2,1,0:T(8,128)(2,1)S(1)} collective-permute-done((bf16[16,56,256]{2,1,0:T(8,128)(2,1)S(1)}, bf16[16,56,256]{2,1,0:T(8,128)(2,1)S(1)}, u32[]{:S(2)}, u32[]{:S(2)}) %collective-permute-start.14) | collective-permute-done | bytes 458784 | tf_op jit(solution)/shard_map/ppermute | solution.py:379
  113.6 2.1 %collective-permute-done.15.refs_6_ = bf16[16,56,256]{2,1,0:T(8,128)(2,1)S(1)} collective-permute-done((bf16[16,56,256]{2,1,0:T(8,128)(2,1)S(1)}, bf16[16,56,256]{2,1,0:T(8,128)(2,1)S(1)}, u32[]{:S(2)}, u32[]{:S(2)}) %collective-permute-start.15) | collective-permute-done | bytes 458784 | tf_op jit(solution)/shard_map/ppermute | solution.py:379
  115.7 4.9 %collective-permute-done.16.refs_7_ = bf16[16,56,256]{2,1,0:T(8,128)(2,1)S(1)} collective-permute-done((bf16[16,56,256]{2,1,0:T(8,128)(2,1)S(1)}, bf16[16,56,256]{2,1,0:T(8,128)(2,1)S(1)}, u32[]{:S(2)}, u32[]{:S(2)}) %collective-permute-start.16) | collective-permute-done | bytes 458784 | tf_op jit(solution)/shard_map/ppermute | solution.py:379
  120.5 2.2 %merge.1 = (bf16[8,56,256]{2,1,0:T(8,128)(2,1)S(1)}, bf16[8,56,256]{2,1,0:T(8,128)(2,1)S(1)}, bf16[8,56,256]{2,1,0:T(8,128)(2,1)S(1)}, bf16[8,56,256]{2,1,0:T(8,128)(2,1)S(1)}) custom-call(bf16[16,56,256]{2,1,0:T(8,128)(2,1)S(1)} %get-tuple-element.20.refs_0_, bf16[16,56,256]{2,1,0:T(8,128)(2,1)S(1)} %collective-permute-done.8.refs_1_, ...), custom_call_target="tpu_custom_call" | custom-call | tf_op jit(solution)/shard_map/merge/pallas_call | solution.py:307
  124.9 3.4 %collective-permute-done.17.p1 = bf16[8,56,256]{2,1,0:T(8,128)(2,1)S(1)} collective-permute-done((bf16[8,56,256]{2,1,0:T(8,128)(2,1)S(1)}, bf16[8,56,256]{2,1,0:T(8,128)(2,1)S(1)}, u32[]{:S(2)}, u32[]{:S(2)}) %collective-permute-start.17) | collective-permute-done | bytes 229408 | tf_op jit(solution)/shard_map/ppermute | solution.py:379
  128.3 1.6 %collective-permute-done.18.p2 = bf16[8,56,256]{2,1,0:T(8,128)(2,1)S(1)} collective-permute-done((bf16[8,56,256]{2,1,0:T(8,128)(2,1)S(1)}, bf16[8,56,256]{2,1,0:T(8,128)(2,1)S(1)}, u32[]{:S(2)}, u32[]{:S(2)}) %collective-permute-start.18) | collective-permute-done | bytes 229408 | tf_op jit(solution)/shard_map/ppermute | solution.py:379
  130.0 2.6 %collective-permute-done.19.p3 = bf16[8,56,256]{2,1,0:T(8,128)(2,1)S(1)} collective-permute-done((bf16[8,56,256]{2,1,0:T(8,128)(2,1)S(1)}, bf16[8,56,256]{2,1,0:T(8,128)(2,1)S(1)}, u32[]{:S(2)}, u32[]{:S(2)}) %collective-permute-start.19) | collective-permute-done | bytes 229408 | tf_op jit(solution)/shard_map/ppermute | solution.py:379
  133.3 2.4 %split.1 = bf16[8,2,32,256]{3,2,1,0:T(8,128)(2,1)} custom-call(bf16[8,56,256]{2,1,0:T(8,128)(2,1)} %copy-done.5, bf16[8,56,256]{2,1,0:T(8,128)(2,1)} %copy-done.10, bf16[8,56,256]{2,1,0:T(8,128)(2,1)} %copy-done.11, bf16[8,56,256]{2,1,0:T(8,128)(2,1)} %copy-done.12), custom_call_target="tpu_custom_call" | custom-call | tf_op jit(solution)/shard_map/split/pallas_call | solution.py:330
  135.7 19.4 %all_to_all.10.got = bf16[8,2,32,256]{3,2,1,0:T(8,128)(2,1)} all-to-all(bf16[8,2,32,256]{3,2,1,0:T(8,128)(2,1)} %split.1), channel_id=1, replica_groups=mesh['y'=4,'core'=2,'z'=4,'x'=4] {'core','z'}, dimensions={0} | all-to-all | bytes 524288 | tf_op jit(solution)/shard_map/all_to_all | solution.py:419
  155.1 3.3 %close.1 = bf16[24,1024]{1,0:T(8,128)(2,1)} custom-call(s32[4]{0:T(128)} %copy-done.6, bf16[8,2,32,256]{3,2,1,0:T(8,128)(2,1)} %all_to_all.10.got, bf16[1024,1024]{1,0:T(8,128)(2,1)} %weight.1), custom_call_target="tpu_custom_call" | custom-call | tf_op jit(solution)/shard_map/close/pallas_call | solution.py:359
  (80 shorter events, 30.4 us)
Async XLA Ops:
  0.0 34.9 %collective-permute-start.4 = (bf16[4,256,1024]{2,1,0:T(8,128)(2,1)}, bf16[4,256,1024]{2,1,0:T(8,128)(2,1)S(1)}, u32[]{:S(2)}, u32[]{:S(2)}) collective-permute-start(bf16[4,256,1024]{2,1,0:T(8,128)(2,1)} %v0.1), channel_id=1, source_target_pairs={{0,16},{16,0},{1,17},{17,1},{2,18},{18,2},{3,19},{19,3},{4,20},{20... | collective-permute-start | bytes 6291464 | tf_op jit(solution)/shard_map/ppermute | solution.py:370
  1.4 33.4 %collective-permute-start.3 = (bf16[4,256,1024]{2,1,0:T(8,128)(2,1)}, bf16[4,256,1024]{2,1,0:T(8,128)(2,1)}, u32[]{:S(2)}, u32[]{:S(2)}) collective-permute-start(bf16[4,256,1024]{2,1,0:T(8,128)(2,1)} %k0.3), channel_id=1, source_target_pairs={{0,16},{16,0},{1,17},{17,1},{2,18},{18,2},{3,19},{19,3},{4,20},{20... | collective-permute-start | bytes 6291464 | tf_op jit(solution)/shard_map/ppermute | solution.py:370
  12.2 11.8 %all-to-all-start = ((bf16[8,24,512]{2,1,0:T(8,128)(2,1)}), bf16[8,24,512]{2,1,0:T(8,128)(2,1)S(1)}, u32[]{:S(2)}, u32[]{:S(2)}) async-start(bf16[8,24,512]{2,1,0:T(8,128)(2,1)} %bitcast_dynamic-update-slice_fusion.3), calls=%async_computation | async-start | bytes 393216 | tf_op jit(solution)/shard_map/all_to_all | solution.py:395
  24.0 10.9 %copy-start.9 = (bf16[8,24,512]{2,1,0:T(8,128)(2,1)}, bf16[8,24,512]{2,1,0:T(8,128)(2,1)S(1)}, u32[]{:S(2)}) copy-start(bf16[8,24,512]{2,1,0:T(8,128)(2,1)S(1)} %all-to-all-done.p0) | copy-start | bytes 589828
  24.0 7.2 %collective-permute-start.2 = (bf16[8,24,512]{2,1,0:T(8,128)(2,1)S(1)}, bf16[8,24,512]{2,1,0:T(8,128)(2,1)S(1)}, u32[]{:S(2)}, u32[]{:S(2)}) collective-permute-start(bf16[8,24,512]{2,1,0:T(8,128)(2,1)S(1)} %all-to-all-done.p0), channel_id=1, source_target_pairs={{0,96},{1,97},{2,98},{3,99},{4,100},{5,101},{6,102},{7,103},{8,104... | collective-permute-start | bytes 589832 | tf_op jit(solution)/shard_map/ppermute | solution.py:379
  26.4 6.4 %collective-permute-start.1 = (bf16[8,24,512]{2,1,0:T(8,128)(2,1)S(1)}, bf16[8,24,512]{2,1,0:T(8,128)(2,1)S(1)}, u32[]{:S(2)}, u32[]{:S(2)}) collective-permute-start(bf16[8,24,512]{2,1,0:T(8,128)(2,1)S(1)} %all-to-all-done.p0), channel_id=1, source_target_pairs={{0,64},{1,65},{2,66},{3,67},{4,68},{5,69},{6,70},{7,71},{8,72},{9,... | collective-permute-start | bytes 589832 | tf_op jit(solution)/shard_map/ppermute | solution.py:379
  27.0 7.9 %collective-permute-start = (bf16[8,24,512]{2,1,0:T(8,128)(2,1)S(1)}, bf16[8,24,512]{2,1,0:T(8,128)(2,1)S(1)}, u32[]{:S(2)}, u32[]{:S(2)}) collective-permute-start(bf16[8,24,512]{2,1,0:T(8,128)(2,1)S(1)} %all-to-all-done.p0), channel_id=1, source_target_pairs={{0,32},{1,33},{2,34},{3,35},{4,36},{5,37},{6,38},{7,39},{8,40},{9,... | collective-permute-start | bytes 589832 | tf_op jit(solution)/shard_map/ppermute | solution.py:379
  61.2 13.6 %collective-permute-start.7 = (bf16[32,24,256]{2,1,0:T(8,128)(2,1)}, bf16[32,24,256]{2,1,0:T(8,128)(2,1)S(1)}, u32[]{:S(2)}, u32[]{:S(2)}) collective-permute-start(bf16[32,24,256]{2,1,0:T(8,128)(2,1)} %get-tuple-element.19.q.q0), channel_id=1, source_target_pairs={{0,3},{1,0},{2,1},{3,2},{4,7},{5,4},{6,5},{7,6},{8,11},{9,8},{10,9... | collective-permute-start | bytes 1179656 | tf_op jit(solution)/shard_map/ppermute | solution.py:379
  63.7 11.2 %collective-permute-start.6 = (bf16[32,24,256]{2,1,0:T(8,128)(2,1)}, bf16[32,24,256]{2,1,0:T(8,128)(2,1)S(1)}, u32[]{:S(2)}, u32[]{:S(2)}) collective-permute-start(bf16[32,24,256]{2,1,0:T(8,128)(2,1)} %get-tuple-element.19.q.q0), channel_id=1, source_target_pairs={{0,2},{1,3},{2,0},{3,1},{4,6},{5,7},{6,4},{7,5},{8,10},{9,11},{10,... | collective-permute-start | bytes 1179656 | tf_op jit(solution)/shard_map/ppermute | solution.py:379
  64.1 12.5 %collective-permute-start.5 = (bf16[32,24,256]{2,1,0:T(8,128)(2,1)}, bf16[32,24,256]{2,1,0:T(8,128)(2,1)S(1)}, u32[]{:S(2)}, u32[]{:S(2)}) collective-permute-start(bf16[32,24,256]{2,1,0:T(8,128)(2,1)} %get-tuple-element.19.q.q0), channel_id=1, source_target_pairs={{0,1},{1,2},{2,3},{3,0},{4,5},{5,6},{6,7},{7,4},{8,9},{9,10},{10,1... | collective-permute-start | bytes 1179656 | tf_op jit(solution)/shard_map/ppermute | solution.py:379
  65.2 26.8 %copy-start.6 = (s32[4]{0:T(128)}, s32[4]{0:T(128)S(1)}, u32[]{:S(2)}) copy-start(s32[4]{0:T(128)S(1)} %pad_add_fusion.me) | copy-start | bytes 52
  65.2 25.6 %collective-permute-start.13 = (bf16[32,24,256]{2,1,0:T(8,128)(2,1)}, bf16[32,24,256]{2,1,0:T(8,128)(2,1)S(1)}, u32[]{:S(2)}, u32[]{:S(2)}) collective-permute-start(bf16[32,24,256]{2,1,0:T(8,128)(2,1)} %get-tuple-element.24.q0), channel_id=1, source_target_pairs={{0,3},{1,0},{2,1},{3,2},{4,7},{5,4},{6,5},{7,6},{8,11},{9,8},{10,9... | collective-permute-start | bytes 1179656 | tf_op jit(solution)/shard_map/ppermute | solution.py:379
  67.3 24.7 %collective-permute-start.12 = (bf16[32,24,256]{2,1,0:T(8,128)(2,1)}, bf16[32,24,256]{2,1,0:T(8,128)(2,1)S(1)}, u32[]{:S(2)}, u32[]{:S(2)}) collective-permute-start(bf16[32,24,256]{2,1,0:T(8,128)(2,1)} %get-tuple-element.24.q0), channel_id=1, source_target_pairs={{0,2},{1,3},{2,0},{3,1},{4,6},{5,7},{6,4},{7,5},{8,10},{9,11},{10,... | collective-permute-start | bytes 1179656 | tf_op jit(solution)/shard_map/ppermute | solution.py:379
  74.8 17.2 %collective-permute-start.11 = (bf16[32,24,256]{2,1,0:T(8,128)(2,1)S(1)}, bf16[32,24,256]{2,1,0:T(8,128)(2,1)S(1)}, u32[]{:S(2)}, u32[]{:S(2)}) collective-permute-start(bf16[32,24,256]{2,1,0:T(8,128)(2,1)S(1)} %copy-done.8), channel_id=1, source_target_pairs={{0,1},{1,2},{2,3},{3,0},{4,5},{5,6},{6,7},{7,4},{8,9},{9,10},{10,1... | collective-permute-start | bytes 1179656 | tf_op jit(solution)/shard_map/ppermute | solution.py:379
  90.4 18.4 %collective-permute-start.8 = (bf16[16,56,256]{2,1,0:T(8,128)(2,1)S(1)}, bf16[16,56,256]{2,1,0:T(8,128)(2,1)S(1)}, u32[]{:S(2)}, u32[]{:S(2)}) collective-permute-start(bf16[16,56,256]{2,1,0:T(8,128)(2,1)S(1)} %get-tuple-element.21), channel_id=1, source_target_pairs={{0,3},{1,0},{2,1},{3,2},{4,7},{5,4},{6,5},{7,6},{8,11},{9,8},{10,9... | collective-permute-start | bytes 1376264 | tf_op jit(solution)/shard_map/ppermute | solution.py:379
  90.5 19.1 %collective-permute-start.9 = (bf16[16,56,256]{2,1,0:T(8,128)(2,1)S(1)}, bf16[16,56,256]{2,1,0:T(8,128)(2,1)S(1)}, u32[]{:S(2)}, u32[]{:S(2)}) collective-permute-start(bf16[16,56,256]{2,1,0:T(8,128)(2,1)S(1)} %get-tuple-element.22), channel_id=1, source_target_pairs={{0,2},{1,3},{2,0},{3,1},{4,6},{5,7},{6,4},{7,5},{8,10},{9,11},{10,... | collective-permute-start | bytes 1376264 | tf_op jit(solution)/shard_map/ppermute | solution.py:379
  90.8 18.8 %collective-permute-start.10 = (bf16[16,56,256]{2,1,0:T(8,128)(2,1)S(1)}, bf16[16,56,256]{2,1,0:T(8,128)(2,1)S(1)}, u32[]{:S(2)}, u32[]{:S(2)}) collective-permute-start(bf16[16,56,256]{2,1,0:T(8,128)(2,1)S(1)} %get-tuple-element.23), channel_id=1, source_target_pairs={{0,1},{1,2},{2,3},{3,0},{4,5},{5,6},{6,7},{7,4},{8,9},{9,10},{10,1... | collective-permute-start | bytes 1376264 | tf_op jit(solution)/shard_map/ppermute | solution.py:379
  105.9 7.7 %collective-permute-start.14 = (bf16[16,56,256]{2,1,0:T(8,128)(2,1)S(1)}, bf16[16,56,256]{2,1,0:T(8,128)(2,1)S(1)}, u32[]{:S(2)}, u32[]{:S(2)}) collective-permute-start(bf16[16,56,256]{2,1,0:T(8,128)(2,1)S(1)} %get-tuple-element.26), channel_id=1, source_target_pairs={{0,3},{1,0},{2,1},{3,2},{4,7},{5,4},{6,5},{7,6},{8,11},{9,8},{10,9... | collective-permute-start | bytes 1376264 | tf_op jit(solution)/shard_map/ppermute | solution.py:379
  106.5 9.2 %collective-permute-start.15 = (bf16[16,56,256]{2,1,0:T(8,128)(2,1)S(1)}, bf16[16,56,256]{2,1,0:T(8,128)(2,1)S(1)}, u32[]{:S(2)}, u32[]{:S(2)}) collective-permute-start(bf16[16,56,256]{2,1,0:T(8,128)(2,1)S(1)} %get-tuple-element.27), channel_id=1, source_target_pairs={{0,2},{1,3},{2,0},{3,1},{4,6},{5,7},{6,4},{7,5},{8,10},{9,11},{10,... | collective-permute-start | bytes 1376264 | tf_op jit(solution)/shard_map/ppermute | solution.py:379
  108.9 11.7 %collective-permute-start.16 = (bf16[16,56,256]{2,1,0:T(8,128)(2,1)S(1)}, bf16[16,56,256]{2,1,0:T(8,128)(2,1)S(1)}, u32[]{:S(2)}, u32[]{:S(2)}) collective-permute-start(bf16[16,56,256]{2,1,0:T(8,128)(2,1)S(1)} %get-tuple-element.28), channel_id=1, source_target_pairs={{0,1},{1,2},{2,3},{3,0},{4,5},{5,6},{6,7},{7,4},{8,9},{9,10},{10,1... | collective-permute-start | bytes 1376264 | tf_op jit(solution)/shard_map/ppermute | solution.py:379
  123.5 4.9 %collective-permute-start.17 = (bf16[8,56,256]{2,1,0:T(8,128)(2,1)S(1)}, bf16[8,56,256]{2,1,0:T(8,128)(2,1)S(1)}, u32[]{:S(2)}, u32[]{:S(2)}) collective-permute-start(bf16[8,56,256]{2,1,0:T(8,128)(2,1)S(1)} %get-tuple-element.30), channel_id=1, source_target_pairs={{0,96},{1,97},{2,98},{3,99},{4,100},{5,101},{6,102},{7,103},{8,104... | collective-permute-start | bytes 688136 | tf_op jit(solution)/shard_map/ppermute | solution.py:379
  123.5 6.5 %collective-permute-start.18 = (bf16[8,56,256]{2,1,0:T(8,128)(2,1)S(1)}, bf16[8,56,256]{2,1,0:T(8,128)(2,1)S(1)}, u32[]{:S(2)}, u32[]{:S(2)}) collective-permute-start(bf16[8,56,256]{2,1,0:T(8,128)(2,1)S(1)} %get-tuple-element.31), channel_id=1, source_target_pairs={{0,64},{1,65},{2,66},{3,67},{4,68},{5,69},{6,70},{7,71},{8,72},{9,... | collective-permute-start | bytes 688136 | tf_op jit(solution)/shard_map/ppermute | solution.py:379
  123.5 9.1 %collective-permute-start.19 = (bf16[8,56,256]{2,1,0:T(8,128)(2,1)S(1)}, bf16[8,56,256]{2,1,0:T(8,128)(2,1)S(1)}, u32[]{:S(2)}, u32[]{:S(2)}) collective-permute-start(bf16[8,56,256]{2,1,0:T(8,128)(2,1)S(1)} %get-tuple-element.32), channel_id=1, source_target_pairs={{0,32},{1,33},{2,34},{3,35},{4,36},{5,37},{6,38},{7,39},{8,40},{9,... | collective-permute-start | bytes 688136 | tf_op jit(solution)/shard_map/ppermute | solution.py:379
  128.3 4.3 %copy-start.10 = (bf16[8,56,256]{2,1,0:T(8,128)(2,1)}, bf16[8,56,256]{2,1,0:T(8,128)(2,1)S(1)}, u32[]{:S(2)}) copy-start(bf16[8,56,256]{2,1,0:T(8,128)(2,1)S(1)} %collective-permute-done.17.p1) | copy-start | bytes 688132
  (13 other events, 25.5 us)

commit v4 on v2

--- a/solution.py
+++ b/solution.py
@@ -20,15 +20,17 @@
 
 
 def attend_kernel(
-    me, cnt, lst, q0, q1, q2, q3, k0, k1, v0, o0, o1, o2, o3,
-    pq, pj, ps, qv, k, vt, qm, acc, sb, top, shrink, yb, sem, *, part,
+    me, cnt, lst, *refs, part,
 ):
+    n_out = 4 if part == 0 else 1
+    qs, (k0, k1, v0), outs = refs[:4], refs[4:7], refs[7:7 + n_out]
+    pq, pj, ps, qv, k, vt, qm, acc, sb, top, shrink, yb, sem = refs[7 + n_out:]
     my_y, my_core, my_z, my_x = me[0], me[1], me[2], me[3]
     col = pl.multiple_of(my_core * 512 + part * WIDE, WIDE)
     copies = [
         pltpu.make_async_copy(src, dst, sem.at[i])
         for i, (src, dst) in enumerate(
-            [(q, qv.at[r3]) for r3, q in enumerate((q0, q1, q2, q3))]
+            [(q, qv.at[pl.ds(i * q.shape[0], q.shape[0])]) for i, q in enumerate(qs)]
             + [
                 (k0.at[:, :, pl.ds(col, WIDE)], k.at[pl.ds(0, 4)]),
                 (k1.at[:, :, pl.ds(col, WIDE)], k.at[pl.ds(4, 4)]),
@@ -65,18 +67,17 @@
         z = lax.rem(my_z + 4 - rz, 4)
         return [pl.multiple_of(y * 768 + (c * 16 + z * 4 + x) * 24, 8) for c in range(2)]
 
-    for r3 in range(4):
-        copies[r3].wait()
-
-        def load(r2, _, r3=r3):
-            for rz in range(4):
-                block = qv[r3, r2 * 4 + rz].astype(F32)
-                for c, row in enumerate(place(r2, r3, rz)):
-                    yb[pl.ds(row, 24), :WIDE] = block[c * 24:(c + 1) * 24]
-            return 0
-
-        for r2 in range(4):
-            load(r2, 0)
+    def rows_of(y, z, x):
+        return [pl.multiple_of(y * 768 + (c * 16 + z * 4 + x) * 24, 8) for c in range(2)]
+
+    near = [[place(r2, r3, rz) for r2 in range(4) for rz in range(4)] for r3 in range(4)]
+    plain = [[rows_of(y, z, x) for y in range(4) for z in range(4) for x in range(4)]]
+    for i, spot in enumerate(near):
+        copies[i].wait()
+        for b, rows in enumerate(spot):
+            block = qv[i * len(spot) + b].astype(F32)
+            for c, row in enumerate(rows):
+                yb[pl.ds(row, 24), :WIDE] = block[c * 24:(c + 1) * 24]
 
     def turn(qi, _):
         rows = pl.ds(pl.multiple_of(qi * 256, 256), 256)
@@ -158,40 +159,35 @@
 
     lax.fori_loop(0, (total + 1) // 2, two, 0)
 
-    for r3, o in enumerate((o0, o1, o2, o3)):
-
-        def emit(r2, _, o=o, r3=r3):
-            for rz in range(4):
-                data, tail = [], jnp.zeros((8, 128), F32)
-                for c, row in enumerate(place(r2, r3, rz)):
-                    block = yb[pl.ds(row, 24), :]
-                    data.append(block[:, :WIDE])
-                    for p in range(3):
-                        piece = block[p * 8:(p + 1) * 8, WIDE:]
-                        g = c * 3 + p
-                        tail = tail + (pltpu.roll(piece, 16 * g, 1) if g else piece)
-                data.append(jnp.concatenate([tail, jnp.zeros((8, WIDE - 128), F32)], axis=1))
-                o[r2 * 4 + rz] = jnp.concatenate(data, axis=0).astype(BF16)
-            return 0
-
-        for r2 in range(4):
-            emit(r2, 0)
+    for o, spot in zip(outs, near if part == 0 else plain):
+        for b, rows in enumerate(spot):
+            data, tail = [], jnp.zeros((8, 128), F32)
+            for c, row in enumerate(rows):
+                block = yb[pl.ds(row, 24), :]
+                data.append(block[:, :WIDE])
+                for p in range(3):
+                    piece = block[p * 8:(p + 1) * 8, WIDE:]
+                    g = c * 3 + p
+                    tail = tail + (pltpu.roll(piece, 16 * g, 1) if g else piece)
+            data.append(jnp.concatenate([tail, jnp.zeros((8, WIDE - 128), F32)], axis=1))
+            o[b] = jnp.concatenate(data, axis=0).astype(BF16)
 
 
 def attend(me, cnt, lst, q, k0, k1, v0, part):
+    n_out = 4 if part == 0 else 1
     vmem = pl.BlockSpec(memory_space=pltpu.VMEM)
     smem = pl.BlockSpec(memory_space=pltpu.SMEM)
     whole = pl.BlockSpec(memory_space=pl.ANY)
     return pl.pallas_call(
         functools.partial(attend_kernel, part=part),
-        out_shape=[jax.ShapeDtypeStruct((16, 56, WIDE), BF16)] * 4,
+        out_shape=[jax.ShapeDtypeStruct((64 // n_out, 56, WIDE), BF16)] * n_out,
         in_specs=[smem] * 3 + [whole] * 7,
-        out_specs=[vmem] * 4,
+        out_specs=[vmem] * n_out,
         scratch_shapes=[
             pltpu.SMEM((104,), jnp.int32),
             pltpu.SMEM((104,), jnp.int32),
             pltpu.SMEM((104,), jnp.int32),
-            pltpu.VMEM((4, 16, 48, WIDE), BF16),
+            pltpu.VMEM((64, 48, WIDE), BF16),
             pltpu.VMEM((8, 256, WIDE), BF16),
             pltpu.VMEM((8, WIDE, 256), BF16),
             pltpu.VMEM((13, NH, 128, 256), BF16),
@@ -261,19 +257,20 @@
     )(*parts, k, v)
 
 
-def add_up(parts, spread):
-    tails = [p[48:56, :128].astype(F32) for p in parts]
+def add_up(data, tails, spread):
+    n = len(data)
     best = functools.reduce(jnp.maximum, tails)
     shares = [jnp.exp2(jnp.minimum(t - best, 0.0)) for t in tails]
     total = sum(f * (pltpu.roll(t, 128 - NH, 1) + pltpu.roll(t, 128 - 2 * NH, 1)) for f, t in zip(shares, tails))
     stack = jnp.concatenate(shares, axis=0)
-    stack = jnp.concatenate([stack] + [pltpu.roll(stack, 128 - 16 * g, 1) for g in range(1, 6)], axis=0)
+    groups = data[0].shape[0] // 8
+    stack = jnp.concatenate([stack] + [pltpu.roll(stack, 128 - 16 * g, 1) for g in range(1, groups)], axis=0)
     wide = jnp.dot(stack.astype(BF16), spread, preferred_element_type=F32)
     numer = []
-    for g in range(6):
-        at = g * 8 * len(parts)
+    for g in range(groups):
+        at = g * 8 * n
         numer.append(
-            sum(wide[at + s * 8:at + s * 8 + 8] * p[g * 8:g * 8 + 8, :].astype(F32) for s, p in enumerate(parts))
+            sum(wide[at + s * 8:at + s * 8 + 8] * d[g * 8:g * 8 + 8, :].astype(F32) for s, d in enumerate(data))
         )
     return numer, best, total
 
@@ -284,68 +281,114 @@
     return src == dst
 
 
-def merge_kernel(*refs, joint, blocks):
-    parts, outs = refs[:-4], refs[-4:]
+def add_blocks(held, spread, is_top):
+    data, tails = [p[:48] for p in held], [p[48:56, :128].astype(F32) for p in held]
+    numer, best, total = add_up(data, tails, spread)
+    total = jnp.where(is_top, total, 0.0)
+    hi = total.astype(BF16).astype(F32)
+    tail = jnp.where(is_top, best, 0.0) + pltpu.roll(hi, NH, 1) + pltpu.roll(total - hi, 2 * NH, 1)
+    return numer, jnp.concatenate([tail, jnp.zeros((8, WIDE - 128), F32)], axis=1)
+
+
+def merge_kernel(p0, p1, p2, p3, after, *outs):
     spread = make_spread().astype(BF16)
     is_top = lax.broadcasted_iota(jnp.int32, (8, 128), 1) % 16 < NH
+    blocks = outs[0].shape[0]
     for r, out in enumerate(outs):
-
-        def one(b, _, r=r, out=out):
-            for c in range(2):
-                if joint:
-                    held = [p[(r * blocks + b) * 2 + c] for p in parts]
-                else:
-                    held = [p[r * blocks + b] for p in parts[c * 4:c * 4 + 4]]
-                numer, best, total = add_up(held, spread)
-                total = jnp.where(is_top, total, 0.0)
-                hi = total.astype(BF16).astype(F32)
-                tail = jnp.where(is_top, best, 0.0) + pltpu.roll(hi, NH, 1) + pltpu.roll(total - hi, 2 * NH, 1)
-                tail = jnp.concatenate([tail, jnp.zeros((8, WIDE - 128), F32)], axis=1)
-                out[b * 2 + c] = jnp.concatenate(numer + [tail], axis=0).astype(BF16)
-            return 0
-
         for b in range(blocks):
-            one(b, 0)
-
-
-def merge(parts, blocks):
-    vmem = pl.BlockSpec(memory_space=pltpu.VMEM)
-    return pl.pallas_call(
-        functools.partial(merge_kernel, joint=len(parts) == 4, blocks=blocks),
-        out_shape=[jax.ShapeDtypeStruct((blocks * 2, 56, WIDE), BF16)] * 4,
-        in_specs=[vmem] * len(parts),
+            numer, tail = add_blocks([p[r * blocks + b] for p in (p0, p1, p2, p3)], spread, is_top)
+            out[b] = jnp.concatenate(numer + [tail], axis=0).astype(BF16)
+
+
+def merge(parts, after):
+    vmem = pl.BlockSpec(memory_space=pltpu.VMEM)
+    blocks = parts[0].shape[0] // 4
+    return pl.pallas_call(
+        merge_kernel,
+        out_shape=[jax.ShapeDtypeStruct((blocks, 56, WIDE), BF16)] * 4,
+        in_specs=[vmem] * 4 + [pl.BlockSpec(memory_space=pl.ANY)],
         out_specs=[vmem] * 4,
-        compiler_params=pltpu.CompilerParams(vmem_limit_bytes=32 * 2**20),
+        compiler_params=pltpu.CompilerParams(vmem_limit_bytes=24 * 2**20),
         name="merge",
+    )(*parts, after)
+
+
+def share_out(numer, total, spread):
+    totals = jnp.concatenate([total] + [pltpu.roll(total, 128 - 16 * g, 1) for g in range(1, 6)], axis=0)
+    wide = jnp.dot(totals, spread.astype(F32), precision=lax.Precision.HIGHEST, preferred_element_type=F32)
+    return jnp.concatenate(numer, axis=0) / wide
+
+
+def ring_close_kernel(p0, p1, p2, p3, out):
+    spread = make_spread()
+    held = [p[0] for p in (p0, p1, p2, p3)]
+    numer, _, total = add_up([p[:48] for p in held], [p[48:56, :128].astype(F32) for p in held], spread.astype(BF16))
+    out[...] = share_out(numer, total, spread)
+
+
+def ring_close(parts):
+    vmem = pl.BlockSpec(memory_space=pltpu.VMEM)
+    return pl.pallas_call(
+        ring_close_kernel,
+        out_shape=jax.ShapeDtypeStruct((48, WIDE), F32),
+        in_specs=[vmem] * 4,
+        out_specs=vmem,
+        name="ring_close",
     )(*parts)
 
 
-def close_kernel(me, p0, p1, p2, p3, keep, give, both):
-    parts = (p0, p1, p2, p3)
+def close_kernel(me, ready, got, keep, give, both, shares):
     spread = make_spread()
-    for c in range(2):
-        numer, _, total = add_up([p[c] for p in parts], spread.astype(BF16))
-        totals = jnp.concatenate([total] + [pltpu.roll(total, 128 - 16 * g, 1) for g in range(1, 6)], axis=0)
-        wide = jnp.dot(
-            totals, spread.astype(F32), precision=lax.Precision.HIGHEST, preferred_element_type=F32
-        )
-        both[:, c * WIDE:(c + 1) * WIDE] = jnp.concatenate(numer, axis=0) / wide
+    narrow = spread.astype(BF16)
+
+    def find(i, best):
+        for u in range(16):
+            best = jnp.maximum(best, got[i * 16 + u, 48:56, :128].astype(F32))
+        return best
+
+    best = lax.fori_loop(0, 4, find, jnp.full((8, 128), NO_TOP, F32))
+
+    def weigh(i, total):
+        for u in range(16):
+            t = got[i * 16 + u, 48:56, :128].astype(F32)
+            f = jnp.exp2(jnp.minimum(t - best, 0.0))
+            shares[pl.ds(pl.multiple_of((i * 16 + u) * 8, 8), 8), :] = f
+            total = total + f * (pltpu.roll(t, 128 - NH, 1) + pltpu.roll(t, 128 - 2 * NH, 1))
+        return total
+
+    total = lax.fori_loop(0, 4, weigh, jnp.zeros((8, 128), F32))
+
+    def add(i, numer):
+        numer = list(numer)
+        f = shares[pl.ds(pl.multiple_of(i * 64, 64), 64), :]
+        f = jnp.concatenate([f] + [pltpu.roll(f, 128 - 16 * g, 1) for g in range(1, 6)], axis=0)
+        wide = jnp.dot(f.astype(BF16), narrow, preferred_element_type=F32)
+        for u in range(8):
+            for g in range(6):
+                at = g * 64 + u * 8
+                numer[g] = numer[g] + wide[at:at + 8] * got[i * 8 + u, g * 8:g * 8 + 8, :].astype(F32)
+        return tuple(numer)
+
+    numer = lax.fori_loop(0, 8, add, tuple(jnp.zeros((8, WIDE), F32) for _ in range(6)))
+    both[:, :WIDE] = ready[...]
+    both[:, WIDE:] = share_out(list(numer), total, spread)
     row = pl.multiple_of(me[1] * 24, 8)
     keep[...] = both[pl.ds(row, 24), :].astype(BF16)
     give[...] = both[pl.ds(24 - row, 24), :].astype(BF16)
 
 
-def close(me, parts):
+def close(me, ready, got):
     vmem = pl.BlockSpec(memory_space=pltpu.VMEM)
     smem = pl.BlockSpec(memory_space=pltpu.SMEM)
     return pl.pallas_call(
         close_kernel,
         out_shape=[jax.ShapeDtypeStruct((24, 512), BF16)] * 2,
-        in_specs=[smem] + [vmem] * 4,
+        in_specs=[smem, vmem, vmem],
         out_specs=[vmem] * 2,
-        scratch_shapes=[pltpu.VMEM((48, 512), F32)],
+        scratch_shapes=[pltpu.VMEM((48, 512), F32), pltpu.VMEM((512, 128), F32)],
+        compiler_params=pltpu.CompilerParams(vmem_limit_bytes=16 * 2**20),
         name="close",
-    )(me, *parts)
+    )(me, ready, got)
 
 
 def swap(x):
@@ -382,8 +425,8 @@
     pair = jnp.concatenate([jnp.where(first, mine, theirs), jnp.where(first, theirs, mine)], axis=0)
     along_z = jnp.concatenate(ring(pair[None], "zz"), axis=0)
     k_theirs, v_theirs = swap(keys), swap(values)
+    me = jnp.stack([lax.axis_index(a) for a in ALL]).astype(jnp.int32)
     planes = pack(ring(along_z, "yx"), k_theirs, v_theirs)
-    me = jnp.stack([lax.axis_index(a) for a in ALL]).astype(jnp.int32)
     v_turned = turn_values(me, values, v_theirs, planes[0])
     q_parts = [ring(plane, "xy") for plane in planes]
 
@@ -400,12 +443,12 @@
     lst = jnp.sum(jnp.where(hit, eight[None, None, :], 0), axis=2).reshape(96)
     cnt = jnp.sum(need_i, axis=1)
 
-    sent = []
-    for c in range(2):
-        sent += deliver(attend(me, cnt, lst, q_parts[c], keys, k_theirs, v_turned, c), "xy")
-    sent = deliver(merge(sent, 4), "yx")
-    sent = deliver(merge(sent, 1), "zz")
-    keep, give = close(me, sent)
+    sent = deliver(attend(me, cnt, lst, q_parts[0], keys, k_theirs, v_turned, 0), "xy")
+    late = attend(me, cnt, lst, q_parts[1], keys, k_theirs, v_turned, 1)[0]
+    got = lax.all_to_all(late, ("y", "z", "x"), 0, 0)
+    sent = deliver(merge(sent, late), "yx")
+    sent = deliver(merge(sent, late), "zz")
+    keep, give = close(me, ring_close(sent), got)
     give = swap(give)
     rows = jnp.concatenate([jnp.where(first, keep, give), jnp.where(first, give, keep)], axis=1)
     return jnp.dot(rows, out_weight, preferred_element_type=F32).astype(BF16)

time: 120 us -> 133 us (1.11); the launches traced: 119 us -> 134 us
  starting transfers between devices: 34.2 us -> 52 us
  waiting for transfers between devices: 38.8 us -> 31.8 us
  local copies, waits for them, and re-layouts: 5.6 us -> 11.3 us
    all_to_all x0 -> x1, starting transfers between devices: none -> 11.8 us  [body(): got = lax.all_to_all(late, ('y', 'z', 'x'), 0, 0)]
    ppermute x24 -> x21, waiting for transfers between devices: 36 us -> 29.2 us  [shift(): return lax.ppermute(x, ALL, pairs)]
    ppermute x24 -> x21, starting transfers between devices: 23.5 us -> 29.7 us  [shift(): return lax.ppermute(x, ALL, pairs)]
    unnamed x30 -> x36, local copies, waits for them, and re-layouts: 4.52 us -> 10.2 us
    pallas_call x2, Pallas kernels: 24.8 us -> 21.1 us  [attend(): pl.pallas_call(functools.partial(attend_kernel, part=part), out_shape=[ja...]
    pallas_call x1, Pallas kernels: 1.94 us -> 4.2 us  [close(): pl.pallas_call(close_kernel, out_shape=[jax.ShapeDtypeStruct((24, 512), B...]
    pallas_call x2 -> x3, Pallas kernels: 2.67 us -> 3.15 us  [the longest x1 1.77 us: ring_close(): pl.pallas_call(ring_close_kernel, out_shape=jax.ShapeDtypeStruct((48, WID...]
  transfers between devices with their start and end apart: 28 -> 26, of which waited for: 17 -> 15; matrix products, arithmetic and copies ran while one was open for 4% -> 4% of each run, Pallas kernels for 23% -> 20%
where the time goes in v4:
time: 133 us; the launch traced here: 134 us
  starting transfers between devices  52 us (39%)
  Pallas kernels  33.7 us (25%)
  waiting for transfers between devices  31.8 us (24%)
  local copies, waits for them, and re-layouts  11.3 us (8%)
  other arithmetic  3.91 us (3%)
    ppermute x21, starting transfers between devices, shift(): return lax.ppermute(x, ALL, pairs)  29.7 us
    ppermute x21, waiting for transfers between devices, shift(): return lax.ppermute(x, ALL, pairs)  29.2 us
    pallas_call x2, Pallas kernels, attend(): pl.pallas_call(functools.partial(attend_kernel, part=part), out_shape=[ja...  21.1 us
    all_to_all x1, starting transfers between devices, body(): got = lax.all_to_all(late, ('y', 'z', 'x'), 0, 0)  11.8 us
    ppermute x4, starting transfers between devices, swap(): return lax.ppermute(x, 'core', [(0, 1), (1, 0)])  10.5 us
    unnamed x36, local copies, waits for them, and re-layouts  10.2 us
    pallas_call x1, Pallas kernels, close(): pl.pallas_call(close_kernel, out_shape=[jax.ShapeDtypeStruct((24, 512), B...  4.2 us
    pallas_call x1, Pallas kernels, turn_values(): pl.pallas_call(turn_kernel, out_shape=jax.ShapeDtypeStruct((8, 512, 256),...  3.09 us
  transfers between devices with their start and end apart: 26, of which 15 were waited for; matrix products, arithmetic and copies ran while one was open for 4% of the time, Pallas kernels for 20%

profile of v4, /device:TPU:1, one launch (start us, length us, event | category | flops | bytes accessed | tf_op | source)
XLA Modules:
  0.0 134.0 jit_solution(12230907750245722256)
XLA Ops:
  3.5 1.8 %collective-permute-done = bf16[24,512]{1,0:T(8,128)(2,1)S(1)} collective-permute-done((bf16[24,512]{1,0:T(8,128)(2,1)S(1)}, bf16[24,512]{1,0:T(8,128)(2,1)S(1)}, u32[]{:S(2)}, u32[]{:S(2)}) %collective-permute-start) | collective-permute-done | bytes 24608 | tf_op jit(solution)/shard_map/ppermute | solution.py:395
  6.0 3.9 %collective-permute-start.3 = (bf16[1,48,512]{2,1,0:T(8,128)(2,1)S(1)}, bf16[1,48,512]{2,1,0:T(8,128)(2,1)S(1)}, u32[]{:S(2)}, u32[]{:S(2)}) collective-permute-start(bf16[1,48,512]{2,1,0:T(8,128)(2,1)S(1)} %maximum_bitcast_fusion), channel_id=1, source_target_pairs={{0,12},{1,13},{2,14},{3,15},{4,0},{5,1},{6,2},{7,3},{8,4},{9,5},{1... | collective-permute-start | bytes 147464 | tf_op jit(solution)/shard_map/ppermute | solution.py:404
  11.1 3.4 %collective-permute-done.2 = bf16[1,48,512]{2,1,0:T(8,128)(2,1)S(1)} collective-permute-done((bf16[1,48,512]{2,1,0:T(8,128)(2,1)S(1)}, bf16[1,48,512]{2,1,0:T(8,128)(2,1)S(1)}, u32[]{:S(2)}, u32[]{:S(2)}) %collective-permute-start.2) | collective-permute-done | bytes 49184 | tf_op jit(solution)/shard_map/ppermute | solution.py:404
  16.0 2.5 %collective-permute-start.5 = (bf16[4,48,512]{2,1,0:T(8,128)(2,1)S(1)}, bf16[4,48,512]{2,1,0:T(8,128)(2,1)S(1)}, u32[]{:S(2)}, u32[]{:S(2)}) collective-permute-start(bf16[4,48,512]{2,1,0:T(8,128)(2,1)S(1)} %pad_maximum_fusion.p0), channel_id=1, source_target_pairs={{0,64},{1,65},{2,66},{3,67},{4,68},{5,69},{6,70},{7,71},{8,72},{9,... | collective-permute-start | bytes 589832 | tf_op jit(solution)/shard_map/ppermute | solution.py:404
  21.8 1.8 %collective-permute-done.5.p2 = bf16[4,48,512]{2,1,0:T(8,128)(2,1)S(1)} collective-permute-done((bf16[4,48,512]{2,1,0:T(8,128)(2,1)S(1)}, bf16[4,48,512]{2,1,0:T(8,128)(2,1)S(1)}, u32[]{:S(2)}, u32[]{:S(2)}) %collective-permute-start.5) | collective-permute-done | bytes 196640 | tf_op jit(solution)/shard_map/ppermute | solution.py:404
  24.3 2.2 %pack.1 = (bf16[16,48,256]{2,1,0:T(8,128)(2,1)}, bf16[16,48,256]{2,1,0:T(8,128)(2,1)}) custom-call(bf16[4,48,512]{2,1,0:T(8,128)(2,1)} %copy-done.11, bf16[4,48,512]{2,1,0:T(8,128)(2,1)} %copy-done.12, bf16[4,48,512]{2,1,0:T(8,128)(2,1)} %copy-done.13, bf16[4,48,512]{2,1,0:T(8,128)(2,1)} %copy-done.14, ...), custom_call_target="tpu_custom_call" | custom-call | tf_op jit(solution)/shard_map/pack/pallas_call | solution.py:251
  27.8 2.6 %collective-permute-start.16 = (bf16[16,48,256]{2,1,0:T(8,128)(2,1)}, bf16[16,48,256]{2,1,0:T(8,128)(2,1)S(1)}, u32[]{:S(2)}, u32[]{:S(2)}) collective-permute-start(bf16[16,48,256]{2,1,0:T(8,128)(2,1)} %get-tuple-element.26.refs_0_), channel_id=1, source_target_pairs={{0,2},{1,3},{2,0},{3,1},{4,6},{5,7},{6,4},{7,5},{8,10},{9,11},{10,... | collective-permute-start | bytes 1179656 | tf_op jit(solution)/shard_map/ppermute | solution.py:404
  34.8 3.1 %turn.1.refs_6_ = bf16[8,512,256]{2,1,0:T(8,128)(2,1)S(1)} custom-call(s32[4]{0:T(128)S(1)} %pad_add_fusion.me, bf16[4,256,1024]{2,1,0:T(8,128)(2,1)S(1)} %copy-done.3, bf16[4,256,1024]{2,1,0:T(8,128)(2,1)} %collective-permute-done.8.v.v1, bf16[16,48,256]{2,1,0:T(8,128)(2,1)} %get-tuple-element.21.q.refs_0_), custom_call_target="tpu_custom_call" | custom-call | flops 1000000 | bytes 8388608 | tf_op jit(solution)/shard_map/turn/pallas_call | solution.py:230
  37.9 1.8 %collective-permute-start.11 = (bf16[16,48,256]{2,1,0:T(8,128)(2,1)}, bf16[16,48,256]{2,1,0:T(8,128)(2,1)}, u32[]{:S(2)}, u32[]{:S(2)}) collective-permute-start(bf16[16,48,256]{2,1,0:T(8,128)(2,1)} %get-tuple-element.21.q.refs_0_), channel_id=1, source_target_pairs={{0,3},{1,0},{2,1},{3,2},{4,7},{5,4},{6,5},{7,6},{8,11},{9,8},{10,9... | collective-permute-start | bytes 1179656 | tf_op jit(solution)/shard_map/ppermute | solution.py:404
  40.4 10.6 %attend.3.after = bf16[64,56,256]{2,1,0:T(8,128)(2,1)S(1)} custom-call(s32[4]{0:T(128)S(1)} %pad_add_fusion.me, s32[12]{0:T(128)S(1)} %get-tuple-element.42.cnt, s32[96]{0:T(128)S(1)} %reshape.37.lst, bf16[16,48,256]{2,1,0:T(8,128)(2,1)S(1)} %copy-done.10, bf16[16,48,256]{2,1,0:T(8,128)(2,1)S(1)} %collective-permute-done.15.refs_1_, ...), custom_call_target="tpu_custom_call" | custom-call | flops 10000000000 | bytes 8388608 | tf_op jit(solution)/shard_map/attend/pallas_call | solution.py:181
  53.6 11.8 %all-to-all-start = ((bf16[64,56,256]{2,1,0:T(8,128)(2,1)}), bf16[64,56,256]{2,1,0:T(8,128)(2,1)}, u32[]{:S(2)}, u32[]{:S(2)}) async-start(bf16[64,56,256]{2,1,0:T(8,128)(2,1)} %copy-done.1), calls=%async_computation | async-start | bytes 3670016 | tf_op jit(solution)/shard_map/all_to_all | solution.py:448
  65.5 1.7 %copy-done.5 = bf16[8,512,256]{2,1,0:T(8,128)(2,1)S(1)} copy-done((bf16[8,512,256]{2,1,0:T(8,128)(2,1)S(1)}, bf16[8,512,256]{2,1,0:T(8,128)(2,1)}, u32[]{:S(2)}) %copy-start.5) | copy-done | bytes 2097176
  67.2 1.6 %copy-done.9 = bf16[4,256,1024]{2,1,0:T(8,128)(2,1)S(1)} copy-done((bf16[4,256,1024]{2,1,0:T(8,128)(2,1)S(1)}, bf16[4,256,1024]{2,1,0:T(8,128)(2,1)}, u32[]{:S(2)}) %copy-start.9) | copy-done | bytes 2097176
  68.8 10.5 %attend.2 = (bf16[16,56,256]{2,1,0:T(8,128)(2,1)S(1)}, bf16[16,56,256]{2,1,0:T(8,128)(2,1)S(1)}, bf16[16,56,256]{2,1,0:T(8,128)(2,1)S(1)}, bf16[16,56,256]{2,1,0:T(8,128)(2,1)S(1)}) custom-call(s32[4]{0:T(128)S(1)} %pad_add_fusion.me, s32[12]{0:T(128)S(1)} %get-tuple-element.42.cnt, s32[96]{0:T(128)S(1)} %reshape.37.lst, ...), custom_call_target="tpu_custom_call" | custom-call | flops 10000000000 | bytes 8388608 | tf_op jit(solution)/shard_map/attend/pallas_call | solution.py:181
  79.9 4.8 %collective-permute-start.13 = (bf16[16,56,256]{2,1,0:T(8,128)(2,1)S(1)}, bf16[16,56,256]{2,1,0:T(8,128)(2,1)S(1)}, u32[]{:S(2)}, u32[]{:S(2)}) collective-permute-start(bf16[16,56,256]{2,1,0:T(8,128)(2,1)S(1)} %get-tuple-element.24), channel_id=1, source_target_pairs={{0,2},{1,3},{2,0},{3,1},{4,6},{5,7},{6,4},{7,5},{8,10},{9,11},{10,... | collective-permute-start | bytes 1376264 | tf_op jit(solution)/shard_map/ppermute | solution.py:404
  85.4 6.6 %collective-permute-done.12.p1 = bf16[16,56,256]{2,1,0:T(8,128)(2,1)S(1)} collective-permute-done((bf16[16,56,256]{2,1,0:T(8,128)(2,1)S(1)}, bf16[16,56,256]{2,1,0:T(8,128)(2,1)S(1)}, u32[]{:S(2)}, u32[]{:S(2)}) %collective-permute-start.12) | collective-permute-done | bytes 458784 | tf_op jit(solution)/shard_map/ppermute | solution.py:404
  92.0 3.0 %collective-permute-done.13.p2 = bf16[16,56,256]{2,1,0:T(8,128)(2,1)S(1)} collective-permute-done((bf16[16,56,256]{2,1,0:T(8,128)(2,1)S(1)}, bf16[16,56,256]{2,1,0:T(8,128)(2,1)S(1)}, u32[]{:S(2)}, u32[]{:S(2)}) %collective-permute-start.13) | collective-permute-done | bytes 458784 | tf_op jit(solution)/shard_map/ppermute | solution.py:404
  95.0 4.9 %collective-permute-done.14.p3 = bf16[16,56,256]{2,1,0:T(8,128)(2,1)S(1)} collective-permute-done((bf16[16,56,256]{2,1,0:T(8,128)(2,1)S(1)}, bf16[16,56,256]{2,1,0:T(8,128)(2,1)S(1)}, u32[]{:S(2)}, u32[]{:S(2)}) %collective-permute-start.14) | collective-permute-done | bytes 458784 | tf_op jit(solution)/shard_map/ppermute | solution.py:404
  104.7 2.5 %collective-permute-done.19.p2 = bf16[4,56,256]{2,1,0:T(8,128)(2,1)S(1)} collective-permute-done((bf16[4,56,256]{2,1,0:T(8,128)(2,1)S(1)}, bf16[4,56,256]{2,1,0:T(8,128)(2,1)S(1)}, u32[]{:S(2)}, u32[]{:S(2)}) %collective-permute-start.19) | collective-permute-done | bytes 114720 | tf_op jit(solution)/shard_map/ppermute | solution.py:404
  109.3 2.7 %collective-permute-start.21 = (bf16[1,56,256]{2,1,0:T(8,128)(2,1)S(1)}, bf16[1,56,256]{2,1,0:T(8,128)(2,1)S(1)}, u32[]{:S(2)}, u32[]{:S(2)}) collective-permute-start(bf16[1,56,256]{2,1,0:T(8,128)(2,1)S(1)} %get-tuple-element.32), channel_id=1, source_target_pairs={{0,12},{1,13},{2,14},{3,15},{4,0},{5,1},{6,2},{7,3},{8,4},{9,5},{1... | collective-permute-start | bytes 86024 | tf_op jit(solution)/shard_map/ppermute | solution.py:404
  113.0 3.3 %collective-permute-done.22.p2 = bf16[1,56,256]{2,1,0:T(8,128)(2,1)S(1)} collective-permute-done((bf16[1,56,256]{2,1,0:T(8,128)(2,1)S(1)}, bf16[1,56,256]{2,1,0:T(8,128)(2,1)S(1)}, u32[]{:S(2)}, u32[]{:S(2)}) %collective-permute-start.22) | collective-permute-done | bytes 28704 | tf_op jit(solution)/shard_map/ppermute | solution.py:404
  116.9 1.8 %ring_close.1.ready = f32[48,256]{1,0:T(8,128)} custom-call(bf16[1,56,256]{2,1,0:T(8,128)(2,1)} %copy-done.7, bf16[1,56,256]{2,1,0:T(8,128)(2,1)} %copy-done.15, bf16[1,56,256]{2,1,0:T(8,128)(2,1)} %copy-done.16, bf16[1,56,256]{2,1,0:T(8,128)(2,1)} %copy-done.17), custom_call_target="tpu_custom_call" | custom-call | tf_op jit(solution)/shard_map/ring_close/pallas_call | solution.py:331
  119.4 4.2 %close.1 = (bf16[24,512]{1,0:T(8,128)(2,1)S(1)}, bf16[24,512]{1,0:T(8,128)(2,1)S(1)}) custom-call(s32[4]{0:T(128)S(1)} %pad_add_fusion.me, f32[48,256]{1,0:T(8,128)S(1)} %copy-done.6, bf16[64,56,256]{2,1,0:T(8,128)(2,1)} %all-to-all-done.got), custom_call_target="tpu_custom_call" | custom-call | tf_op jit(solution)/shard_map/close/pallas_call | solution.py:383
  123.6 8.4 %collective-permute-start.24 = (bf16[24,512]{1,0:T(8,128)(2,1)S(1)}, bf16[24,512]{1,0:T(8,128)(2,1)S(1)}, u32[]{:S(2)}, u32[]{:S(2)}) collective-permute-start(bf16[24,512]{1,0:T(8,128)(2,1)S(1)} %get-tuple-element.36), channel_id=1, source_target_pairs={{0,16},{16,0},{1,17},{17,1},{2,18},{18,2},{3,19},{19,3},{4,20},{20... | collective-permute-start | bytes 73736 | tf_op jit(solution)/shard_map/ppermute | solution.py:395
  (92 shorter events, 32.4 us)
Async XLA Ops:
  0.0 23.6 %collective-permute-start.7 = (bf16[4,256,1024]{2,1,0:T(8,128)(2,1)}, bf16[4,256,1024]{2,1,0:T(8,128)(2,1)}, u32[]{:S(2)}, u32[]{:S(2)}) collective-permute-start(bf16[4,256,1024]{2,1,0:T(8,128)(2,1)} %refs_4_.3), channel_id=1, source_target_pairs={{0,16},{16,0},{1,17},{17,1},{2,18},{18,2},{3,19},{19,3},{4,20},{20... | collective-permute-start | bytes 6291464 | tf_op jit(solution)/shard_map/ppermute | solution.py:395
  1.4 22.2 %collective-permute-start.8 = (bf16[4,256,1024]{2,1,0:T(8,128)(2,1)}, bf16[4,256,1024]{2,1,0:T(8,128)(2,1)}, u32[]{:S(2)}, u32[]{:S(2)}) collective-permute-start(bf16[4,256,1024]{2,1,0:T(8,128)(2,1)} %v0.1), channel_id=1, source_target_pairs={{0,16},{16,0},{1,17},{17,1},{2,18},{18,2},{3,19},{19,3},{4,20},{20... | collective-permute-start | bytes 6291464 | tf_op jit(solution)/shard_map/ppermute | solution.py:395
  6.0 5.1 %collective-permute-start.3 = (bf16[1,48,512]{2,1,0:T(8,128)(2,1)S(1)}, bf16[1,48,512]{2,1,0:T(8,128)(2,1)S(1)}, u32[]{:S(2)}, u32[]{:S(2)}) collective-permute-start(bf16[1,48,512]{2,1,0:T(8,128)(2,1)S(1)} %maximum_bitcast_fusion), channel_id=1, source_target_pairs={{0,12},{1,13},{2,14},{3,15},{4,0},{5,1},{6,2},{7,3},{8,4},{9,5},{1... | collective-permute-start | bytes 147464 | tf_op jit(solution)/shard_map/ppermute | solution.py:404
  10.0 4.5 %collective-permute-start.2 = (bf16[1,48,512]{2,1,0:T(8,128)(2,1)S(1)}, bf16[1,48,512]{2,1,0:T(8,128)(2,1)S(1)}, u32[]{:S(2)}, u32[]{:S(2)}) collective-permute-start(bf16[1,48,512]{2,1,0:T(8,128)(2,1)S(1)} %maximum_bitcast_fusion), channel_id=1, source_target_pairs={{0,8},{1,9},{2,10},{3,11},{4,12},{5,13},{6,14},{7,15},{8,0},{9,1},... | collective-permute-start | bytes 147464 | tf_op jit(solution)/shard_map/ppermute | solution.py:404
  10.0 4.7 %collective-permute-start.1 = (bf16[1,48,512]{2,1,0:T(8,128)(2,1)S(1)}, bf16[1,48,512]{2,1,0:T(8,128)(2,1)S(1)}, u32[]{:S(2)}, u32[]{:S(2)}) collective-permute-start(bf16[1,48,512]{2,1,0:T(8,128)(2,1)S(1)} %maximum_bitcast_fusion), channel_id=1, source_target_pairs={{0,4},{1,5},{2,6},{3,7},{4,8},{5,9},{6,10},{7,11},{8,12},{9,13},{1... | collective-permute-start | bytes 147464 | tf_op jit(solution)/shard_map/ppermute | solution.py:404
  14.7 7.1 %collective-permute-start.4 = (bf16[4,48,512]{2,1,0:T(8,128)(2,1)S(1)}, bf16[4,48,512]{2,1,0:T(8,128)(2,1)S(1)}, u32[]{:S(2)}, u32[]{:S(2)}) collective-permute-start(bf16[4,48,512]{2,1,0:T(8,128)(2,1)S(1)} %pad_maximum_fusion.p0), channel_id=1, source_target_pairs={{0,32},{1,33},{2,34},{3,35},{4,36},{5,37},{6,38},{7,39},{8,40},{9,... | collective-permute-start | bytes 589832 | tf_op jit(solution)/shard_map/ppermute | solution.py:404
  16.0 7.6 %collective-permute-start.5 = (bf16[4,48,512]{2,1,0:T(8,128)(2,1)S(1)}, bf16[4,48,512]{2,1,0:T(8,128)(2,1)S(1)}, u32[]{:S(2)}, u32[]{:S(2)}) collective-permute-start(bf16[4,48,512]{2,1,0:T(8,128)(2,1)S(1)} %pad_maximum_fusion.p0), channel_id=1, source_target_pairs={{0,64},{1,65},{2,66},{3,67},{4,68},{5,69},{6,70},{7,71},{8,72},{9,... | collective-permute-start | bytes 589832 | tf_op jit(solution)/shard_map/ppermute | solution.py:404
  18.4 5.2 %collective-permute-start.6 = (bf16[4,48,512]{2,1,0:T(8,128)(2,1)S(1)}, bf16[4,48,512]{2,1,0:T(8,128)(2,1)S(1)}, u32[]{:S(2)}, u32[]{:S(2)}) collective-permute-start(bf16[4,48,512]{2,1,0:T(8,128)(2,1)S(1)} %pad_maximum_fusion.p0), channel_id=1, source_target_pairs={{0,96},{1,97},{2,98},{3,99},{4,100},{5,101},{6,102},{7,103},{8,104... | collective-permute-start | bytes 589832 | tf_op jit(solution)/shard_map/ppermute | solution.py:404
  26.5 11.4 %collective-permute-start.15 = (bf16[16,48,256]{2,1,0:T(8,128)(2,1)}, bf16[16,48,256]{2,1,0:T(8,128)(2,1)S(1)}, u32[]{:S(2)}, u32[]{:S(2)}) collective-permute-start(bf16[16,48,256]{2,1,0:T(8,128)(2,1)} %get-tuple-element.26.refs_0_), channel_id=1, source_target_pairs={{0,1},{1,2},{2,3},{3,0},{4,5},{5,6},{6,7},{7,4},{8,9},{9,10},{10,1... | collective-permute-start | bytes 1179656 | tf_op jit(solution)/shard_map/ppermute | solution.py:404
  27.8 12.5 %collective-permute-start.16 = (bf16[16,48,256]{2,1,0:T(8,128)(2,1)}, bf16[16,48,256]{2,1,0:T(8,128)(2,1)S(1)}, u32[]{:S(2)}, u32[]{:S(2)}) collective-permute-start(bf16[16,48,256]{2,1,0:T(8,128)(2,1)} %get-tuple-element.26.refs_0_), channel_id=1, source_target_pairs={{0,2},{1,3},{2,0},{3,1},{4,6},{5,7},{6,4},{7,5},{8,10},{9,11},{10,... | collective-permute-start | bytes 1179656 | tf_op jit(solution)/shard_map/ppermute | solution.py:404
  30.4 9.9 %collective-permute-start.17 = (bf16[16,48,256]{2,1,0:T(8,128)(2,1)}, bf16[16,48,256]{2,1,0:T(8,128)(2,1)S(1)}, u32[]{:S(2)}, u32[]{:S(2)}) collective-permute-start(bf16[16,48,256]{2,1,0:T(8,128)(2,1)} %get-tuple-element.26.refs_0_), channel_id=1, source_target_pairs={{0,3},{1,0},{2,1},{3,2},{4,7},{5,4},{6,5},{7,6},{8,11},{9,8},{10,9... | collective-permute-start | bytes 1179656 | tf_op jit(solution)/shard_map/ppermute | solution.py:404
  32.0 33.5 %collective-permute-start.9 = (bf16[16,48,256]{2,1,0:T(8,128)(2,1)}, bf16[16,48,256]{2,1,0:T(8,128)(2,1)}, u32[]{:S(2)}, u32[]{:S(2)}) collective-permute-start(bf16[16,48,256]{2,1,0:T(8,128)(2,1)} %get-tuple-element.21.q.refs_0_), channel_id=1, source_target_pairs={{0,1},{1,2},{2,3},{3,0},{4,5},{5,6},{6,7},{7,4},{8,9},{9,10},{10,1... | collective-permute-start | bytes 1179656 | tf_op jit(solution)/shard_map/ppermute | solution.py:404
  32.4 33.1 %collective-permute-start.10 = (bf16[16,48,256]{2,1,0:T(8,128)(2,1)}, bf16[16,48,256]{2,1,0:T(8,128)(2,1)}, u32[]{:S(2)}, u32[]{:S(2)}) collective-permute-start(bf16[16,48,256]{2,1,0:T(8,128)(2,1)} %get-tuple-element.21.q.refs_0_), channel_id=1, source_target_pairs={{0,2},{1,3},{2,0},{3,1},{4,6},{5,7},{6,4},{7,5},{8,10},{9,11},{10,... | collective-permute-start | bytes 1179656 | tf_op jit(solution)/shard_map/ppermute | solution.py:404
  37.9 27.6 %collective-permute-start.11 = (bf16[16,48,256]{2,1,0:T(8,128)(2,1)}, bf16[16,48,256]{2,1,0:T(8,128)(2,1)}, u32[]{:S(2)}, u32[]{:S(2)}) collective-permute-start(bf16[16,48,256]{2,1,0:T(8,128)(2,1)} %get-tuple-element.21.q.refs_0_), channel_id=1, source_target_pairs={{0,3},{1,0},{2,1},{3,2},{4,7},{5,4},{6,5},{7,6},{8,11},{9,8},{10,9... | collective-permute-start | bytes 1179656 | tf_op jit(solution)/shard_map/ppermute | solution.py:404
  53.6 65.0 %all-to-all-start = ((bf16[64,56,256]{2,1,0:T(8,128)(2,1)}), bf16[64,56,256]{2,1,0:T(8,128)(2,1)}, u32[]{:S(2)}, u32[]{:S(2)}) async-start(bf16[64,56,256]{2,1,0:T(8,128)(2,1)} %copy-done.1), calls=%async_computation | async-start | bytes 3670016 | tf_op jit(solution)/shard_map/all_to_all | solution.py:448
  79.2 12.8 %collective-permute-start.12 = (bf16[16,56,256]{2,1,0:T(8,128)(2,1)S(1)}, bf16[16,56,256]{2,1,0:T(8,128)(2,1)S(1)}, u32[]{:S(2)}, u32[]{:S(2)}) collective-permute-start(bf16[16,56,256]{2,1,0:T(8,128)(2,1)S(1)} %get-tuple-element.23), channel_id=1, source_target_pairs={{0,3},{1,0},{2,1},{3,2},{4,7},{5,4},{6,5},{7,6},{8,11},{9,8},{10,9... | collective-permute-start | bytes 1376264 | tf_op jit(solution)/shard_map/ppermute | solution.py:404
  79.9 15.1 %collective-permute-start.13 = (bf16[16,56,256]{2,1,0:T(8,128)(2,1)S(1)}, bf16[16,56,256]{2,1,0:T(8,128)(2,1)S(1)}, u32[]{:S(2)}, u32[]{:S(2)}) collective-permute-start(bf16[16,56,256]{2,1,0:T(8,128)(2,1)S(1)} %get-tuple-element.24), channel_id=1, source_target_pairs={{0,2},{1,3},{2,0},{3,1},{4,6},{5,7},{6,4},{7,5},{8,10},{9,11},{10,... | collective-permute-start | bytes 1376264 | tf_op jit(solution)/shard_map/ppermute | solution.py:404
  84.7 15.3 %collective-permute-start.14 = (bf16[16,56,256]{2,1,0:T(8,128)(2,1)S(1)}, bf16[16,56,256]{2,1,0:T(8,128)(2,1)S(1)}, u32[]{:S(2)}, u32[]{:S(2)}) collective-permute-start(bf16[16,56,256]{2,1,0:T(8,128)(2,1)S(1)} %get-tuple-element.25), channel_id=1, source_target_pairs={{0,1},{1,2},{2,3},{3,0},{4,5},{5,6},{6,7},{7,4},{8,9},{9,10},{10,1... | collective-permute-start | bytes 1376264 | tf_op jit(solution)/shard_map/ppermute | solution.py:404
  102.0 5.2 %collective-permute-start.19 = (bf16[4,56,256]{2,1,0:T(8,128)(2,1)S(1)}, bf16[4,56,256]{2,1,0:T(8,128)(2,1)S(1)}, u32[]{:S(2)}, u32[]{:S(2)}) collective-permute-start(bf16[4,56,256]{2,1,0:T(8,128)(2,1)S(1)} %get-tuple-element.29), channel_id=1, source_target_pairs={{0,64},{1,65},{2,66},{3,67},{4,68},{5,69},{6,70},{7,71},{8,72},{9,... | collective-permute-start | bytes 344072 | tf_op jit(solution)/shard_map/ppermute | solution.py:404
  102.9 5.5 %collective-permute-start.20 = (bf16[4,56,256]{2,1,0:T(8,128)(2,1)S(1)}, bf16[4,56,256]{2,1,0:T(8,128)(2,1)S(1)}, u32[]{:S(2)}, u32[]{:S(2)}) collective-permute-start(bf16[4,56,256]{2,1,0:T(8,128)(2,1)S(1)} %get-tuple-element.30), channel_id=1, source_target_pairs={{0,32},{1,33},{2,34},{3,35},{4,36},{5,37},{6,38},{7,39},{8,40},{9,... | collective-permute-start | bytes 344072 | tf_op jit(solution)/shard_map/ppermute | solution.py:404
  109.3 3.7 %collective-permute-start.21 = (bf16[1,56,256]{2,1,0:T(8,128)(2,1)S(1)}, bf16[1,56,256]{2,1,0:T(8,128)(2,1)S(1)}, u32[]{:S(2)}, u32[]{:S(2)}) collective-permute-start(bf16[1,56,256]{2,1,0:T(8,128)(2,1)S(1)} %get-tuple-element.32), channel_id=1, source_target_pairs={{0,12},{1,13},{2,14},{3,15},{4,0},{5,1},{6,2},{7,3},{8,4},{9,5},{1... | collective-permute-start | bytes 86024 | tf_op jit(solution)/shard_map/ppermute | solution.py:404
  112.0 4.2 %collective-permute-start.22 = (bf16[1,56,256]{2,1,0:T(8,128)(2,1)S(1)}, bf16[1,56,256]{2,1,0:T(8,128)(2,1)S(1)}, u32[]{:S(2)}, u32[]{:S(2)}) collective-permute-start(bf16[1,56,256]{2,1,0:T(8,128)(2,1)S(1)} %get-tuple-element.33), channel_id=1, source_target_pairs={{0,8},{1,9},{2,10},{3,11},{4,12},{5,13},{6,14},{7,15},{8,0},{9,1},... | collective-permute-start | bytes 86024 | tf_op jit(solution)/shard_map/ppermute | solution.py:404
  112.0 4.2 %collective-permute-start.23 = (bf16[1,56,256]{2,1,0:T(8,128)(2,1)S(1)}, bf16[1,56,256]{2,1,0:T(8,128)(2,1)S(1)}, u32[]{:S(2)}, u32[]{:S(2)}) collective-permute-start(bf16[1,56,256]{2,1,0:T(8,128)(2,1)S(1)} %get-tuple-element.34), channel_id=1, source_target_pairs={{0,4},{1,5},{2,6},{3,7},{4,8},{5,9},{6,10},{7,11},{8,12},{9,13},{1... | collective-permute-start | bytes 86024 | tf_op jit(solution)/shard_map/ppermute | solution.py:404
  123.6 9.3 %collective-permute-start.24 = (bf16[24,512]{1,0:T(8,128)(2,1)S(1)}, bf16[24,512]{1,0:T(8,128)(2,1)S(1)}, u32[]{:S(2)}, u32[]{:S(2)}) collective-permute-start(bf16[24,512]{1,0:T(8,128)(2,1)S(1)} %get-tuple-element.36), channel_id=1, source_target_pairs={{0,16},{16,0},{1,17},{17,1},{2,18},{18,2},{3,19},{19,3},{4,20},{20... | collective-permute-start | bytes 73736 | tf_op jit(solution)/shard_map/ppermute | solution.py:395
  (20 other events, 211.0 us)

commit v5 on v4

--- a/solution.py
+++ b/solution.py
@@ -19,13 +19,34 @@
 BF16 = jnp.bfloat16
 
 
+def spread_kernel(me, q, theirs, out):
+    first = me[1] == 0
+    mine = jnp.where(first, q[:, :512].astype(F32), q[:, 512:].astype(F32))
+    other = theirs[...].astype(F32)
+    pair = jnp.concatenate([jnp.where(first, mine, other), jnp.where(first, other, mine)], axis=0).astype(BF16)
+    for i in range(16):
+        for c in range(2):
+            out[i, c] = pair[:, c * WIDE:(c + 1) * WIDE]
+
+
+def spread_rows(me, q, theirs):
+    vmem = pl.BlockSpec(memory_space=pltpu.VMEM)
+    smem = pl.BlockSpec(memory_space=pltpu.SMEM)
+    return pl.pallas_call(
+        spread_kernel,
+        out_shape=jax.ShapeDtypeStruct((16, 2, 48, WIDE), BF16),
+        in_specs=[smem, vmem, vmem],
+        out_specs=vmem,
+        name="spread",
+    )(me, q, theirs)
+
+
 def attend_kernel(
     me, cnt, lst, *refs, part,
 ):
-    n_out = 4 if part == 0 else 1
-    qs, (k0, k1, v0), outs = refs[:4], refs[4:7], refs[7:7 + n_out]
-    pq, pj, ps, qv, k, vt, qm, acc, sb, top, shrink, yb, sem = refs[7 + n_out:]
-    my_y, my_core, my_z, my_x = me[0], me[1], me[2], me[3]
+    qs, (k0, k1, v0, _), outs = refs[:4], refs[4:8], refs[8:12]
+    pq, pj, ps, qv, k, vt, qm, acc, sb, top, shrink, yb, sem = refs[12:]
+    my_y, my_core, my_x = me[0], me[1], me[3]
     col = pl.multiple_of(my_core * 512 + part * WIDE, WIDE)
     copies = [
         pltpu.make_async_copy(src, dst, sem.at[i])
@@ -61,18 +82,13 @@
         pj[total + u] = 0
         ps[total + u] = spare
 
-    def place(r2, r3, rz):
-        y = lax.rem(my_y + 4 - jnp.where(my_core == 0, r2, r3), 4)
-        x = lax.rem(my_x + 4 - jnp.where(my_core == 0, r3, r2), 4)
-        z = lax.rem(my_z + 4 - rz, 4)
+    def place(r3, z, a):
+        y = jnp.where(my_core == 0, a, lax.rem(my_y + 4 - r3, 4))
+        x = jnp.where(my_core == 0, lax.rem(my_x + 4 - r3, 4), a)
         return [pl.multiple_of(y * 768 + (c * 16 + z * 4 + x) * 24, 8) for c in range(2)]
 
-    def rows_of(y, z, x):
-        return [pl.multiple_of(y * 768 + (c * 16 + z * 4 + x) * 24, 8) for c in range(2)]
-
-    near = [[place(r2, r3, rz) for r2 in range(4) for rz in range(4)] for r3 in range(4)]
-    plain = [[rows_of(y, z, x) for y in range(4) for z in range(4) for x in range(4)]]
-    for i, spot in enumerate(near):
+    spots = [[place(r3, z, a) for z in range(4) for a in range(4)] for r3 in range(4)]
+    for i, spot in enumerate(spots):
         copies[i].wait()
         for b, rows in enumerate(spot):
             block = qv[i * len(spot) + b].astype(F32)
@@ -159,7 +175,7 @@
 
     lax.fori_loop(0, (total + 1) // 2, two, 0)
 
-    for o, spot in zip(outs, near if part == 0 else plain):
+    for o, spot in zip(outs, spots):
         for b, rows in enumerate(spot):
             data, tail = [], jnp.zeros((8, 128), F32)
             for c, row in enumerate(rows):
@@ -173,16 +189,15 @@
             o[b] = jnp.concatenate(data, axis=0).astype(BF16)
 
 
-def attend(me, cnt, lst, q, k0, k1, v0, part):
-    n_out = 4 if part == 0 else 1
+def attend(me, cnt, lst, q, k0, k1, v0, after, part):
     vmem = pl.BlockSpec(memory_space=pltpu.VMEM)
     smem = pl.BlockSpec(memory_space=pltpu.SMEM)
     whole = pl.BlockSpec(memory_space=pl.ANY)
     return pl.pallas_call(
         functools.partial(attend_kernel, part=part),
-        out_shape=[jax.ShapeDtypeStruct((64 // n_out, 56, WIDE), BF16)] * n_out,
-        in_specs=[smem] * 3 + [whole] * 7,
-        out_specs=[vmem] * n_out,
+        out_shape=[jax.ShapeDtypeStruct((16, 56, WIDE), BF16)] * 4,
+        in_specs=[smem] * 3 + [whole] * 8,
+        out_specs=[vmem] * 4,
         scratch_shapes=[
             pltpu.SMEM((104,), jnp.int32),
             pltpu.SMEM((104,), jnp.int32),
@@ -198,13 +213,13 @@
             pltpu.VMEM((3072, WIDE + 128), F32),
             pltpu.SemaphoreType.DMA((7,)),
         ],
-        compiler_params=pltpu.CompilerParams(vmem_limit_bytes=36 * 2**20),
+        compiler_params=pltpu.CompilerParams(vmem_limit_bytes=24 * 2**20),
         cost_estimate=pl.CostEstimate(flops=10**10, bytes_accessed=2**23, transcendentals=2 * 10**7),
         name="attend",
-    )(me, cnt, lst, *q, k0, k1, v0)
-
-
-def turn_kernel(me, v0, v1, q, out, held, sem):
+    )(me, cnt, lst, *q, k0, k1, v0, after)
+
+
+def turn_kernel(me, v0, v1, out, held, sem):
     col = pl.multiple_of(me[1] * 512, 512)
     copies = [
         pltpu.make_async_copy(v.at[:, :, pl.ds(col, 512)], held.at[pl.ds(i * 4, 4)], sem.at[i])
@@ -223,38 +238,20 @@
     lax.fori_loop(0, 8, one, 0)
 
 
-def turn_values(me, v0, v1, q):
+def turn_values(me, v0, v1):
     vmem = pl.BlockSpec(memory_space=pltpu.VMEM)
     smem = pl.BlockSpec(memory_space=pltpu.SMEM)
     whole = pl.BlockSpec(memory_space=pl.ANY)
     return pl.pallas_call(
         turn_kernel,
         out_shape=jax.ShapeDtypeStruct((8, 512, 256), BF16),
-        in_specs=[smem] + [whole] * 3,
+        in_specs=[smem] + [whole] * 2,
         out_specs=vmem,
         scratch_shapes=[pltpu.VMEM((8, 256, 512), BF16), pltpu.SemaphoreType.DMA((2,))],
         cost_estimate=pl.CostEstimate(flops=10**6, bytes_accessed=2**23, transcendentals=0),
         compiler_params=pltpu.CompilerParams(vmem_limit_bytes=16 * 2**20),
         name="turn",
-    )(me, v0, v1, q)
-
-
-def pack_kernel(p0, p1, p2, p3, k, v, o0, o1):
-    for at, p in enumerate((p0, p1, p2, p3)):
-        for c, o in enumerate((o0, o1)):
-            o[at * 4:at * 4 + 4] = p[:, :, c * WIDE:(c + 1) * WIDE]
-
-
-def pack(parts, k, v):
-    vmem = pl.BlockSpec(memory_space=pltpu.VMEM)
-    whole = pl.BlockSpec(memory_space=pl.ANY)
-    return pl.pallas_call(
-        pack_kernel,
-        out_shape=[jax.ShapeDtypeStruct((16, 48, WIDE), BF16)] * 2,
-        in_specs=[vmem] * 4 + [whole] * 2,
-        out_specs=[vmem] * 2,
-        name="pack",
-    )(*parts, k, v)
+    )(me, v0, v1)
 
 
 def add_up(data, tails, spread):
@@ -290,88 +287,53 @@
     return numer, jnp.concatenate([tail, jnp.zeros((8, WIDE - 128), F32)], axis=1)
 
 
-def merge_kernel(p0, p1, p2, p3, after, *outs):
+def merge_kernel(p0, p1, p2, p3, after, out):
     spread = make_spread().astype(BF16)
     is_top = lax.broadcasted_iota(jnp.int32, (8, 128), 1) % 16 < NH
-    blocks = outs[0].shape[0]
-    for r, out in enumerate(outs):
-        for b in range(blocks):
-            numer, tail = add_blocks([p[r * blocks + b] for p in (p0, p1, p2, p3)], spread, is_top)
-            out[b] = jnp.concatenate(numer + [tail], axis=0).astype(BF16)
+    for b in range(16):
+        numer, tail = add_blocks([p[b] for p in (p0, p1, p2, p3)], spread, is_top)
+        out[b] = jnp.concatenate(numer + [tail], axis=0).astype(BF16)
 
 
 def merge(parts, after):
     vmem = pl.BlockSpec(memory_space=pltpu.VMEM)
-    blocks = parts[0].shape[0] // 4
     return pl.pallas_call(
         merge_kernel,
-        out_shape=[jax.ShapeDtypeStruct((blocks, 56, WIDE), BF16)] * 4,
+        out_shape=jax.ShapeDtypeStruct((16, 56, WIDE), BF16),
         in_specs=[vmem] * 4 + [pl.BlockSpec(memory_space=pl.ANY)],
-        out_specs=[vmem] * 4,
-        compiler_params=pltpu.CompilerParams(vmem_limit_bytes=24 * 2**20),
+        out_specs=vmem,
+        compiler_params=pltpu.CompilerParams(vmem_limit_bytes=16 * 2**20),
         name="merge",
     )(*parts, after)
 
 
-def share_out(numer, total, spread):
+def settle_rows(got):
+    spread = make_spread()
+    held = [got[i] for i in range(16)]
+    numer, _, total = add_up([p[:48] for p in held], [p[48:56, :128].astype(F32) for p in held], spread.astype(BF16))
     totals = jnp.concatenate([total] + [pltpu.roll(total, 128 - 16 * g, 1) for g in range(1, 6)], axis=0)
     wide = jnp.dot(totals, spread.astype(F32), precision=lax.Precision.HIGHEST, preferred_element_type=F32)
     return jnp.concatenate(numer, axis=0) / wide
 
 
-def ring_close_kernel(p0, p1, p2, p3, out):
-    spread = make_spread()
-    held = [p[0] for p in (p0, p1, p2, p3)]
-    numer, _, total = add_up([p[:48] for p in held], [p[48:56, :128].astype(F32) for p in held], spread.astype(BF16))
-    out[...] = share_out(numer, total, spread)
-
-
-def ring_close(parts):
-    vmem = pl.BlockSpec(memory_space=pltpu.VMEM)
-    return pl.pallas_call(
-        ring_close_kernel,
+def first_close_kernel(got, out):
+    out[...] = settle_rows(got)
+
+
+def first_close(got):
+    vmem = pl.BlockSpec(memory_space=pltpu.VMEM)
+    return pl.pallas_call(
+        first_close_kernel,
         out_shape=jax.ShapeDtypeStruct((48, WIDE), F32),
-        in_specs=[vmem] * 4,
+        in_specs=[vmem],
         out_specs=vmem,
-        name="ring_close",
-    )(*parts)
-
-
-def close_kernel(me, ready, got, keep, give, both, shares):
-    spread = make_spread()
-    narrow = spread.astype(BF16)
-
-    def find(i, best):
-        for u in range(16):
-            best = jnp.maximum(best, got[i * 16 + u, 48:56, :128].astype(F32))
-        return best
-
-    best = lax.fori_loop(0, 4, find, jnp.full((8, 128), NO_TOP, F32))
-
-    def weigh(i, total):
-        for u in range(16):
-            t = got[i * 16 + u, 48:56, :128].astype(F32)
-            f = jnp.exp2(jnp.minimum(t - best, 0.0))
-            shares[pl.ds(pl.multiple_of((i * 16 + u) * 8, 8), 8), :] = f
-            total = total + f * (pltpu.roll(t, 128 - NH, 1) + pltpu.roll(t, 128 - 2 * NH, 1))
-        return total
-
-    total = lax.fori_loop(0, 4, weigh, jnp.zeros((8, 128), F32))
-
-    def add(i, numer):
-        numer = list(numer)
-        f = shares[pl.ds(pl.multiple_of(i * 64, 64), 64), :]
-        f = jnp.concatenate([f] + [pltpu.roll(f, 128 - 16 * g, 1) for g in range(1, 6)], axis=0)
-        wide = jnp.dot(f.astype(BF16), narrow, preferred_element_type=F32)
-        for u in range(8):
-            for g in range(6):
-                at = g * 64 + u * 8
-                numer[g] = numer[g] + wide[at:at + 8] * got[i * 8 + u, g * 8:g * 8 + 8, :].astype(F32)
-        return tuple(numer)
-
-    numer = lax.fori_loop(0, 8, add, tuple(jnp.zeros((8, WIDE), F32) for _ in range(6)))
+        name="first_close",
+    )(got)
+
+
+def close_kernel(me, ready, got, keep, give, both):
     both[:, :WIDE] = ready[...]
-    both[:, WIDE:] = share_out(list(numer), total, spread)
+    both[:, WIDE:] = settle_rows(got)
     row = pl.multiple_of(me[1] * 24, 8)
     keep[...] = both[pl.ds(row, 24), :].astype(BF16)
     give[...] = both[pl.ds(24 - row, 24), :].astype(BF16)
@@ -385,8 +347,7 @@
         out_shape=[jax.ShapeDtypeStruct((24, 512), BF16)] * 2,
         in_specs=[smem, vmem, vmem],
         out_specs=[vmem] * 2,
-        scratch_shapes=[pltpu.VMEM((48, 512), F32), pltpu.VMEM((512, 128), F32)],
-        compiler_params=pltpu.CompilerParams(vmem_limit_bytes=16 * 2**20),
+        scratch_shapes=[pltpu.VMEM((48, 512), F32)],
         name="close",
     )(me, ready, got)
 
@@ -408,6 +369,19 @@
     return [x] + [shift(x, axes, by) for by in (1, 2, 3)]
 
 
+def spot(y, c, z, x):
+    return ((y * 2 + c) * 4 + z) * 4 + x
+
+
+GROUPS = [[spot(a, 0, z, w) for z in range(4) for a in range(4)] for w in range(4)] + [
+    [spot(w, 1, z, a) for z in range(4) for a in range(4)] for w in range(4)
+]
+
+
+def exchange(x):
+    return lax.all_to_all(x, ALL, 0, 0, axis_index_groups=GROUPS)
+
+
 def deliver(parts, axes):
     return [parts[0]] + [shift(parts[by], axes, -by) for by in (1, 2, 3)]
 
@@ -417,18 +391,14 @@
     device = lax.axis_index(ALL)
     partner = device + 16 - 32 * core
     own_col = core * 512
-    other_col = 512 - own_col
-
-    mine = lax.dynamic_slice_in_dim(queries, own_col, 512, 1)
-    theirs = swap(lax.dynamic_slice_in_dim(queries, other_col, 512, 1))
+
+    theirs = swap(lax.dynamic_slice_in_dim(queries, 512 - own_col, 512, 1))
     first = core == 0
-    pair = jnp.concatenate([jnp.where(first, mine, theirs), jnp.where(first, theirs, mine)], axis=0)
-    along_z = jnp.concatenate(ring(pair[None], "zz"), axis=0)
+    me = jnp.stack([lax.axis_index(a) for a in ALL]).astype(jnp.int32)
+    plane = exchange(spread_rows(me, queries, theirs))
     k_theirs, v_theirs = swap(keys), swap(values)
-    me = jnp.stack([lax.axis_index(a) for a in ALL]).astype(jnp.int32)
-    planes = pack(ring(along_z, "yx"), k_theirs, v_theirs)
-    v_turned = turn_values(me, values, v_theirs, planes[0])
-    q_parts = [ring(plane, "xy") for plane in planes]
+    v_turned = turn_values(me, values, v_theirs)
+    q_parts = [ring(plane[:, c], "xy") for c in range(2)]
 
     four = jnp.arange(4, dtype=jnp.int32)
     slots = jnp.concatenate([device * 4 + four, partner * 4 + four])
@@ -443,12 +413,11 @@
     lst = jnp.sum(jnp.where(hit, eight[None, None, :], 0), axis=2).reshape(96)
     cnt = jnp.sum(need_i, axis=1)
 
-    sent = deliver(attend(me, cnt, lst, q_parts[0], keys, k_theirs, v_turned, 0), "xy")
-    late = attend(me, cnt, lst, q_parts[1], keys, k_theirs, v_turned, 1)[0]
-    got = lax.all_to_all(late, ("y", "z", "x"), 0, 0)
-    sent = deliver(merge(sent, late), "yx")
-    sent = deliver(merge(sent, late), "zz")
-    keep, give = close(me, ring_close(sent), got)
+    early = attend(me, cnt, lst, q_parts[0], keys, k_theirs, v_turned, q_parts[0][0], 0)
+    late = attend(me, cnt, lst, q_parts[1], keys, k_theirs, v_turned, early[0], 1)
+    early = exchange(merge(deliver(early, "xy"), late[0]))
+    late = exchange(merge(deliver(late, "xy"), late[0]))
+    keep, give = close(me, first_close(early), late)
     give = swap(give)
     rows = jnp.concatenate([jnp.where(first, keep, give), jnp.where(first, give, keep)], axis=1)
     return jnp.dot(rows, out_weight, preferred_element_type=F32).astype(BF16)

time: 133 us -> 122 us (0.917); the launches traced: 134 us -> 121 us
  starting transfers between devices: 52 us -> 44.5 us
  local copies, waits for them, and re-layouts: 11.3 us -> 5.24 us
  Pallas kernels: 33.7 us -> 36.1 us
  other arithmetic: 3.91 us -> 2.34 us
    ppermute x21 -> x12, waiting for transfers between devices: 29.2 us -> 7.36 us  [shift(): return lax.ppermute(x, ALL, pairs)]
    all_to_all x1 -> x3, waiting for transfers between devices: 0.01 us -> 20.9 us  [exchange(): return lax.all_to_all(x, ALL, 0, 0, axis_index_groups=GROUPS)]
    ppermute x21 -> x12, starting transfers between devices: 29.7 us -> 17.1 us  [shift(): return lax.ppermute(x, ALL, pairs)]
    unnamed x36 -> x18, local copies, waits for them, and re-layouts: 10.2 us -> 2.99 us
    all_to_all x1 -> x3, starting transfers between devices: 11.8 us -> 17.4 us  [exchange(): return lax.all_to_all(x, ALL, 0, 0, axis_index_groups=GROUPS)]
    pallas_call x4, Pallas kernels: 5.34 us -> 8.56 us  [the longest x2 4.7 us: merge(): pl.pallas_call(merge_kernel, out_shape=jax.ShapeDtypeStruct((16, 56, WIDE...]
    pallas_call x1, Pallas kernels: 4.2 us -> 2.1 us  [close(): pl.pallas_call(close_kernel, out_shape=[jax.ShapeDtypeStruct((24, 512), B...]
  transfers between devices with their start and end apart: 26 -> 19, of which waited for: 15 -> 8; matrix products, arithmetic and copies ran while one was open for 4% -> 3% of each run, Pallas kernels for 20% -> 28%
where the time goes in v5:
time: 122 us; the launch traced here: 121 us
  starting transfers between devices  44.5 us (36%)
  Pallas kernels  36.1 us (30%)
  waiting for transfers between devices  31.3 us (26%)
  local copies, waits for them, and re-layouts  5.24 us (4%)
  other arithmetic  2.34 us (2%)
    pallas_call x2, Pallas kernels, attend(): pl.pallas_call(functools.partial(attend_kernel, part=part), out_shape=[ja...  22.4 us
    all_to_all x3, waiting for transfers between devices, exchange(): return lax.all_to_all(x, ALL, 0, 0, axis_index_groups=GROUPS)  20.9 us
    all_to_all x3, starting transfers between devices, exchange(): return lax.all_to_all(x, ALL, 0, 0, axis_index_groups=GROUPS)  17.4 us
    ppermute x12, starting transfers between devices, shift(): return lax.ppermute(x, ALL, pairs)  17.1 us
    ppermute x4, starting transfers between devices, swap(): return lax.ppermute(x, 'core', [(0, 1), (1, 0)])  10 us
    ppermute x12, waiting for transfers between devices, shift(): return lax.ppermute(x, ALL, pairs)  7.36 us
    pallas_call x2, Pallas kernels, merge(): pl.pallas_call(merge_kernel, out_shape=jax.ShapeDtypeStruct((16, 56, WIDE...  4.7 us
    pallas_call x1, Pallas kernels, turn_values(): pl.pallas_call(turn_kernel, out_shape=jax.ShapeDtypeStruct((8, 512, 256),...  3.04 us
  transfers between devices with their start and end apart: 19, of which 8 were waited for; matrix products, arithmetic and copies ran while one was open for 3% of the time, Pallas kernels for 28%

profile of v5, /device:TPU:1, one launch (start us, length us, event | category | flops | bytes accessed | tf_op | source)
XLA Modules:
  0.0 120.7 jit_solution(3504474873181737656)
XLA Ops:
  3.4 1.9 %collective-permute-done.theirs = bf16[24,512]{1,0:T(8,128)(2,1)S(1)} collective-permute-done((bf16[24,512]{1,0:T(8,128)(2,1)S(1)}, bf16[24,512]{1,0:T(8,128)(2,1)S(1)}, u32[]{:S(2)}, u32[]{:S(2)}) %collective-permute-start) | collective-permute-done | bytes 24608 | tf_op jit(solution)/shard_map/ppermute | solution.py:356
  6.0 1.8 %spread.1 = bf16[16,2,48,256]{3,2,1,0:T(8,128)(2,1)} custom-call(s32[4]{0:T(128)} %pad_add_fusion.me, bf16[24,1024]{1,0:T(8,128)(2,1)} %q.1, bf16[24,512]{1,0:T(8,128)(2,1)} %copy-done.5), custom_call_target="tpu_custom_call" | custom-call | tf_op jit(solution)/shard_map/spread/pallas_call | solution.py:35
  7.8 7.7 %all-to-all-start = ((bf16[16,2,48,256]{3,2,1,0:T(8,128)(2,1)}), bf16[16,2,48,256]{3,2,1,0:T(8,128)(2,1)}, u32[]{:S(2)}, u32[]{:S(2)}) async-start(bf16[16,2,48,256]{3,2,1,0:T(8,128)(2,1)} %spread.1), calls=%async_computation | async-start | bytes 1572864 | tf_op jit(solution)/shard_map/all_to_all | solution.py:382
  15.9 11.4 %all-to-all-done = bf16[16,2,48,256]{3,2,1,0:T(8,128)(2,1)} async-done(((bf16[16,2,48,256]{3,2,1,0:T(8,128)(2,1)}), bf16[16,2,48,256]{3,2,1,0:T(8,128)(2,1)}, u32[]{:S(2)}, u32[]{:S(2)}) %all-to-all-start) | async-done | bytes 786464 | tf_op jit(solution)/shard_map/all_to_all | solution.py:382
  28.5 1.6 %collective-permute-start.1 = (bf16[16,48,256]{2,1,0:T(8,128)(2,1)S(1)}, bf16[16,48,256]{2,1,0:T(8,128)(2,1)S(1)}, u32[]{:S(2)}, u32[]{:S(2)}) collective-permute-start(bf16[16,48,256]{2,1,0:T(8,128)(2,1)S(1)} %get-tuple-element.26.refs_0_.refs_7_), channel_id=1, source_target_pairs={{0,1},{1,2},{2,3},{3,0},{4,5},{5,6},{6,7},{7,4},{8,9},{9,10},{10,1... | collective-permute-start | bytes 1179656 | tf_op jit(solution)/shard_map/ppermute | solution.py:365
  30.1 2.6 %collective-permute-start.2 = (bf16[16,48,256]{2,1,0:T(8,128)(2,1)S(1)}, bf16[16,48,256]{2,1,0:T(8,128)(2,1)}, u32[]{:S(2)}, u32[]{:S(2)}) collective-permute-start(bf16[16,48,256]{2,1,0:T(8,128)(2,1)S(1)} %get-tuple-element.26.refs_0_.refs_7_), channel_id=1, source_target_pairs={{0,2},{1,3},{2,0},{3,1},{4,6},{5,7},{6,4},{7,5},{8,10},{9,11},{10,... | collective-permute-start | bytes 1179656 | tf_op jit(solution)/shard_map/ppermute | solution.py:365
  35.2 1.6 %copy-done.1 = bf16[4,256,1024]{2,1,0:T(8,128)(2,1)S(1)} copy-done((bf16[4,256,1024]{2,1,0:T(8,128)(2,1)S(1)}, bf16[4,256,1024]{2,1,0:T(8,128)(2,1)}, u32[]{:S(2)}) %copy-start.1) | copy-done | bytes 2097176
  36.8 3.0 %turn.1.refs_6_ = bf16[8,512,256]{2,1,0:T(8,128)(2,1)S(1)} custom-call(s32[4]{0:T(128)S(1)} %copy-done.2, bf16[4,256,1024]{2,1,0:T(8,128)(2,1)S(1)} %copy-done.1, bf16[4,256,1024]{2,1,0:T(8,128)(2,1)} %collective-permute-done.5.v1), custom_call_target="tpu_custom_call" | custom-call | flops 1000000 | bytes 8388608 | tf_op jit(solution)/shard_map/turn/pallas_call | solution.py:245
  40.5 2.0 %collective-permute-done.2.refs_2_ = bf16[16,48,256]{2,1,0:T(8,128)(2,1)} collective-permute-done((bf16[16,48,256]{2,1,0:T(8,128)(2,1)S(1)}, bf16[16,48,256]{2,1,0:T(8,128)(2,1)}, u32[]{:S(2)}, u32[]{:S(2)}) %collective-permute-start.2) | collective-permute-done | bytes 393248 | tf_op jit(solution)/shard_map/ppermute | solution.py:365
  42.5 10.7 %attend.2 = (bf16[16,56,256]{2,1,0:T(8,128)(2,1)S(1)}, bf16[16,56,256]{2,1,0:T(8,128)(2,1)S(1)}, bf16[16,56,256]{2,1,0:T(8,128)(2,1)S(1)}, bf16[16,56,256]{2,1,0:T(8,128)(2,1)S(1)}) custom-call(s32[4]{0:T(128)S(1)} %copy-done.2, s32[12]{0:T(128)S(1)} %get-tuple-element.30.cnt, s32[96]{0:T(128)S(1)} %reshape.37.lst, ...), custom_call_target="tpu_custom_call" | custom-call | flops 10000000000 | bytes 8388608 | tf_op jit(solution)/shard_map/attend/pallas_call | solution.py:196
  53.2 4.2 %collective-permute-start.6 = (bf16[16,56,256]{2,1,0:T(8,128)(2,1)S(1)}, bf16[16,56,256]{2,1,0:T(8,128)(2,1)S(1)}, u32[]{:S(2)}, u32[]{:S(2)}) collective-permute-start(bf16[16,56,256]{2,1,0:T(8,128)(2,1)S(1)} %get-tuple-element.16), channel_id=1, source_target_pairs={{0,3},{1,0},{2,1},{3,2},{4,7},{5,4},{6,5},{7,6},{8,11},{9,8},{10,9... | collective-permute-start | bytes 1376264 | tf_op jit(solution)/shard_map/ppermute | solution.py:365
  58.7 11.7 %attend.3 = (bf16[16,56,256]{2,1,0:T(8,128)(2,1)S(1)}, bf16[16,56,256]{2,1,0:T(8,128)(2,1)}, bf16[16,56,256]{2,1,0:T(8,128)(2,1)}, bf16[16,56,256]{2,1,0:T(8,128)(2,1)}) custom-call(s32[4]{0:T(128)S(1)} %copy-done.2, s32[12]{0:T(128)S(1)} %get-tuple-element.30.cnt, s32[96]{0:T(128)S(1)} %reshape.37.lst, bf16[16,48,256]{2,1,0:T(8,128)(2,1)S(1)} %get-tuple-element.25.refs_0_, ...), custom_call_target="tpu_custom_call" | custom-call | flops 10000000000 | bytes 8388608 | tf_op jit(solution)/shard_map/attend/pallas_call | solution.py:196
  70.4 4.4 %collective-permute-start.12 = (bf16[16,56,256]{2,1,0:T(8,128)(2,1)}, bf16[16,56,256]{2,1,0:T(8,128)(2,1)S(1)}, u32[]{:S(2)}, u32[]{:S(2)}) collective-permute-start(bf16[16,56,256]{2,1,0:T(8,128)(2,1)} %get-tuple-element.20), channel_id=1, source_target_pairs={{0,3},{1,0},{2,1},{3,2},{4,7},{5,4},{6,5},{7,6},{8,11},{9,8},{10,9... | collective-permute-start | bytes 1376264 | tf_op jit(solution)/shard_map/ppermute | solution.py:365
  75.7 1.9 %merge.2 = bf16[16,56,256]{2,1,0:T(8,128)(2,1)} custom-call(bf16[16,56,256]{2,1,0:T(8,128)(2,1)S(1)} %get-tuple-element.15.refs_7_.p0, bf16[16,56,256]{2,1,0:T(8,128)(2,1)S(1)} %collective-permute-done.6.p1, bf16[16,56,256]{2,1,0:T(8,128)(2,1)S(1)} %collective-permute-done.7.p2, bf16[16,56,256]{2,1,0:T(8,128)(2,1)S(1)} %collective-permute-done.8.p3, ...), custom_call_target="tpu_custom_call" | custom-call | tf_op jit(solution)/shard_map/merge/pallas_call | solution.py:300
  77.6 6.1 %all-to-all-start.1 = ((bf16[16,56,256]{2,1,0:T(8,128)(2,1)}), bf16[16,56,256]{2,1,0:T(8,128)(2,1)}, u32[]{:S(2)}, u32[]{:S(2)}) async-start(bf16[16,56,256]{2,1,0:T(8,128)(2,1)} %merge.2), calls=%async_computation.1 | async-start | bytes 917504 | tf_op jit(solution)/shard_map/all_to_all | solution.py:382
  83.7 1.7 %collective-permute-done.12.p1 = bf16[16,56,256]{2,1,0:T(8,128)(2,1)S(1)} collective-permute-done((bf16[16,56,256]{2,1,0:T(8,128)(2,1)}, bf16[16,56,256]{2,1,0:T(8,128)(2,1)S(1)}, u32[]{:S(2)}, u32[]{:S(2)}) %collective-permute-start.12) | collective-permute-done | bytes 458784 | tf_op jit(solution)/shard_map/ppermute | solution.py:365
  85.4 3.6 %collective-permute-done.14.p3 = bf16[16,56,256]{2,1,0:T(8,128)(2,1)} collective-permute-done((bf16[16,56,256]{2,1,0:T(8,128)(2,1)}, bf16[16,56,256]{2,1,0:T(8,128)(2,1)}, u32[]{:S(2)}, u32[]{:S(2)}) %collective-permute-start.14) | collective-permute-done | bytes 458784 | tf_op jit(solution)/shard_map/ppermute | solution.py:365
  89.0 2.8 %merge.3 = bf16[16,56,256]{2,1,0:T(8,128)(2,1)} custom-call(bf16[16,56,256]{2,1,0:T(8,128)(2,1)S(1)} %get-tuple-element.19.after.p0, bf16[16,56,256]{2,1,0:T(8,128)(2,1)S(1)} %collective-permute-done.12.p1, bf16[16,56,256]{2,1,0:T(8,128)(2,1)S(1)} %collective-permute-done.13.p2, bf16[16,56,256]{2,1,0:T(8,128)(2,1)} %collective-permute-done.14.p3, ...), custom_call_target="tpu_custom_call" | custom-call | tf_op jit(solution)/shard_map/merge/pallas_call | solution.py:300
  91.9 3.0 %all-to-all-done.1.got = bf16[16,56,256]{2,1,0:T(8,128)(2,1)} async-done(((bf16[16,56,256]{2,1,0:T(8,128)(2,1)}), bf16[16,56,256]{2,1,0:T(8,128)(2,1)}, u32[]{:S(2)}, u32[]{:S(2)}) %all-to-all-start.1) | async-done | bytes 458784 | tf_op jit(solution)/shard_map/all_to_all | solution.py:382
  94.9 3.6 %all-to-all-start.2 = ((bf16[16,56,256]{2,1,0:T(8,128)(2,1)}), bf16[16,56,256]{2,1,0:T(8,128)(2,1)S(1)}, u32[]{:S(2)}, u32[]{:S(2)}) async-start(bf16[16,56,256]{2,1,0:T(8,128)(2,1)} %merge.3), calls=%async_computation.2 | async-start | bytes 917504 | tf_op jit(solution)/shard_map/all_to_all | solution.py:382
  98.5 2.1 %first_close.1.ready = f32[48,256]{1,0:T(8,128)} custom-call(bf16[16,56,256]{2,1,0:T(8,128)(2,1)} %all-to-all-done.1.got), custom_call_target="tpu_custom_call" | custom-call | tf_op jit(solution)/shard_map/first_close/pallas_call | solution.py:325
  100.5 6.5 %all-to-all-done.2.got = bf16[16,56,256]{2,1,0:T(8,128)(2,1)S(1)} async-done(((bf16[16,56,256]{2,1,0:T(8,128)(2,1)}), bf16[16,56,256]{2,1,0:T(8,128)(2,1)S(1)}, u32[]{:S(2)}, u32[]{:S(2)}) %all-to-all-start.2) | async-done | bytes 458784 | tf_op jit(solution)/shard_map/all_to_all | solution.py:382
  107.8 2.1 %close.1 = (bf16[24,512]{1,0:T(8,128)(2,1)}, bf16[24,512]{1,0:T(8,128)(2,1)}) custom-call(s32[4]{0:T(128)} %pad_add_fusion.me, f32[48,256]{1,0:T(8,128)} %first_close.1.ready, bf16[16,56,256]{2,1,0:T(8,128)(2,1)} %copy-done.4), custom_call_target="tpu_custom_call" | custom-call | tf_op jit(solution)/shard_map/close/pallas_call | solution.py:345
  109.9 7.9 %collective-permute-start.15 = (bf16[24,512]{1,0:T(8,128)(2,1)}, bf16[24,512]{1,0:T(8,128)(2,1)S(1)}, u32[]{:S(2)}, u32[]{:S(2)}) collective-permute-start(bf16[24,512]{1,0:T(8,128)(2,1)} %get-tuple-element.24), channel_id=1, source_target_pairs={{0,16},{16,0},{1,17},{17,1},{2,18},{18,2},{3,19},{19,3},{4,20},{20... | collective-permute-start | bytes 73736 | tf_op jit(solution)/shard_map/ppermute | solution.py:356
  (58 shorter events, 14.5 us)
Async XLA Ops:
  0.0 119.7 %copy-start = (bf16[1024,1024]{1,0:T(8,128)(2,1)S(1)}, bf16[1024,1024]{1,0:T(8,128)(2,1)}, u32[]{:S(2)}) copy-start(bf16[1024,1024]{1,0:T(8,128)(2,1)} %param.13) | copy-start | bytes 6291460
  0.0 15.6 %copy-start.7 = (s32[512]{0:T(512)S(1)}, s32[512]{0:T(512)}, u32[]{:S(2)}) copy-start(s32[512]{0:T(512)} %param.10) | copy-start | bytes 6148
  0.0 15.8 %copy-start.8 = (s32[12]{0:T(128)S(1)}, s32[12]{0:T(128)}, u32[]{:S(2)}) copy-start(s32[12]{0:T(128)} %param.12) | copy-start | bytes 148
  0.0 33.4 %copy-start.6 = (s32[12,160]{1,0:T(8,128)S(1)}, s32[12,160]{1,0:T(8,128)}, u32[]{:S(2)}) copy-start(s32[12,160]{1,0:T(8,128)} %param.11) | copy-start | bytes 23044
  0.0 34.4 %collective-permute-start.5 = (bf16[4,256,1024]{2,1,0:T(8,128)(2,1)}, bf16[4,256,1024]{2,1,0:T(8,128)(2,1)}, u32[]{:S(2)}, u32[]{:S(2)}) collective-permute-start(bf16[4,256,1024]{2,1,0:T(8,128)(2,1)} %v0.1), channel_id=1, source_target_pairs={{0,16},{16,0},{1,17},{17,1},{2,18},{18,2},{3,19},{19,3},{4,20},{20... | collective-permute-start | bytes 6291464 | tf_op jit(solution)/shard_map/ppermute | solution.py:356
  1.5 41.0 %collective-permute-start.4 = (bf16[4,256,1024]{2,1,0:T(8,128)(2,1)}, bf16[4,256,1024]{2,1,0:T(8,128)(2,1)}, u32[]{:S(2)}, u32[]{:S(2)}) collective-permute-start(bf16[4,256,1024]{2,1,0:T(8,128)(2,1)} %refs_4_.3), channel_id=1, source_target_pairs={{0,16},{16,0},{1,17},{17,1},{2,18},{18,2},{3,19},{19,3},{4,20},{20... | collective-permute-start | bytes 6291464 | tf_op jit(solution)/shard_map/ppermute | solution.py:356
  2.3 3.0 %collective-permute-start = (bf16[24,512]{1,0:T(8,128)(2,1)S(1)}, bf16[24,512]{1,0:T(8,128)(2,1)S(1)}, u32[]{:S(2)}, u32[]{:S(2)}) collective-permute-start(bf16[24,512]{1,0:T(8,128)(2,1)S(1)} %constant_dynamic-slice_fusion), channel_id=1, source_target_pairs={{0,16},{16,0},{1,17},{17,1},{2,18},{18,2},{3,19},{19,3},{4,20},{20... | collective-permute-start | bytes 73736 | tf_op jit(solution)/shard_map/ppermute | solution.py:356
  3.4 31.8 %copy-start.2 = (s32[4]{0:T(128)S(1)}, s32[4]{0:T(128)}, u32[]{:S(2)}) copy-start(s32[4]{0:T(128)} %pad_add_fusion.me) | copy-start | bytes 52
  7.8 19.5 %all-to-all-start = ((bf16[16,2,48,256]{3,2,1,0:T(8,128)(2,1)}), bf16[16,2,48,256]{3,2,1,0:T(8,128)(2,1)}, u32[]{:S(2)}, u32[]{:S(2)}) async-start(bf16[16,2,48,256]{3,2,1,0:T(8,128)(2,1)} %spread.1), calls=%async_computation | async-start | bytes 1572864 | tf_op jit(solution)/shard_map/all_to_all | solution.py:382
  28.5 11.4 %collective-permute-start.1 = (bf16[16,48,256]{2,1,0:T(8,128)(2,1)S(1)}, bf16[16,48,256]{2,1,0:T(8,128)(2,1)S(1)}, u32[]{:S(2)}, u32[]{:S(2)}) collective-permute-start(bf16[16,48,256]{2,1,0:T(8,128)(2,1)S(1)} %get-tuple-element.26.refs_0_.refs_7_), channel_id=1, source_target_pairs={{0,1},{1,2},{2,3},{3,0},{4,5},{5,6},{6,7},{7,4},{8,9},{9,10},{10,1... | collective-permute-start | bytes 1179656 | tf_op jit(solution)/shard_map/ppermute | solution.py:365
  30.1 12.4 %collective-permute-start.2 = (bf16[16,48,256]{2,1,0:T(8,128)(2,1)S(1)}, bf16[16,48,256]{2,1,0:T(8,128)(2,1)}, u32[]{:S(2)}, u32[]{:S(2)}) collective-permute-start(bf16[16,48,256]{2,1,0:T(8,128)(2,1)S(1)} %get-tuple-element.26.refs_0_.refs_7_), channel_id=1, source_target_pairs={{0,2},{1,3},{2,0},{3,1},{4,6},{5,7},{6,4},{7,5},{8,10},{9,11},{10,... | collective-permute-start | bytes 1179656 | tf_op jit(solution)/shard_map/ppermute | solution.py:365
  32.7 9.8 %collective-permute-start.3 = (bf16[16,48,256]{2,1,0:T(8,128)(2,1)S(1)}, bf16[16,48,256]{2,1,0:T(8,128)(2,1)}, u32[]{:S(2)}, u32[]{:S(2)}) collective-permute-start(bf16[16,48,256]{2,1,0:T(8,128)(2,1)S(1)} %get-tuple-element.26.refs_0_.refs_7_), channel_id=1, source_target_pairs={{0,3},{1,0},{2,1},{3,2},{4,7},{5,4},{6,5},{7,6},{8,11},{9,8},{10,9... | collective-permute-start | bytes 1179656 | tf_op jit(solution)/shard_map/ppermute | solution.py:365
  34.5 23.5 %collective-permute-start.9 = (bf16[16,48,256]{2,1,0:T(8,128)(2,1)S(1)}, bf16[16,48,256]{2,1,0:T(8,128)(2,1)S(1)}, u32[]{:S(2)}, u32[]{:S(2)}) collective-permute-start(bf16[16,48,256]{2,1,0:T(8,128)(2,1)S(1)} %get-tuple-element.25.refs_0_), channel_id=1, source_target_pairs={{0,1},{1,2},{2,3},{3,0},{4,5},{5,6},{6,7},{7,4},{8,9},{9,10},{10,1... | collective-permute-start | bytes 1179656 | tf_op jit(solution)/shard_map/ppermute | solution.py:365
  39.9 18.9 %collective-permute-start.10 = (bf16[16,48,256]{2,1,0:T(8,128)(2,1)S(1)}, bf16[16,48,256]{2,1,0:T(8,128)(2,1)S(1)}, u32[]{:S(2)}, u32[]{:S(2)}) collective-permute-start(bf16[16,48,256]{2,1,0:T(8,128)(2,1)S(1)} %get-tuple-element.25.refs_0_), channel_id=1, source_target_pairs={{0,2},{1,3},{2,0},{3,1},{4,6},{5,7},{6,4},{7,5},{8,10},{9,11},{10,... | collective-permute-start | bytes 1179656 | tf_op jit(solution)/shard_map/ppermute | solution.py:365
  42.5 16.3 %collective-permute-start.11 = (bf16[16,48,256]{2,1,0:T(8,128)(2,1)S(1)}, bf16[16,48,256]{2,1,0:T(8,128)(2,1)S(1)}, u32[]{:S(2)}, u32[]{:S(2)}) collective-permute-start(bf16[16,48,256]{2,1,0:T(8,128)(2,1)S(1)} %get-tuple-element.25.refs_0_), channel_id=1, source_target_pairs={{0,3},{1,0},{2,1},{3,2},{4,7},{5,4},{6,5},{7,6},{8,11},{9,8},{10,9... | collective-permute-start | bytes 1179656 | tf_op jit(solution)/shard_map/ppermute | solution.py:365
  53.2 21.7 %collective-permute-start.6 = (bf16[16,56,256]{2,1,0:T(8,128)(2,1)S(1)}, bf16[16,56,256]{2,1,0:T(8,128)(2,1)S(1)}, u32[]{:S(2)}, u32[]{:S(2)}) collective-permute-start(bf16[16,56,256]{2,1,0:T(8,128)(2,1)S(1)} %get-tuple-element.16), channel_id=1, source_target_pairs={{0,3},{1,0},{2,1},{3,2},{4,7},{5,4},{6,5},{7,6},{8,11},{9,8},{10,9... | collective-permute-start | bytes 1376264 | tf_op jit(solution)/shard_map/ppermute | solution.py:365
  57.4 18.3 %collective-permute-start.7 = (bf16[16,56,256]{2,1,0:T(8,128)(2,1)S(1)}, bf16[16,56,256]{2,1,0:T(8,128)(2,1)S(1)}, u32[]{:S(2)}, u32[]{:S(2)}) collective-permute-start(bf16[16,56,256]{2,1,0:T(8,128)(2,1)S(1)} %get-tuple-element.17), channel_id=1, source_target_pairs={{0,2},{1,3},{2,0},{3,1},{4,6},{5,7},{6,4},{7,5},{8,10},{9,11},{10,... | collective-permute-start | bytes 1376264 | tf_op jit(solution)/shard_map/ppermute | solution.py:365
  58.0 17.8 %collective-permute-start.8 = (bf16[16,56,256]{2,1,0:T(8,128)(2,1)S(1)}, bf16[16,56,256]{2,1,0:T(8,128)(2,1)S(1)}, u32[]{:S(2)}, u32[]{:S(2)}) collective-permute-start(bf16[16,56,256]{2,1,0:T(8,128)(2,1)S(1)} %get-tuple-element.18), channel_id=1, source_target_pairs={{0,1},{1,2},{2,3},{3,0},{4,5},{5,6},{6,7},{7,4},{8,9},{9,10},{10,1... | collective-permute-start | bytes 1376264 | tf_op jit(solution)/shard_map/ppermute | solution.py:365
  70.4 15.0 %collective-permute-start.12 = (bf16[16,56,256]{2,1,0:T(8,128)(2,1)}, bf16[16,56,256]{2,1,0:T(8,128)(2,1)S(1)}, u32[]{:S(2)}, u32[]{:S(2)}) collective-permute-start(bf16[16,56,256]{2,1,0:T(8,128)(2,1)} %get-tuple-element.20), channel_id=1, source_target_pairs={{0,3},{1,0},{2,1},{3,2},{4,7},{5,4},{6,5},{7,6},{8,11},{9,8},{10,9... | collective-permute-start | bytes 1376264 | tf_op jit(solution)/shard_map/ppermute | solution.py:365
  74.8 10.7 %collective-permute-start.13 = (bf16[16,56,256]{2,1,0:T(8,128)(2,1)}, bf16[16,56,256]{2,1,0:T(8,128)(2,1)S(1)}, u32[]{:S(2)}, u32[]{:S(2)}) collective-permute-start(bf16[16,56,256]{2,1,0:T(8,128)(2,1)} %get-tuple-element.21), channel_id=1, source_target_pairs={{0,2},{1,3},{2,0},{3,1},{4,6},{5,7},{6,4},{7,5},{8,10},{9,11},{10,... | collective-permute-start | bytes 1376264 | tf_op jit(solution)/shard_map/ppermute | solution.py:365
  75.0 14.1 %collective-permute-start.14 = (bf16[16,56,256]{2,1,0:T(8,128)(2,1)}, bf16[16,56,256]{2,1,0:T(8,128)(2,1)}, u32[]{:S(2)}, u32[]{:S(2)}) collective-permute-start(bf16[16,56,256]{2,1,0:T(8,128)(2,1)} %get-tuple-element.22), channel_id=1, source_target_pairs={{0,1},{1,2},{2,3},{3,0},{4,5},{5,6},{6,7},{7,4},{8,9},{9,10},{10,1... | collective-permute-start | bytes 1376264 | tf_op jit(solution)/shard_map/ppermute | solution.py:365
  77.6 17.3 %all-to-all-start.1 = ((bf16[16,56,256]{2,1,0:T(8,128)(2,1)}), bf16[16,56,256]{2,1,0:T(8,128)(2,1)}, u32[]{:S(2)}, u32[]{:S(2)}) async-start(bf16[16,56,256]{2,1,0:T(8,128)(2,1)} %merge.2), calls=%async_computation.1 | async-start | bytes 917504 | tf_op jit(solution)/shard_map/all_to_all | solution.py:382
  94.9 12.1 %all-to-all-start.2 = ((bf16[16,56,256]{2,1,0:T(8,128)(2,1)}), bf16[16,56,256]{2,1,0:T(8,128)(2,1)S(1)}, u32[]{:S(2)}, u32[]{:S(2)}) async-start(bf16[16,56,256]{2,1,0:T(8,128)(2,1)} %merge.3), calls=%async_computation.2 | async-start | bytes 917504 | tf_op jit(solution)/shard_map/all_to_all | solution.py:382
  109.9 9.0 %collective-permute-start.15 = (bf16[24,512]{1,0:T(8,128)(2,1)}, bf16[24,512]{1,0:T(8,128)(2,1)S(1)}, u32[]{:S(2)}, u32[]{:S(2)}) collective-permute-start(bf16[24,512]{1,0:T(8,128)(2,1)} %get-tuple-element.24), channel_id=1, source_target_pairs={{0,16},{16,0},{1,17},{17,1},{2,18},{18,2},{3,19},{19,3},{4,20},{20... | collective-permute-start | bytes 73736 | tf_op jit(solution)/shard_map/ppermute | solution.py:356
  (4 other events, 8.6 us)

commit v6 on v5

--- a/solution.py
+++ b/solution.py
@@ -42,10 +42,10 @@
 
 
 def attend_kernel(
-    me, cnt, lst, *refs, part,
+    me, need, *refs, part,
 ):
     qs, (k0, k1, v0, _), outs = refs[:4], refs[4:8], refs[8:12]
-    pq, pj, ps, qv, k, vt, qm, acc, sb, top, shrink, yb, sem = refs[12:]
+    cnt, plan, qv, k, vt, qm, acc, sb, top, shrink, yb, sem = refs[12:]
     my_y, my_core, my_x = me[0], me[1], me[3]
     col = pl.multiple_of(my_core * 512 + part * WIDE, WIDE)
     copies = [
@@ -64,23 +64,25 @@
     scale = HD ** -0.5 * LOG2E
     ones = jnp.ones((16, 256), BF16)
 
-    def list_frame(qi, carry):
-        at, slot = carry
-
-        def put(i, at):
-            pj[at] = lst[qi * 8 + i]
-            pq[at] = qi
-            ps[at] = slot
-            return at + 1
-
-        n = cnt[qi]
-        return lax.fori_loop(0, n, put, at), jnp.where(n > 0, 1 - slot, slot)
-
-    total, spare = lax.fori_loop(0, 12, list_frame, (jnp.int32(0), jnp.int32(0)))
-    for u in range(5):
-        pq[total + u] = 12
-        pj[total + u] = 0
-        ps[total + u] = spare
+    total, slot = jnp.int32(0), jnp.int32(0)
+    for qi in range(12):
+        begin = total
+        for j in range(8):
+            plan[total] = qi + 16 * j + 256 * slot
+            total = total + need[qi, j]
+        cnt[qi] = total - begin
+        slot = (slot + jnp.minimum(total - begin, 1)) & 3
+    for u in range(8):
+        plan[total + u] = 12 + 256 * slot
+
+    def frame_of(t):
+        return plan[t] & 15
+
+    def held_of(t):
+        return (plan[t] >> 4) & 7
+
+    def slot_of(t):
+        return plan[t] >> 8
 
     def place(r3, z, a):
         y = jnp.where(my_core == 0, a, lax.rem(my_y + 4 - r3, 4))
@@ -119,13 +121,13 @@
 
     def score(t, p, h):
         hp = h // 2
-        keys = k[pj[t + p], :, hp * 128:(hp + 1) * 128]
-        s = jnp.dot(keys, qm[pq[t + p], h], preferred_element_type=F32) * scale
+        keys = k[held_of(t + p), :, hp * 128:(hp + 1) * 128]
+        s = jnp.dot(keys, qm[frame_of(t + p), h], preferred_element_type=F32) * scale
         sb[p, h] = s
         return jnp.max(s, axis=0, keepdims=True)
 
     def settle(t, p, highs, old):
-        first = pq[t + p] != pq[jnp.maximum(t + p - 1, 0)]
+        first = frame_of(t + p) != frame_of(jnp.maximum(t + p - 1, 0))
         old = jnp.where(first, NO_TOP, old)
         high = jnp.concatenate(highs, axis=0)
         new = jnp.maximum(old, jnp.ceil(high * (1.0 / TOP_STEP)) * TOP_STEP)
@@ -135,17 +137,17 @@
 
     def weigh(t, p, h, tops, shrinks):
         weights = jnp.exp2(sb[p, h] - tops[h:h + 1]).astype(BF16)
-        vals = jnp.concatenate([vt[pj[t + p], h * 64:(h + 1) * 64, :], ones], axis=0)
+        vals = jnp.concatenate([vt[held_of(t + p), h * 64:(h + 1) * 64, :], ones], axis=0)
         part = jnp.dot(vals, weights, preferred_element_type=F32)
-        at = ps[t + p]
+        at = slot_of(t + p)
         acc[at, h] = acc[at, h] * shrinks[h:h + 1] + part
 
     def finish(t, p, tops):
-        qi = pq[t + p]
-
-        @pl.when((qi < 12) & (pq[t + p + 1] != qi))
+        qi = frame_of(t + p)
+
+        @pl.when((qi < 12) & (frame_of(t + p + 1) != qi))
         def _():
-            at = ps[t + p]
+            at = slot_of(t + p)
             rows = pl.ds(pl.multiple_of(qi * 256, 256), 256)
             totals = jnp.concatenate([acc[at, h, 64:65, :] for h in range(NH)], axis=0)
             hi = totals.astype(BF16).astype(F32)
@@ -156,24 +158,25 @@
             yb[rows, WIDE:] = jnp.concatenate(extra, axis=0).T
 
     old = jnp.full((NH, 256), NO_TOP, F32)
-    for p in range(2):
+    for p in range(4):
         old = settle(0, p, [score(0, p, h) for h in range(NH)], old)
 
     def two(u, _):
-        t = u * 2
-        tops, shrinks = [top[0], top[1]], [shrink[0], shrink[1]]
-        highs = [[], []]
-        for p in range(2):
+        t = u * 4
+        tops, shrinks = [top[p] for p in range(4)], [shrink[p] for p in range(4)]
+        highs = [[] for p in range(4)]
+        for p in range(4):
             for h in range(NH):
                 weigh(t, p, h, tops[p], shrinks[p])
-                highs[p].append(score(t + 2, p, h))
-        old = settle(t + 2, 0, highs[0], tops[1])
-        settle(t + 2, 1, highs[1], old)
-        for p in range(2):
+                highs[p].append(score(t + 4, p, h))
+        old = tops[3]
+        for p in range(4):
+            old = settle(t + 4, p, highs[p], old)
+        for p in range(4):
             finish(t, p, tops[p])
         return 0
 
-    lax.fori_loop(0, (total + 1) // 2, two, 0)
+    lax.fori_loop(0, (total + 3) // 4, two, 0)
 
     for o, spot in zip(outs, spots):
         for b, rows in enumerate(spot):
@@ -189,37 +192,38 @@
             o[b] = jnp.concatenate(data, axis=0).astype(BF16)
 
 
-def attend(me, cnt, lst, q, k0, k1, v0, after, part):
+def attend(me, need, q, k0, k1, v0, after, part):
     vmem = pl.BlockSpec(memory_space=pltpu.VMEM)
     smem = pl.BlockSpec(memory_space=pltpu.SMEM)
     whole = pl.BlockSpec(memory_space=pl.ANY)
     return pl.pallas_call(
         functools.partial(attend_kernel, part=part),
         out_shape=[jax.ShapeDtypeStruct((16, 56, WIDE), BF16)] * 4,
-        in_specs=[smem] * 3 + [whole] * 8,
+        in_specs=[smem] * 2 + [whole] * 8,
         out_specs=[vmem] * 4,
         scratch_shapes=[
-            pltpu.SMEM((104,), jnp.int32),
-            pltpu.SMEM((104,), jnp.int32),
-            pltpu.SMEM((104,), jnp.int32),
+            pltpu.SMEM((12,), jnp.int32),
+            pltpu.SMEM((112,), jnp.int32),
             pltpu.VMEM((64, 48, WIDE), BF16),
             pltpu.VMEM((8, 256, WIDE), BF16),
             pltpu.VMEM((8, WIDE, 256), BF16),
             pltpu.VMEM((13, NH, 128, 256), BF16),
-            pltpu.VMEM((2, NH, 80, 256), F32),
-            pltpu.VMEM((2, NH, 256, 256), F32),
-            pltpu.VMEM((2, NH, 256), F32),
-            pltpu.VMEM((2, NH, 256), F32),
+            pltpu.VMEM((4, NH, 80, 256), F32),
+            pltpu.VMEM((4, NH, 256, 256), F32),
+            pltpu.VMEM((4, NH, 256), F32),
+            pltpu.VMEM((4, NH, 256), F32),
             pltpu.VMEM((3072, WIDE + 128), F32),
             pltpu.SemaphoreType.DMA((7,)),
         ],
         compiler_params=pltpu.CompilerParams(vmem_limit_bytes=24 * 2**20),
         cost_estimate=pl.CostEstimate(flops=10**10, bytes_accessed=2**23, transcendentals=2 * 10**7),
         name="attend",
-    )(me, cnt, lst, *q, k0, k1, v0, after)
-
-
-def turn_kernel(me, v0, v1, out, held, sem):
+    )(me, need, *q, k0, k1, v0, after)
+
+
+def turn_kernel(me, v0, v1, k, out, parts, held, sem):
+    parts[0] = 0
+    parts[1] = 1
     col = pl.multiple_of(me[1] * 512, 512)
     copies = [
         pltpu.make_async_copy(v.at[:, :, pl.ds(col, 512)], held.at[pl.ds(i * 4, 4)], sem.at[i])
@@ -238,20 +242,20 @@
     lax.fori_loop(0, 8, one, 0)
 
 
-def turn_values(me, v0, v1):
+def turn_values(me, v0, v1, k):
     vmem = pl.BlockSpec(memory_space=pltpu.VMEM)
     smem = pl.BlockSpec(memory_space=pltpu.SMEM)
     whole = pl.BlockSpec(memory_space=pl.ANY)
     return pl.pallas_call(
         turn_kernel,
-        out_shape=jax.ShapeDtypeStruct((8, 512, 256), BF16),
-        in_specs=[smem] + [whole] * 2,
-        out_specs=vmem,
+        out_shape=[jax.ShapeDtypeStruct((8, 512, 256), BF16), jax.ShapeDtypeStruct((2,), jnp.int32)],
+        in_specs=[smem] + [whole] * 3,
+        out_specs=[vmem, smem],
         scratch_shapes=[pltpu.VMEM((8, 256, 512), BF16), pltpu.SemaphoreType.DMA((2,))],
         cost_estimate=pl.CostEstimate(flops=10**6, bytes_accessed=2**23, transcendentals=0),
         compiler_params=pltpu.CompilerParams(vmem_limit_bytes=16 * 2**20),
         name="turn",
-    )(me, v0, v1)
+    )(me, v0, v1, k)
 
 
 def add_up(data, tails, spread):
@@ -352,6 +356,27 @@
     )(me, ready, got)
 
 
+def project_kernel(me, keep, give, weight, out):
+    first = me[1] == 0
+    mine, other = keep[...].astype(F32), give[...].astype(F32)
+    left = jnp.where(first, mine, other).astype(BF16)
+    right = jnp.where(first, other, mine).astype(BF16)
+    total = jnp.dot(left, weight[:512], preferred_element_type=F32)
+    out[...] = (total + jnp.dot(right, weight[512:], preferred_element_type=F32)).astype(BF16)
+
+
+def project(me, keep, give, weight):
+    vmem = pl.BlockSpec(memory_space=pltpu.VMEM)
+    smem = pl.BlockSpec(memory_space=pltpu.SMEM)
+    return pl.pallas_call(
+        project_kernel,
+        out_shape=jax.ShapeDtypeStruct((24, 1024), BF16),
+        in_specs=[smem] + [vmem] * 3,
+        out_specs=vmem,
+        name="project",
+    )(me, keep, give, weight)
+
+
 def swap(x):
     return lax.ppermute(x, "core", [(0, 1), (1, 0)])
 
@@ -393,12 +418,11 @@
     own_col = core * 512
 
     theirs = swap(lax.dynamic_slice_in_dim(queries, 512 - own_col, 512, 1))
-    first = core == 0
     me = jnp.stack([lax.axis_index(a) for a in ALL]).astype(jnp.int32)
     plane = exchange(spread_rows(me, queries, theirs))
     k_theirs, v_theirs = swap(keys), swap(values)
-    v_turned = turn_values(me, values, v_theirs)
-    q_parts = [ring(plane[:, c], "xy") for c in range(2)]
+    v_turned, parts = turn_values(me, values, v_theirs, k_theirs)
+    q_parts = [ring(lax.dynamic_index_in_dim(plane, parts[c], 1, False), "xy") for c in range(2)]
 
     four = jnp.arange(4, dtype=jnp.int32)
     slots = jnp.concatenate([device * 4 + four, partner * 4 + four])
@@ -406,21 +430,15 @@
     local = jnp.sum(jnp.where(frame_slot[None, :] == slots[:, None], frame_ids[None, :], 0), axis=1)
     used = jnp.arange(covisible.shape[1], dtype=jnp.int32)[None, :] < counts[:, None]
     need = jnp.any((covisible[:, None, :] == local[None, :, None]) & used[:, None, :], axis=2)
-    need_i = need.astype(jnp.int32)
-    place = jnp.cumsum(need_i, axis=1) - need_i
-    eight = jnp.arange(8, dtype=jnp.int32)
-    hit = need[:, None, :] & (place[:, None, :] == eight[None, :, None])
-    lst = jnp.sum(jnp.where(hit, eight[None, None, :], 0), axis=2).reshape(96)
-    cnt = jnp.sum(need_i, axis=1)
-
-    early = attend(me, cnt, lst, q_parts[0], keys, k_theirs, v_turned, q_parts[0][0], 0)
-    late = attend(me, cnt, lst, q_parts[1], keys, k_theirs, v_turned, early[0], 1)
+    need = need.astype(jnp.int32)
+
+    early = attend(me, need, q_parts[0], keys, k_theirs, v_turned, q_parts[0][0], 0)
+    late = attend(me, need, q_parts[1], keys, k_theirs, v_turned, early[0], 1)
     early = exchange(merge(deliver(early, "xy"), late[0]))
     late = exchange(merge(deliver(late, "xy"), late[0]))
     keep, give = close(me, first_close(early), late)
     give = swap(give)
-    rows = jnp.concatenate([jnp.where(first, keep, give), jnp.where(first, give, keep)], axis=1)
-    return jnp.dot(rows, out_weight, preferred_element_type=F32).astype(BF16)
+    return project(me, keep, give, out_weight)
 
 
 def solution(mesh):

time: 122 us -> 121 us (level); the launches traced: 121 us -> 122 us
  waiting for transfers between devices: 31.3 us -> 24.6 us
  starting transfers between devices: 44.5 us -> 49.7 us
  between operations: 0.17 us -> 3.82 us
  local copies, waits for them, and re-layouts: 5.24 us -> 7.88 us
  Pallas kernels: 36.1 us -> 34.2 us
    all_to_all x3, starting transfers between devices: 17.4 us -> 24.1 us  [exchange(): return lax.all_to_all(x, ALL, 0, 0, axis_index_groups=GROUPS)]
    all_to_all x3, waiting for transfers between devices: 20.9 us -> 16.1 us  [exchange(): return lax.all_to_all(x, ALL, 0, 0, axis_index_groups=GROUPS)]
    pallas_call x2, Pallas kernels: 22.4 us -> 18.3 us  [attend(): pl.pallas_call(functools.partial(attend_kernel, part=part), out_shape=[ja...]
    unnamed x18 -> x24, local copies, waits for them, and re-layouts: 2.99 us -> 6.5 us
    ppermute x4, starting transfers between devices: 10 us -> 6.8 us  [swap(): return lax.ppermute(x, 'core', [(0, 1), (1, 0)])]
    pallas_call x1 -> x2, Pallas kernels: 3.04 us -> 6.21 us  [the longest x1 3.49 us: turn_values(): pl.pallas_call(turn_kernel, out_shape=[jax.ShapeDtypeStruct((8, 512, 256)...]
    ppermute x12, starting transfers between devices: 17.1 us -> 18.9 us  [shift(): return lax.ppermute(x, ALL, pairs)]
    ppermute x12, waiting for transfers between devices: 7.36 us -> 5.61 us  [shift(): return lax.ppermute(x, ALL, pairs)]
  transfers between devices with their start and end apart: 19 -> 19, of which waited for: 8 -> 7; matrix products, arithmetic and copies ran while one was open for 3% -> 2% of each run, Pallas kernels for 28% -> 24%
where the time goes in v6:
time: 121 us; the launch traced here: 122 us
  starting transfers between devices  49.7 us (41%)
  Pallas kernels  34.2 us (28%)
  waiting for transfers between devices  24.6 us (20%)
  local copies, waits for them, and re-layouts  7.88 us (7%)
  between operations  3.82 us (3%)
  other arithmetic  1.37 us (1%)
    all_to_all x3, starting transfers between devices, exchange(): return lax.all_to_all(x, ALL, 0, 0, axis_index_groups=GROUPS)  24.1 us
    ppermute x12, starting transfers between devices, shift(): return lax.ppermute(x, ALL, pairs)  18.9 us
    pallas_call x2, Pallas kernels, attend(): pl.pallas_call(functools.partial(attend_kernel, part=part), out_shape=[ja...  18.3 us
    all_to_all x3, waiting for transfers between devices, exchange(): return lax.all_to_all(x, ALL, 0, 0, axis_index_groups=GROUPS)  16.1 us
    ppermute x4, starting transfers between devices, swap(): return lax.ppermute(x, 'core', [(0, 1), (1, 0)])  6.8 us
    unnamed x24, local copies, waits for them, and re-layouts  6.5 us
    ppermute x12, waiting for transfers between devices, shift(): return lax.ppermute(x, ALL, pairs)  5.61 us
    pallas_call x2, Pallas kernels, merge(): pl.pallas_call(merge_kernel, out_shape=jax.ShapeDtypeStruct((16, 56, WIDE...  3.7 us
  transfers between devices with their start and end apart: 19, of which 7 were waited for; matrix products, arithmetic and copies ran while one was open for 2% of the time, Pallas kernels for 24%

profile of v6, /device:TPU:1, one launch (start us, length us, event | category | flops | bytes accessed | tf_op | source)
XLA Modules:
  0.0 121.6 jit_solution(17518596774200832464)
XLA Ops:
  3.5 1.8 %collective-permute-done.theirs = bf16[24,512]{1,0:T(8,128)(2,1)S(1)} collective-permute-done((bf16[24,512]{1,0:T(8,128)(2,1)S(1)}, bf16[24,512]{1,0:T(8,128)(2,1)S(1)}, u32[]{:S(2)}, u32[]{:S(2)}) %collective-permute-start) | collective-permute-done | bytes 24608 | tf_op jit(solution)/shard_map/ppermute | solution.py:381
  5.9 1.8 %spread.1 = bf16[16,2,48,256]{3,2,1,0:T(8,128)(2,1)} custom-call(s32[4]{0:T(128)} %pad_add_fusion.me, bf16[24,1024]{1,0:T(8,128)(2,1)} %q.1, bf16[24,512]{1,0:T(8,128)(2,1)} %copy-done.8), custom_call_target="tpu_custom_call" | custom-call | tf_op jit(solution)/shard_map/spread/pallas_call | solution.py:35
  7.7 7.7 %all-to-all-start = ((bf16[16,2,48,256]{3,2,1,0:T(8,128)(2,1)}), bf16[16,2,48,256]{3,2,1,0:T(8,128)(2,1)S(1)}, u32[]{:S(2)}, u32[]{:S(2)}) async-start(bf16[16,2,48,256]{3,2,1,0:T(8,128)(2,1)} %spread.1), calls=%async_computation | async-start | bytes 1572864 | tf_op jit(solution)/shard_map/all_to_all | solution.py:407
  15.5 3.5 %turn.1 = (bf16[8,512,256]{2,1,0:T(8,128)(2,1)S(1)}, s32[2]{0:T(128)S(1)}) custom-call(s32[4]{0:T(128)S(1)} %copy-done.1, bf16[4,256,1024]{2,1,0:T(8,128)(2,1)S(1)} %copy-done, bf16[4,256,1024]{2,1,0:T(8,128)(2,1)} %collective-permute-done.1.v1, bf16[4,256,1024]{2,1,0:T(8,128)(2,1)} %collective-permute-done.2.k.refs_5_), custom_call_target="tpu_custom_call" | custom-call | flops 1000000 | bytes 8388608 | tf_op jit(solution)/shard_map/turn/pallas_call | solution.py:249
  24.5 2.5 %all-to-all-done = bf16[16,2,48,256]{3,2,1,0:T(8,128)(2,1)S(1)} async-done(((bf16[16,2,48,256]{3,2,1,0:T(8,128)(2,1)}), bf16[16,2,48,256]{3,2,1,0:T(8,128)(2,1)S(1)}, u32[]{:S(2)}, u32[]{:S(2)}) %all-to-all-start) | async-done | bytes 786464 | tf_op jit(solution)/shard_map/all_to_all | solution.py:407
  27.1 1.6 %collective-permute-start.3 = (bf16[16,48,256]{2,1,0:T(8,128)(2,1)S(1)}, bf16[16,48,256]{2,1,0:T(8,128)(2,1)S(1)}, u32[]{:S(2)}, u32[]{:S(2)}) collective-permute-start(bf16[16,48,256]{2,1,0:T(8,128)(2,1)S(1)} %get-tuple-element.30.refs_0_.refs_7_), channel_id=1, source_target_pairs={{0,1},{1,2},{2,3},{3,0},{4,5},{5,6},{6,7},{7,4},{8,9},{9,10},{10,1... | collective-permute-start | bytes 1179656 | tf_op jit(solution)/shard_map/ppermute | solution.py:390
  28.8 2.6 %collective-permute-start.4 = (bf16[16,48,256]{2,1,0:T(8,128)(2,1)S(1)}, bf16[16,48,256]{2,1,0:T(8,128)(2,1)S(1)}, u32[]{:S(2)}, u32[]{:S(2)}) collective-permute-start(bf16[16,48,256]{2,1,0:T(8,128)(2,1)S(1)} %get-tuple-element.30.refs_0_.refs_7_), channel_id=1, source_target_pairs={{0,2},{1,3},{2,0},{3,1},{4,6},{5,7},{6,4},{7,5},{8,10},{9,11},{10,... | collective-permute-start | bytes 1179656 | tf_op jit(solution)/shard_map/ppermute | solution.py:390
  37.1 4.0 %collective-permute-done.4.refs_2_ = bf16[16,48,256]{2,1,0:T(8,128)(2,1)S(1)} collective-permute-done((bf16[16,48,256]{2,1,0:T(8,128)(2,1)S(1)}, bf16[16,48,256]{2,1,0:T(8,128)(2,1)S(1)}, u32[]{:S(2)}, u32[]{:S(2)}) %collective-permute-start.4) | collective-permute-done | bytes 393248 | tf_op jit(solution)/shard_map/ppermute | solution.py:390
  44.2 9.1 %attend.2 = (bf16[16,56,256]{2,1,0:T(8,128)(2,1)S(1)}, bf16[16,56,256]{2,1,0:T(8,128)(2,1)S(1)}, bf16[16,56,256]{2,1,0:T(8,128)(2,1)S(1)}, bf16[16,56,256]{2,1,0:T(8,128)(2,1)S(1)}) custom-call(s32[4]{0:T(128)S(1)} %copy-done.1, s32[12,8]{1,0:T(8,128)S(1)} %convert_element_type.3.need, bf16[16,48,256]{2,1,0:T(8,128)(2,1)S(1)} %get-tuple-element.30.refs_0_.refs_7_, ...), custom_call_target="tpu_custom_call" | custom-call | flops 10000000000 | bytes 8388608 | tf_op jit(solution)/shard_map/attend/pallas_call | solution.py:199
  53.3 1.9 %collective-permute-start.6 = (bf16[16,56,256]{2,1,0:T(8,128)(2,1)S(1)}, bf16[16,56,256]{2,1,0:T(8,128)(2,1)S(1)}, u32[]{:S(2)}, u32[]{:S(2)}) collective-permute-start(bf16[16,56,256]{2,1,0:T(8,128)(2,1)S(1)} %get-tuple-element.20), channel_id=1, source_target_pairs={{0,3},{1,0},{2,1},{3,2},{4,7},{5,4},{6,5},{7,6},{8,11},{9,8},{10,9... | collective-permute-start | bytes 1376264 | tf_op jit(solution)/shard_map/ppermute | solution.py:390
  55.2 4.3 %collective-permute-start.7 = (bf16[16,56,256]{2,1,0:T(8,128)(2,1)S(1)}, bf16[16,56,256]{2,1,0:T(8,128)(2,1)S(1)}, u32[]{:S(2)}, u32[]{:S(2)}) collective-permute-start(bf16[16,56,256]{2,1,0:T(8,128)(2,1)S(1)} %get-tuple-element.21), channel_id=1, source_target_pairs={{0,2},{1,3},{2,0},{3,1},{4,6},{5,7},{6,4},{7,5},{8,10},{9,11},{10,... | collective-permute-start | bytes 1376264 | tf_op jit(solution)/shard_map/ppermute | solution.py:390
  59.6 9.3 %attend.3 = (bf16[16,56,256]{2,1,0:T(8,128)(2,1)S(1)}, bf16[16,56,256]{2,1,0:T(8,128)(2,1)S(1)}, bf16[16,56,256]{2,1,0:T(8,128)(2,1)S(1)}, bf16[16,56,256]{2,1,0:T(8,128)(2,1)S(1)}) custom-call(s32[4]{0:T(128)S(1)} %copy-done.1, s32[12,8]{1,0:T(8,128)S(1)} %convert_element_type.3.need, bf16[16,48,256]{2,1,0:T(8,128)(2,1)S(1)} %get-tuple-element.29.refs_0_, ...), custom_call_target="tpu_custom_call" | custom-call | flops 10000000000 | bytes 8388608 | tf_op jit(solution)/shard_map/attend/pallas_call | solution.py:199
  68.8 2.7 %collective-permute-start.12 = (bf16[16,56,256]{2,1,0:T(8,128)(2,1)S(1)}, bf16[16,56,256]{2,1,0:T(8,128)(2,1)S(1)}, u32[]{:S(2)}, u32[]{:S(2)}) collective-permute-start(bf16[16,56,256]{2,1,0:T(8,128)(2,1)S(1)} %get-tuple-element.24), channel_id=1, source_target_pairs={{0,3},{1,0},{2,1},{3,2},{4,7},{5,4},{6,5},{7,6},{8,11},{9,8},{10,9... | collective-permute-start | bytes 1376264 | tf_op jit(solution)/shard_map/ppermute | solution.py:390
  71.6 2.2 %collective-permute-start.13 = (bf16[16,56,256]{2,1,0:T(8,128)(2,1)S(1)}, bf16[16,56,256]{2,1,0:T(8,128)(2,1)S(1)}, u32[]{:S(2)}, u32[]{:S(2)}) collective-permute-start(bf16[16,56,256]{2,1,0:T(8,128)(2,1)S(1)} %get-tuple-element.25), channel_id=1, source_target_pairs={{0,2},{1,3},{2,0},{3,1},{4,6},{5,7},{6,4},{7,5},{8,10},{9,11},{10,... | collective-permute-start | bytes 1376264 | tf_op jit(solution)/shard_map/ppermute | solution.py:390
  73.8 1.9 %merge.2 = bf16[16,56,256]{2,1,0:T(8,128)(2,1)} custom-call(bf16[16,56,256]{2,1,0:T(8,128)(2,1)S(1)} %get-tuple-element.19.refs_7_.p0, bf16[16,56,256]{2,1,0:T(8,128)(2,1)S(1)} %collective-permute-done.6.p1, bf16[16,56,256]{2,1,0:T(8,128)(2,1)S(1)} %collective-permute-done.7.p2, bf16[16,56,256]{2,1,0:T(8,128)(2,1)S(1)} %collective-permute-done.8.p3, ...), custom_call_target="tpu_custom_call" | custom-call | tf_op jit(solution)/shard_map/merge/pallas_call | solution.py:304
  75.7 10.4 %all-to-all-start.1 = ((bf16[16,56,256]{2,1,0:T(8,128)(2,1)}), bf16[16,56,256]{2,1,0:T(8,128)(2,1)}, u32[]{:S(2)}, u32[]{:S(2)}) async-start(bf16[16,56,256]{2,1,0:T(8,128)(2,1)} %merge.2), calls=%async_computation.1 | async-start | bytes 917504 | tf_op jit(solution)/shard_map/all_to_all | solution.py:407
  86.1 1.8 %merge.3 = bf16[16,56,256]{2,1,0:T(8,128)(2,1)} custom-call(bf16[16,56,256]{2,1,0:T(8,128)(2,1)S(1)} %get-tuple-element.23.after.p0, bf16[16,56,256]{2,1,0:T(8,128)(2,1)S(1)} %collective-permute-done.12.p1, bf16[16,56,256]{2,1,0:T(8,128)(2,1)S(1)} %collective-permute-done.13.p2, bf16[16,56,256]{2,1,0:T(8,128)(2,1)S(1)} %collective-permute-done.14.p3, ...), custom_call_target="tpu_custom_call" | custom-call | tf_op jit(solution)/shard_map/merge/pallas_call | solution.py:304
  87.9 6.9 %all-to-all-done.1.got = bf16[16,56,256]{2,1,0:T(8,128)(2,1)} async-done(((bf16[16,56,256]{2,1,0:T(8,128)(2,1)}), bf16[16,56,256]{2,1,0:T(8,128)(2,1)}, u32[]{:S(2)}, u32[]{:S(2)}) %all-to-all-start.1) | async-done | bytes 458784 | tf_op jit(solution)/shard_map/all_to_all | solution.py:407
  94.9 6.0 %all-to-all-start.2 = ((bf16[16,56,256]{2,1,0:T(8,128)(2,1)}), bf16[16,56,256]{2,1,0:T(8,128)(2,1)S(1)}, u32[]{:S(2)}, u32[]{:S(2)}) async-start(bf16[16,56,256]{2,1,0:T(8,128)(2,1)} %merge.3), calls=%async_computation.2 | async-start | bytes 917504 | tf_op jit(solution)/shard_map/all_to_all | solution.py:407
  100.9 2.1 %first_close.1.ready = f32[48,256]{1,0:T(8,128)} custom-call(bf16[16,56,256]{2,1,0:T(8,128)(2,1)} %all-to-all-done.1.got), custom_call_target="tpu_custom_call" | custom-call | tf_op jit(solution)/shard_map/first_close/pallas_call | solution.py:329
  103.0 6.6 %all-to-all-done.2.got = bf16[16,56,256]{2,1,0:T(8,128)(2,1)S(1)} async-done(((bf16[16,56,256]{2,1,0:T(8,128)(2,1)}), bf16[16,56,256]{2,1,0:T(8,128)(2,1)S(1)}, u32[]{:S(2)}, u32[]{:S(2)}) %all-to-all-start.2) | async-done | bytes 458784 | tf_op jit(solution)/shard_map/all_to_all | solution.py:407
  110.4 2.1 %close.1 = (bf16[24,512]{1,0:T(8,128)(2,1)}, bf16[24,512]{1,0:T(8,128)(2,1)}) custom-call(s32[4]{0:T(128)} %pad_add_fusion.me, f32[48,256]{1,0:T(8,128)} %first_close.1.ready, bf16[16,56,256]{2,1,0:T(8,128)(2,1)} %copy-done.6), custom_call_target="tpu_custom_call" | custom-call | tf_op jit(solution)/shard_map/close/pallas_call | solution.py:349
  112.5 4.7 %collective-permute-start.15 = (bf16[24,512]{1,0:T(8,128)(2,1)}, bf16[24,512]{1,0:T(8,128)(2,1)S(1)}, u32[]{:S(2)}, u32[]{:S(2)}) collective-permute-start(bf16[24,512]{1,0:T(8,128)(2,1)} %get-tuple-element.28), channel_id=1, source_target_pairs={{0,16},{16,0},{1,17},{17,1},{2,18},{18,2},{3,19},{19,3},{4,20},{20... | collective-permute-start | bytes 73736 | tf_op jit(solution)/shard_map/ppermute | solution.py:381
  118.9 2.7 %project.1 = bf16[24,1024]{1,0:T(8,128)(2,1)} custom-call(s32[4]{0:T(128)} %pad_add_fusion.me, bf16[24,512]{1,0:T(8,128)(2,1)} %get-tuple-element.27.keep, bf16[24,512]{1,0:T(8,128)(2,1)} %copy-done.7, bf16[1024,1024]{1,0:T(8,128)(2,1)} %weight.1), custom_call_target="tpu_custom_call" | custom-call | tf_op jit(solution)/shard_map/project/pallas_call | solution.py:371
  (57 shorter events, 17.5 us)
Async XLA Ops:
  0.0 15.5 %copy-start = (bf16[4,256,1024]{2,1,0:T(8,128)(2,1)S(1)}, bf16[4,256,1024]{2,1,0:T(8,128)(2,1)}, u32[]{:S(2)}) copy-start(bf16[4,256,1024]{2,1,0:T(8,128)(2,1)} %v0.1) | copy-start | bytes 6291460
  0.0 15.5 %collective-permute-start.1 = (bf16[4,256,1024]{2,1,0:T(8,128)(2,1)}, bf16[4,256,1024]{2,1,0:T(8,128)(2,1)}, u32[]{:S(2)}, u32[]{:S(2)}) collective-permute-start(bf16[4,256,1024]{2,1,0:T(8,128)(2,1)} %v0.1), channel_id=1, source_target_pairs={{0,16},{16,0},{1,17},{17,1},{2,18},{18,2},{3,19},{19,3},{4,20},{20... | collective-permute-start | bytes 6291464 | tf_op jit(solution)/shard_map/ppermute | solution.py:381
  1.4 14.1 %collective-permute-start.2 = (bf16[4,256,1024]{2,1,0:T(8,128)(2,1)}, bf16[4,256,1024]{2,1,0:T(8,128)(2,1)}, u32[]{:S(2)}, u32[]{:S(2)}) collective-permute-start(bf16[4,256,1024]{2,1,0:T(8,128)(2,1)} %refs_4_.3), channel_id=1, source_target_pairs={{0,16},{16,0},{1,17},{17,1},{2,18},{18,2},{3,19},{19,3},{4,20},{20... | collective-permute-start | bytes 6291464 | tf_op jit(solution)/shard_map/ppermute | solution.py:381
  2.2 3.1 %collective-permute-start = (bf16[24,512]{1,0:T(8,128)(2,1)S(1)}, bf16[24,512]{1,0:T(8,128)(2,1)S(1)}, u32[]{:S(2)}, u32[]{:S(2)}) collective-permute-start(bf16[24,512]{1,0:T(8,128)(2,1)S(1)} %constant_dynamic-slice_fusion), channel_id=1, source_target_pairs={{0,16},{16,0},{1,17},{17,1},{2,18},{18,2},{3,19},{19,3},{4,20},{20... | collective-permute-start | bytes 73736 | tf_op jit(solution)/shard_map/ppermute | solution.py:381
  7.7 19.4 %all-to-all-start = ((bf16[16,2,48,256]{3,2,1,0:T(8,128)(2,1)}), bf16[16,2,48,256]{3,2,1,0:T(8,128)(2,1)S(1)}, u32[]{:S(2)}, u32[]{:S(2)}) async-start(bf16[16,2,48,256]{3,2,1,0:T(8,128)(2,1)} %spread.1), calls=%async_computation | async-start | bytes 1572864 | tf_op jit(solution)/shard_map/all_to_all | solution.py:407
  15.5 16.6 %copy-start.10 = (s32[512]{0:T(512)S(1)}, s32[512]{0:T(512)}, u32[]{:S(2)}) copy-start(s32[512]{0:T(512)} %param.10) | copy-start | bytes 6148
  15.5 16.8 %copy-start.11 = (s32[12]{0:T(128)S(1)}, s32[12]{0:T(128)}, u32[]{:S(2)}) copy-start(s32[12]{0:T(128)} %param.12) | copy-start | bytes 148
  15.5 16.9 %copy-start.9 = (s32[12,160]{1,0:T(8,128)S(1)}, s32[12,160]{1,0:T(8,128)}, u32[]{:S(2)}) copy-start(s32[12,160]{1,0:T(8,128)} %param.11) | copy-start | bytes 23044
  27.1 8.5 %collective-permute-start.3 = (bf16[16,48,256]{2,1,0:T(8,128)(2,1)S(1)}, bf16[16,48,256]{2,1,0:T(8,128)(2,1)S(1)}, u32[]{:S(2)}, u32[]{:S(2)}) collective-permute-start(bf16[16,48,256]{2,1,0:T(8,128)(2,1)S(1)} %get-tuple-element.30.refs_0_.refs_7_), channel_id=1, source_target_pairs={{0,1},{1,2},{2,3},{3,0},{4,5},{5,6},{6,7},{7,4},{8,9},{9,10},{10,1... | collective-permute-start | bytes 1179656 | tf_op jit(solution)/shard_map/ppermute | solution.py:390
  28.8 12.3 %collective-permute-start.4 = (bf16[16,48,256]{2,1,0:T(8,128)(2,1)S(1)}, bf16[16,48,256]{2,1,0:T(8,128)(2,1)S(1)}, u32[]{:S(2)}, u32[]{:S(2)}) collective-permute-start(bf16[16,48,256]{2,1,0:T(8,128)(2,1)S(1)} %get-tuple-element.30.refs_0_.refs_7_), channel_id=1, source_target_pairs={{0,2},{1,3},{2,0},{3,1},{4,6},{5,7},{6,4},{7,5},{8,10},{9,11},{10,... | collective-permute-start | bytes 1179656 | tf_op jit(solution)/shard_map/ppermute | solution.py:390
  31.3 9.7 %collective-permute-start.5 = (bf16[16,48,256]{2,1,0:T(8,128)(2,1)S(1)}, bf16[16,48,256]{2,1,0:T(8,128)(2,1)S(1)}, u32[]{:S(2)}, u32[]{:S(2)}) collective-permute-start(bf16[16,48,256]{2,1,0:T(8,128)(2,1)S(1)} %get-tuple-element.30.refs_0_.refs_7_), channel_id=1, source_target_pairs={{0,3},{1,0},{2,1},{3,2},{4,7},{5,4},{6,5},{7,6},{8,11},{9,8},{10,9... | collective-permute-start | bytes 1179656 | tf_op jit(solution)/shard_map/ppermute | solution.py:390
  32.7 26.8 %collective-permute-start.9 = (bf16[16,48,256]{2,1,0:T(8,128)(2,1)S(1)}, bf16[16,48,256]{2,1,0:T(8,128)(2,1)S(1)}, u32[]{:S(2)}, u32[]{:S(2)}) collective-permute-start(bf16[16,48,256]{2,1,0:T(8,128)(2,1)S(1)} %get-tuple-element.29.refs_0_), channel_id=1, source_target_pairs={{0,1},{1,2},{2,3},{3,0},{4,5},{5,6},{6,7},{7,4},{8,9},{9,10},{10,1... | collective-permute-start | bytes 1179656 | tf_op jit(solution)/shard_map/ppermute | solution.py:390
  33.5 26.0 %collective-permute-start.10 = (bf16[16,48,256]{2,1,0:T(8,128)(2,1)S(1)}, bf16[16,48,256]{2,1,0:T(8,128)(2,1)S(1)}, u32[]{:S(2)}, u32[]{:S(2)}) collective-permute-start(bf16[16,48,256]{2,1,0:T(8,128)(2,1)S(1)} %get-tuple-element.29.refs_0_), channel_id=1, source_target_pairs={{0,2},{1,3},{2,0},{3,1},{4,6},{5,7},{6,4},{7,5},{8,10},{9,11},{10,... | collective-permute-start | bytes 1179656 | tf_op jit(solution)/shard_map/ppermute | solution.py:390
  35.6 23.9 %collective-permute-start.11 = (bf16[16,48,256]{2,1,0:T(8,128)(2,1)S(1)}, bf16[16,48,256]{2,1,0:T(8,128)(2,1)S(1)}, u32[]{:S(2)}, u32[]{:S(2)}) collective-permute-start(bf16[16,48,256]{2,1,0:T(8,128)(2,1)S(1)} %get-tuple-element.29.refs_0_), channel_id=1, source_target_pairs={{0,3},{1,0},{2,1},{3,2},{4,7},{5,4},{6,5},{7,6},{8,11},{9,8},{10,9... | collective-permute-start | bytes 1179656 | tf_op jit(solution)/shard_map/ppermute | solution.py:390
  44.2 15.3 %copy-start.3 = (bf16[4,256,1024]{2,1,0:T(8,128)(2,1)S(1)}, bf16[4,256,1024]{2,1,0:T(8,128)(2,1)}, u32[]{:S(2)}) copy-start(bf16[4,256,1024]{2,1,0:T(8,128)(2,1)} %refs_4_.3) | copy-start | bytes 6291460
  53.3 20.5 %collective-permute-start.6 = (bf16[16,56,256]{2,1,0:T(8,128)(2,1)S(1)}, bf16[16,56,256]{2,1,0:T(8,128)(2,1)S(1)}, u32[]{:S(2)}, u32[]{:S(2)}) collective-permute-start(bf16[16,56,256]{2,1,0:T(8,128)(2,1)S(1)} %get-tuple-element.20), channel_id=1, source_target_pairs={{0,3},{1,0},{2,1},{3,2},{4,7},{5,4},{6,5},{7,6},{8,11},{9,8},{10,9... | collective-permute-start | bytes 1376264 | tf_op jit(solution)/shard_map/ppermute | solution.py:390
  55.2 18.6 %collective-permute-start.7 = (bf16[16,56,256]{2,1,0:T(8,128)(2,1)S(1)}, bf16[16,56,256]{2,1,0:T(8,128)(2,1)S(1)}, u32[]{:S(2)}, u32[]{:S(2)}) collective-permute-start(bf16[16,56,256]{2,1,0:T(8,128)(2,1)S(1)} %get-tuple-element.21), channel_id=1, source_target_pairs={{0,2},{1,3},{2,0},{3,1},{4,6},{5,7},{6,4},{7,5},{8,10},{9,11},{10,... | collective-permute-start | bytes 1376264 | tf_op jit(solution)/shard_map/ppermute | solution.py:390
  59.5 14.3 %collective-permute-start.8 = (bf16[16,56,256]{2,1,0:T(8,128)(2,1)S(1)}, bf16[16,56,256]{2,1,0:T(8,128)(2,1)S(1)}, u32[]{:S(2)}, u32[]{:S(2)}) collective-permute-start(bf16[16,56,256]{2,1,0:T(8,128)(2,1)S(1)} %get-tuple-element.22), channel_id=1, source_target_pairs={{0,1},{1,2},{2,3},{3,0},{4,5},{5,6},{6,7},{7,4},{8,9},{9,10},{10,1... | collective-permute-start | bytes 1376264 | tf_op jit(solution)/shard_map/ppermute | solution.py:390
  68.8 17.2 %collective-permute-start.12 = (bf16[16,56,256]{2,1,0:T(8,128)(2,1)S(1)}, bf16[16,56,256]{2,1,0:T(8,128)(2,1)S(1)}, u32[]{:S(2)}, u32[]{:S(2)}) collective-permute-start(bf16[16,56,256]{2,1,0:T(8,128)(2,1)S(1)} %get-tuple-element.24), channel_id=1, source_target_pairs={{0,3},{1,0},{2,1},{3,2},{4,7},{5,4},{6,5},{7,6},{8,11},{9,8},{10,9... | collective-permute-start | bytes 1376264 | tf_op jit(solution)/shard_map/ppermute | solution.py:390
  71.6 14.5 %collective-permute-start.13 = (bf16[16,56,256]{2,1,0:T(8,128)(2,1)S(1)}, bf16[16,56,256]{2,1,0:T(8,128)(2,1)S(1)}, u32[]{:S(2)}, u32[]{:S(2)}) collective-permute-start(bf16[16,56,256]{2,1,0:T(8,128)(2,1)S(1)} %get-tuple-element.25), channel_id=1, source_target_pairs={{0,2},{1,3},{2,0},{3,1},{4,6},{5,7},{6,4},{7,5},{8,10},{9,11},{10,... | collective-permute-start | bytes 1376264 | tf_op jit(solution)/shard_map/ppermute | solution.py:390
  73.8 12.3 %collective-permute-start.14 = (bf16[16,56,256]{2,1,0:T(8,128)(2,1)S(1)}, bf16[16,56,256]{2,1,0:T(8,128)(2,1)S(1)}, u32[]{:S(2)}, u32[]{:S(2)}) collective-permute-start(bf16[16,56,256]{2,1,0:T(8,128)(2,1)S(1)} %get-tuple-element.26), channel_id=1, source_target_pairs={{0,1},{1,2},{2,3},{3,0},{4,5},{5,6},{6,7},{7,4},{8,9},{9,10},{10,1... | collective-permute-start | bytes 1376264 | tf_op jit(solution)/shard_map/ppermute | solution.py:390
  75.7 19.2 %all-to-all-start.1 = ((bf16[16,56,256]{2,1,0:T(8,128)(2,1)}), bf16[16,56,256]{2,1,0:T(8,128)(2,1)}, u32[]{:S(2)}, u32[]{:S(2)}) async-start(bf16[16,56,256]{2,1,0:T(8,128)(2,1)} %merge.2), calls=%async_computation.1 | async-start | bytes 917504 | tf_op jit(solution)/shard_map/all_to_all | solution.py:407
  94.9 14.7 %all-to-all-start.2 = ((bf16[16,56,256]{2,1,0:T(8,128)(2,1)}), bf16[16,56,256]{2,1,0:T(8,128)(2,1)S(1)}, u32[]{:S(2)}, u32[]{:S(2)}) async-start(bf16[16,56,256]{2,1,0:T(8,128)(2,1)} %merge.3), calls=%async_computation.2 | async-start | bytes 917504 | tf_op jit(solution)/shard_map/all_to_all | solution.py:407
  112.5 5.8 %collective-permute-start.15 = (bf16[24,512]{1,0:T(8,128)(2,1)}, bf16[24,512]{1,0:T(8,128)(2,1)S(1)}, u32[]{:S(2)}, u32[]{:S(2)}) collective-permute-start(bf16[24,512]{1,0:T(8,128)(2,1)} %get-tuple-element.28), channel_id=1, source_target_pairs={{0,16},{16,0},{1,17},{17,1},{2,18},{18,2},{3,19},{19,3},{4,20},{20... | collective-permute-start | bytes 73736 | tf_op jit(solution)/shard_map/ppermute | solution.py:381
  (7 other events, 18.5 us)

commit v7 on v6

--- a/solution.py
+++ b/solution.py
@@ -44,17 +44,15 @@
 def attend_kernel(
     me, need, *refs, part,
 ):
-    qs, (k0, k1, v0, _), outs = refs[:4], refs[4:8], refs[8:12]
-    cnt, plan, qv, k, vt, qm, acc, sb, top, shrink, yb, sem = refs[12:]
+    qs, (k0, v0, _), outs = refs[:4], refs[4:7], refs[7:11]
+    cnt, plan, qv, k, vt, qm, acc, sb, top, shrink, yb, sem = refs[11:]
     my_y, my_core, my_x = me[0], me[1], me[3]
-    col = pl.multiple_of(my_core * 512 + part * WIDE, WIDE)
     copies = [
         pltpu.make_async_copy(src, dst, sem.at[i])
         for i, (src, dst) in enumerate(
             [(q, qv.at[pl.ds(i * q.shape[0], q.shape[0])]) for i, q in enumerate(qs)]
             + [
-                (k0.at[:, :, pl.ds(col, WIDE)], k.at[pl.ds(0, 4)]),
-                (k1.at[:, :, pl.ds(col, WIDE)], k.at[pl.ds(4, 4)]),
+                (k0.at[:, :, pl.ds(part * WIDE, WIDE)], k),
                 (v0.at[:, pl.ds(part * WIDE, WIDE), :], vt),
             ]
         )
@@ -101,19 +99,28 @@
         rows = pl.ds(pl.multiple_of(qi * 256, 256), 256)
         zero = jnp.zeros((64, 256), BF16)
         for hp in range(NH // 2):
-            turned = yb[rows, hp * 128:(hp + 1) * 128].T.astype(BF16)
+            turned = yb[rows, hp * 128:(hp + 1) * 128].astype(BF16).T
             qm[qi, 2 * hp] = jnp.concatenate([turned[:64], zero], axis=0)
             qm[qi, 2 * hp + 1] = jnp.concatenate([zero, turned[64:]], axis=0)
-
+        return 0
+
+    def turns(u, _):
+        for i in range(3):
+            turn(u * 3 + i, 0)
+        return 0
+
+    lax.fori_loop(0, 4, turns, 0)
+    def blank(qi, _):
         @pl.when(cnt[qi] == 0)
         def _():
+            rows = pl.ds(pl.multiple_of(qi * 256, 256), 256)
             yb[rows, :WIDE] = jnp.zeros((256, WIDE), F32)
             lane = lax.broadcasted_iota(jnp.int32, (256, 128), 1)
             yb[rows, WIDE:] = jnp.where(lane < NH, NO_TOP, 0.0)
 
         return 0
 
-    lax.fori_loop(0, 12, turn, 0)
+    lax.fori_loop(0, 12, blank, 0)
     for copy in copies[4:]:
         copy.wait()
     acc[...] = jnp.zeros_like(acc)
@@ -154,8 +161,8 @@
             extra = [tops, hi, totals - hi, jnp.zeros((128 - 3 * NH, 256), F32)]
             for hp in range(NH // 2):
                 both = jnp.concatenate([acc[at, 2 * hp, :64, :], acc[at, 2 * hp + 1, :64, :]], axis=0)
-                yb[rows, hp * 128:(hp + 1) * 128] = both.T
-            yb[rows, WIDE:] = jnp.concatenate(extra, axis=0).T
+                yb[rows, hp * 128:(hp + 1) * 128] = both.astype(BF16).T.astype(F32)
+            yb[rows, WIDE:] = jnp.concatenate(extra, axis=0).astype(BF16).T.astype(F32)
 
     old = jnp.full((NH, 256), NO_TOP, F32)
     for p in range(4):
@@ -192,14 +199,14 @@
             o[b] = jnp.concatenate(data, axis=0).astype(BF16)
 
 
-def attend(me, need, q, k0, k1, v0, after, part):
+def attend(me, need, q, k0, v0, after, part):
     vmem = pl.BlockSpec(memory_space=pltpu.VMEM)
     smem = pl.BlockSpec(memory_space=pltpu.SMEM)
     whole = pl.BlockSpec(memory_space=pl.ANY)
     return pl.pallas_call(
         functools.partial(attend_kernel, part=part),
         out_shape=[jax.ShapeDtypeStruct((16, 56, WIDE), BF16)] * 4,
-        in_specs=[smem] * 2 + [whole] * 8,
+        in_specs=[smem] * 2 + [whole] * 7,
         out_specs=[vmem] * 4,
         scratch_shapes=[
             pltpu.SMEM((12,), jnp.int32),
@@ -213,25 +220,25 @@
             pltpu.VMEM((4, NH, 256), F32),
             pltpu.VMEM((4, NH, 256), F32),
             pltpu.VMEM((3072, WIDE + 128), F32),
-            pltpu.SemaphoreType.DMA((7,)),
+            pltpu.SemaphoreType.DMA((6,)),
         ],
         compiler_params=pltpu.CompilerParams(vmem_limit_bytes=24 * 2**20),
         cost_estimate=pl.CostEstimate(flops=10**10, bytes_accessed=2**23, transcendentals=2 * 10**7),
         name="attend",
-    )(me, need, *q, k0, k1, v0, after)
-
-
-def turn_kernel(me, v0, v1, k, out, parts, held, sem):
+    )(me, need, *q, k0, v0, after)
+
+
+def turn_kernel(me, v0, v1, k0, k1, out, keys, parts, held, sem):
     parts[0] = 0
     parts[1] = 1
     col = pl.multiple_of(me[1] * 512, 512)
     copies = [
-        pltpu.make_async_copy(v.at[:, :, pl.ds(col, 512)], held.at[pl.ds(i * 4, 4)], sem.at[i])
-        for i, v in enumerate((v0, v1))
+        pltpu.make_async_copy(src.at[:, :, pl.ds(col, 512)], dst.at[pl.ds(i % 2 * 4, 4)], sem.at[i])
+        for i, (src, dst) in enumerate([(v0, held), (v1, held), (k0, keys), (k1, keys)])
     ]
     for copy in copies:
         copy.start()
-    for copy in copies:
+    for copy in copies[:2]:
         copy.wait()
 
     def one(j, _):
@@ -240,22 +247,28 @@
         return 0
 
     lax.fori_loop(0, 8, one, 0)
-
-
-def turn_values(me, v0, v1, k):
+    for copy in copies[2:]:
+        copy.wait()
+
+
+def turn_values(me, v0, v1, k0, k1):
     vmem = pl.BlockSpec(memory_space=pltpu.VMEM)
     smem = pl.BlockSpec(memory_space=pltpu.SMEM)
     whole = pl.BlockSpec(memory_space=pl.ANY)
     return pl.pallas_call(
         turn_kernel,
-        out_shape=[jax.ShapeDtypeStruct((8, 512, 256), BF16), jax.ShapeDtypeStruct((2,), jnp.int32)],
-        in_specs=[smem] + [whole] * 3,
-        out_specs=[vmem, smem],
-        scratch_shapes=[pltpu.VMEM((8, 256, 512), BF16), pltpu.SemaphoreType.DMA((2,))],
+        out_shape=[
+            jax.ShapeDtypeStruct((8, 512, 256), BF16),
+            jax.ShapeDtypeStruct((8, 256, 512), BF16),
+            jax.ShapeDtypeStruct((2,), jnp.int32),
+        ],
+        in_specs=[smem] + [whole] * 4,
+        out_specs=[vmem, vmem, smem],
+        scratch_shapes=[pltpu.VMEM((8, 256, 512), BF16), pltpu.SemaphoreType.DMA((4,))],
         cost_estimate=pl.CostEstimate(flops=10**6, bytes_accessed=2**23, transcendentals=0),
         compiler_params=pltpu.CompilerParams(vmem_limit_bytes=16 * 2**20),
         name="turn",
-    )(me, v0, v1, k)
+    )(me, v0, v1, k0, k1)
 
 
 def add_up(data, tails, spread):
@@ -356,27 +369,6 @@
     )(me, ready, got)
 
 
-def project_kernel(me, keep, give, weight, out):
-    first = me[1] == 0
-    mine, other = keep[...].astype(F32), give[...].astype(F32)
-    left = jnp.where(first, mine, other).astype(BF16)
-    right = jnp.where(first, other, mine).astype(BF16)
-    total = jnp.dot(left, weight[:512], preferred_element_type=F32)
-    out[...] = (total + jnp.dot(right, weight[512:], preferred_element_type=F32)).astype(BF16)
-
-
-def project(me, keep, give, weight):
-    vmem = pl.BlockSpec(memory_space=pltpu.VMEM)
-    smem = pl.BlockSpec(memory_space=pltpu.SMEM)
-    return pl.pallas_call(
-        project_kernel,
-        out_shape=jax.ShapeDtypeStruct((24, 1024), BF16),
-        in_specs=[smem] + [vmem] * 3,
-        out_specs=vmem,
-        name="project",
-    )(me, keep, give, weight)
-
-
 def swap(x):
     return lax.ppermute(x, "core", [(0, 1), (1, 0)])
 
@@ -421,7 +413,7 @@
     me = jnp.stack([lax.axis_index(a) for a in ALL]).astype(jnp.int32)
     plane = exchange(spread_rows(me, queries, theirs))
     k_theirs, v_theirs = swap(keys), swap(values)
-    v_turned, parts = turn_values(me, values, v_theirs, k_theirs)
+    v_turned, k_half, parts = turn_values(me, values, v_theirs, keys, k_theirs)
     q_parts = [ring(lax.dynamic_index_in_dim(plane, parts[c], 1, False), "xy") for c in range(2)]
 
     four = jnp.arange(4, dtype=jnp.int32)
@@ -432,13 +424,15 @@
     need = jnp.any((covisible[:, None, :] == local[None, :, None]) & used[:, None, :], axis=2)
     need = need.astype(jnp.int32)
 
-    early = attend(me, need, q_parts[0], keys, k_theirs, v_turned, q_parts[0][0], 0)
-    late = attend(me, need, q_parts[1], keys, k_theirs, v_turned, early[0], 1)
+    early = attend(me, need, q_parts[0], k_half, v_turned, q_parts[0][0], 0)
+    late = attend(me, need, q_parts[1], k_half, v_turned, early[0], 1)
     early = exchange(merge(deliver(early, "xy"), late[0]))
     late = exchange(merge(deliver(late, "xy"), late[0]))
     keep, give = close(me, first_close(early), late)
     give = swap(give)
-    return project(me, keep, give, out_weight)
+    first = core == 0
+    rows = jnp.concatenate([jnp.where(first, keep, give), jnp.where(first, give, keep)], axis=1)
+    return jnp.dot(rows, out_weight, preferred_element_type=F32).astype(BF16)
 
 
 def solution(mesh):

time: 121 us -> 124 us (1.025); the launches traced: 122 us -> 122 us
  starting transfers between devices: 49.7 us -> 38.9 us
  Pallas kernels: 34.2 us -> 40.8 us
  local copies, waits for them, and re-layouts: 7.88 us -> 11.8 us
    pallas_call x2, Pallas kernels: 18.3 us -> 26.4 us  [attend(): pl.pallas_call(functools.partial(attend_kernel, part=part), out_shape=[ja...]
    ppermute x12, starting transfers between devices: 18.9 us -> 11.7 us  [shift(): return lax.ppermute(x, ALL, pairs)]
    all_to_all x3, starting transfers between devices: 24.1 us -> 18.9 us  [exchange(): return lax.all_to_all(x, ALL, 0, 0, axis_index_groups=GROUPS)]
    all_to_all x3, waiting for transfers between devices: 16.1 us -> 11.1 us  [exchange(): return lax.all_to_all(x, ALL, 0, 0, axis_index_groups=GROUPS)]
    unnamed x24 -> x26, local copies, waits for them, and re-layouts: 6.5 us -> 10.4 us
    ppermute x12, waiting for transfers between devices: 5.61 us -> 9.3 us  [shift(): return lax.ppermute(x, ALL, pairs)]
    pallas_call x1 -> x0, Pallas kernels: 2.72 us -> none  [project(): pl.pallas_call(project_kernel, out_shape=jax.ShapeDtypeStruct((24, 1024),...]
    ppermute x4, starting transfers between devices: 6.8 us -> 8.39 us  [swap(): return lax.ppermute(x, 'core', [(0, 1), (1, 0)])]
  transfers between devices with their start and end apart: 19 -> 19, of which waited for: 7 -> 7; matrix products, arithmetic and copies ran while one was open for 2% -> 2% of each run, Pallas kernels for 24% -> 32%
where the time goes in v7:
time: 124 us; the launch traced here: 122 us
  Pallas kernels  40.8 us (33%)
  starting transfers between devices  38.9 us (31%)
  waiting for transfers between devices  23.4 us (19%)
  local copies, waits for them, and re-layouts  11.8 us (10%)
  between operations  4.19 us (3%)
  other arithmetic  2.04 us (2%)
    pallas_call x2, Pallas kernels, attend(): pl.pallas_call(functools.partial(attend_kernel, part=part), out_shape=[ja...  26.4 us
    all_to_all x3, starting transfers between devices, exchange(): return lax.all_to_all(x, ALL, 0, 0, axis_index_groups=GROUPS)  18.9 us
    ppermute x12, starting transfers between devices, shift(): return lax.ppermute(x, ALL, pairs)  11.7 us
    all_to_all x3, waiting for transfers between devices, exchange(): return lax.all_to_all(x, ALL, 0, 0, axis_index_groups=GROUPS)  11.1 us
    unnamed x26, local copies, waits for them, and re-layouts  10.4 us
    ppermute x12, waiting for transfers between devices, shift(): return lax.ppermute(x, ALL, pairs)  9.3 us
    ppermute x4, starting transfers between devices, swap(): return lax.ppermute(x, 'core', [(0, 1), (1, 0)])  8.39 us
    pallas_call x2, Pallas kernels, merge(): pl.pallas_call(merge_kernel, out_shape=jax.ShapeDtypeStruct((16, 56, WIDE...  4.75 us
  transfers between devices with their start and end apart: 19, of which 7 were waited for; matrix products, arithmetic and copies ran while one was open for 2% of the time, Pallas kernels for 32%

profile of v7, /device:TPU:1, one launch (start us, length us, event | category | flops | bytes accessed | tf_op | source)
XLA Modules:
  0.0 122.2 jit_solution(14614953787639357720)
XLA Ops:
  3.4 1.9 %collective-permute-done.theirs = bf16[24,512]{1,0:T(8,128)(2,1)S(1)} collective-permute-done((bf16[24,512]{1,0:T(8,128)(2,1)S(1)}, bf16[24,512]{1,0:T(8,128)(2,1)S(1)}, u32[]{:S(2)}, u32[]{:S(2)}) %collective-permute-start) | collective-permute-done | bytes 24608 | tf_op jit(solution)/shard_map/ppermute | solution.py:373
  5.9 1.8 %spread.1 = bf16[16,2,48,256]{3,2,1,0:T(8,128)(2,1)} custom-call(s32[4]{0:T(128)} %pad_add_fusion.me, bf16[24,1024]{1,0:T(8,128)(2,1)} %q.1, bf16[24,512]{1,0:T(8,128)(2,1)} %copy-done.9), custom_call_target="tpu_custom_call" | custom-call | tf_op jit(solution)/shard_map/spread/pallas_call | solution.py:35
  7.7 7.7 %all-to-all-start = ((bf16[16,2,48,256]{3,2,1,0:T(8,128)(2,1)}), bf16[16,2,48,256]{3,2,1,0:T(8,128)(2,1)S(1)}, u32[]{:S(2)}, u32[]{:S(2)}) async-start(bf16[16,2,48,256]{3,2,1,0:T(8,128)(2,1)} %spread.1), calls=%async_computation | async-start | bytes 1572864 | tf_op jit(solution)/shard_map/all_to_all | solution.py:399
  15.5 1.6 %copy-done.1 = bf16[4,256,1024]{2,1,0:T(8,128)(2,1)S(1)} copy-done((bf16[4,256,1024]{2,1,0:T(8,128)(2,1)S(1)}, bf16[4,256,1024]{2,1,0:T(8,128)(2,1)}, u32[]{:S(2)}) %copy-start.1) | copy-done | bytes 2097176
  17.1 1.6 %copy-done.2 = bf16[4,256,1024]{2,1,0:T(8,128)(2,1)S(1)} copy-done((bf16[4,256,1024]{2,1,0:T(8,128)(2,1)S(1)}, bf16[4,256,1024]{2,1,0:T(8,128)(2,1)}, u32[]{:S(2)}) %copy-start.2) | copy-done | bytes 2097176
  18.7 3.6 %turn.1 = (bf16[8,512,256]{2,1,0:T(8,128)(2,1)S(1)}, bf16[8,256,512]{2,1,0:T(8,128)(2,1)S(1)}, s32[2]{0:T(128)S(1)}) custom-call(s32[4]{0:T(128)S(1)} %copy-done.3, bf16[4,256,1024]{2,1,0:T(8,128)(2,1)S(1)} %copy-done.1, bf16[4,256,1024]{2,1,0:T(8,128)(2,1)} %collective-permute-done.1.v1, bf16[4,256,1024]{2,1,0:T(8,128)(2,1)S(1)} %copy-done.2, ...), custom_call_target="tpu_custom_call" | custom-call | flops 1000000 | bytes 8388608 | tf_op jit(solution)/shard_map/turn/pallas_call | solution.py:258
  31.1 2.6 %collective-permute-start.4 = (bf16[16,48,256]{2,1,0:T(8,128)(2,1)S(1)}, bf16[16,48,256]{2,1,0:T(8,128)(2,1)S(1)}, u32[]{:S(2)}, u32[]{:S(2)}) collective-permute-start(bf16[16,48,256]{2,1,0:T(8,128)(2,1)S(1)} %get-tuple-element.32.refs_0_.refs_6_), channel_id=1, source_target_pairs={{0,2},{1,3},{2,0},{3,1},{4,6},{5,7},{6,4},{7,5},{8,10},{9,11},{10,... | collective-permute-start | bytes 1179656 | tf_op jit(solution)/shard_map/ppermute | solution.py:382
  38.0 1.5 %collective-permute-start.11 = (bf16[16,48,256]{2,1,0:T(8,128)(2,1)S(1)}, bf16[16,48,256]{2,1,0:T(8,128)(2,1)S(1)}, u32[]{:S(2)}, u32[]{:S(2)}) collective-permute-start(bf16[16,48,256]{2,1,0:T(8,128)(2,1)S(1)} %get-tuple-element.31.refs_0_), channel_id=1, source_target_pairs={{0,3},{1,0},{2,1},{3,2},{4,7},{5,4},{6,5},{7,6},{8,11},{9,8},{10,9... | collective-permute-start | bytes 1179656 | tf_op jit(solution)/shard_map/ppermute | solution.py:382
  39.4 4.0 %collective-permute-done.4.refs_2_ = bf16[16,48,256]{2,1,0:T(8,128)(2,1)S(1)} collective-permute-done((bf16[16,48,256]{2,1,0:T(8,128)(2,1)S(1)}, bf16[16,48,256]{2,1,0:T(8,128)(2,1)S(1)}, u32[]{:S(2)}, u32[]{:S(2)}) %collective-permute-start.4) | collective-permute-done | bytes 393248 | tf_op jit(solution)/shard_map/ppermute | solution.py:382
  43.4 1.6 %copy-done.5 = bf16[8,512,256]{2,1,0:T(8,128)(2,1)S(1)} copy-done((bf16[8,512,256]{2,1,0:T(8,128)(2,1)S(1)}, bf16[8,512,256]{2,1,0:T(8,128)(2,1)}, u32[]{:S(2)}) %copy-start.5) | copy-done | bytes 2097176
  45.0 1.6 %copy-done.7 = bf16[8,256,512]{2,1,0:T(8,128)(2,1)S(1)} copy-done((bf16[8,256,512]{2,1,0:T(8,128)(2,1)S(1)}, bf16[8,256,512]{2,1,0:T(8,128)(2,1)}, u32[]{:S(2)}) %copy-start.7) | copy-done | bytes 2097176
  46.6 12.6 %attend.2 = (bf16[16,56,256]{2,1,0:T(8,128)(2,1)S(1)}, bf16[16,56,256]{2,1,0:T(8,128)(2,1)S(1)}, bf16[16,56,256]{2,1,0:T(8,128)(2,1)S(1)}, bf16[16,56,256]{2,1,0:T(8,128)(2,1)S(1)}) custom-call(s32[4]{0:T(128)S(1)} %copy-done.3, s32[12,8]{1,0:T(8,128)S(1)} %convert_element_type.6.need, bf16[16,48,256]{2,1,0:T(8,128)(2,1)S(1)} %get-tuple-element.32.refs_0_.refs_6_, ...), custom_call_target="tpu_custom_call" | custom-call | flops 10000000000 | bytes 8388608 | tf_op jit(solution)/shard_map/attend/pallas_call | solution.py:206
  60.8 13.8 %attend.3 = (bf16[16,56,256]{2,1,0:T(8,128)(2,1)S(1)}, bf16[16,56,256]{2,1,0:T(8,128)(2,1)}, bf16[16,56,256]{2,1,0:T(8,128)(2,1)}, bf16[16,56,256]{2,1,0:T(8,128)(2,1)}) custom-call(s32[4]{0:T(128)S(1)} %copy-done.3, s32[12,8]{1,0:T(8,128)S(1)} %convert_element_type.6.need, bf16[16,48,256]{2,1,0:T(8,128)(2,1)S(1)} %get-tuple-element.31.refs_0_, ...), custom_call_target="tpu_custom_call" | custom-call | flops 10000000000 | bytes 8388608 | tf_op jit(solution)/shard_map/attend/pallas_call | solution.py:206
  74.7 1.5 %collective-permute-start.13 = (bf16[16,56,256]{2,1,0:T(8,128)(2,1)}, bf16[16,56,256]{2,1,0:T(8,128)(2,1)S(1)}, u32[]{:S(2)}, u32[]{:S(2)}) collective-permute-start(bf16[16,56,256]{2,1,0:T(8,128)(2,1)} %get-tuple-element.27), channel_id=1, source_target_pairs={{0,2},{1,3},{2,0},{3,1},{4,6},{5,7},{6,4},{7,5},{8,10},{9,11},{10,... | collective-permute-start | bytes 1376264 | tf_op jit(solution)/shard_map/ppermute | solution.py:382
  77.0 1.9 %merge.2 = bf16[16,56,256]{2,1,0:T(8,128)(2,1)} custom-call(bf16[16,56,256]{2,1,0:T(8,128)(2,1)S(1)} %get-tuple-element.21.refs_6_.p0, bf16[16,56,256]{2,1,0:T(8,128)(2,1)S(1)} %collective-permute-done.6.p1, bf16[16,56,256]{2,1,0:T(8,128)(2,1)S(1)} %collective-permute-done.7.p2, bf16[16,56,256]{2,1,0:T(8,128)(2,1)S(1)} %collective-permute-done.8.p3, ...), custom_call_target="tpu_custom_call" | custom-call | tf_op jit(solution)/shard_map/merge/pallas_call | solution.py:317
  78.9 6.2 %all-to-all-start.1 = ((bf16[16,56,256]{2,1,0:T(8,128)(2,1)}), bf16[16,56,256]{2,1,0:T(8,128)(2,1)}, u32[]{:S(2)}, u32[]{:S(2)}) async-start(bf16[16,56,256]{2,1,0:T(8,128)(2,1)} %merge.2), calls=%async_computation.1 | async-start | bytes 917504 | tf_op jit(solution)/shard_map/all_to_all | solution.py:399
  85.1 4.0 %collective-permute-done.14.p3 = bf16[16,56,256]{2,1,0:T(8,128)(2,1)} collective-permute-done((bf16[16,56,256]{2,1,0:T(8,128)(2,1)}, bf16[16,56,256]{2,1,0:T(8,128)(2,1)}, u32[]{:S(2)}, u32[]{:S(2)}) %collective-permute-start.14) | collective-permute-done | bytes 458784 | tf_op jit(solution)/shard_map/ppermute | solution.py:382
  89.1 2.9 %merge.3 = bf16[16,56,256]{2,1,0:T(8,128)(2,1)} custom-call(bf16[16,56,256]{2,1,0:T(8,128)(2,1)S(1)} %get-tuple-element.25.after.p0, bf16[16,56,256]{2,1,0:T(8,128)(2,1)S(1)} %collective-permute-done.12.p1, bf16[16,56,256]{2,1,0:T(8,128)(2,1)S(1)} %collective-permute-done.13.p2, bf16[16,56,256]{2,1,0:T(8,128)(2,1)} %collective-permute-done.14.p3, ...), custom_call_target="tpu_custom_call" | custom-call | tf_op jit(solution)/shard_map/merge/pallas_call | solution.py:317
  92.0 4.6 %all-to-all-done.1.got = bf16[16,56,256]{2,1,0:T(8,128)(2,1)} async-done(((bf16[16,56,256]{2,1,0:T(8,128)(2,1)}), bf16[16,56,256]{2,1,0:T(8,128)(2,1)}, u32[]{:S(2)}, u32[]{:S(2)}) %all-to-all-start.1) | async-done | bytes 458784 | tf_op jit(solution)/shard_map/all_to_all | solution.py:399
  96.6 4.9 %all-to-all-start.2 = ((bf16[16,56,256]{2,1,0:T(8,128)(2,1)}), bf16[16,56,256]{2,1,0:T(8,128)(2,1)S(1)}, u32[]{:S(2)}, u32[]{:S(2)}) async-start(bf16[16,56,256]{2,1,0:T(8,128)(2,1)} %merge.3), calls=%async_computation.2 | async-start | bytes 917504 | tf_op jit(solution)/shard_map/all_to_all | solution.py:399
  101.5 2.1 %first_close.1.ready = f32[48,256]{1,0:T(8,128)} custom-call(bf16[16,56,256]{2,1,0:T(8,128)(2,1)} %all-to-all-done.1.got), custom_call_target="tpu_custom_call" | custom-call | tf_op jit(solution)/shard_map/first_close/pallas_call | solution.py:342
  103.6 6.5 %all-to-all-done.2.got = bf16[16,56,256]{2,1,0:T(8,128)(2,1)S(1)} async-done(((bf16[16,56,256]{2,1,0:T(8,128)(2,1)}), bf16[16,56,256]{2,1,0:T(8,128)(2,1)S(1)}, u32[]{:S(2)}, u32[]{:S(2)}) %all-to-all-start.2) | async-done | bytes 458784 | tf_op jit(solution)/shard_map/all_to_all | solution.py:399
  110.9 2.1 %close.1 = (bf16[24,512]{1,0:T(8,128)(2,1)}, bf16[24,512]{1,0:T(8,128)(2,1)}) custom-call(s32[4]{0:T(128)} %pad_add_fusion.me, f32[48,256]{1,0:T(8,128)} %first_close.1.ready, bf16[16,56,256]{2,1,0:T(8,128)(2,1)} %copy-done.8), custom_call_target="tpu_custom_call" | custom-call | tf_op jit(solution)/shard_map/close/pallas_call | solution.py:362
  113.0 6.3 %collective-permute-start.15 = (bf16[24,512]{1,0:T(8,128)(2,1)}, bf16[24,512]{1,0:T(8,128)(2,1)S(1)}, u32[]{:S(2)}, u32[]{:S(2)}) collective-permute-start(bf16[24,512]{1,0:T(8,128)(2,1)} %get-tuple-element.30), channel_id=1, source_target_pairs={{0,16},{16,0},{1,17},{17,1},{2,18},{18,2},{3,19},{19,3},{4,20},{20... | collective-permute-start | bytes 73736 | tf_op jit(solution)/shard_map/ppermute | solution.py:373
  (60 shorter events, 19.1 us)
Async XLA Ops:
  0.0 121.2 %copy-start = (bf16[1024,1024]{1,0:T(8,128)(2,1)S(1)}, bf16[1024,1024]{1,0:T(8,128)(2,1)}, u32[]{:S(2)}) copy-start(bf16[1024,1024]{1,0:T(8,128)(2,1)} %param.13) | copy-start | bytes 6291460
  0.0 15.5 %collective-permute-start.1 = (bf16[4,256,1024]{2,1,0:T(8,128)(2,1)}, bf16[4,256,1024]{2,1,0:T(8,128)(2,1)}, u32[]{:S(2)}, u32[]{:S(2)}) collective-permute-start(bf16[4,256,1024]{2,1,0:T(8,128)(2,1)} %v0.1), channel_id=1, source_target_pairs={{0,16},{16,0},{1,17},{17,1},{2,18},{18,2},{3,19},{19,3},{4,20},{20... | collective-permute-start | bytes 6291464 | tf_op jit(solution)/shard_map/ppermute | solution.py:373
  1.4 14.1 %collective-permute-start.2 = (bf16[4,256,1024]{2,1,0:T(8,128)(2,1)}, bf16[4,256,1024]{2,1,0:T(8,128)(2,1)}, u32[]{:S(2)}, u32[]{:S(2)}) collective-permute-start(bf16[4,256,1024]{2,1,0:T(8,128)(2,1)} %k0.1), channel_id=1, source_target_pairs={{0,16},{16,0},{1,17},{17,1},{2,18},{18,2},{3,19},{19,3},{4,20},{20... | collective-permute-start | bytes 6291464 | tf_op jit(solution)/shard_map/ppermute | solution.py:373
  2.2 3.1 %collective-permute-start = (bf16[24,512]{1,0:T(8,128)(2,1)S(1)}, bf16[24,512]{1,0:T(8,128)(2,1)S(1)}, u32[]{:S(2)}, u32[]{:S(2)}) collective-permute-start(bf16[24,512]{1,0:T(8,128)(2,1)S(1)} %constant_dynamic-slice_fusion), channel_id=1, source_target_pairs={{0,16},{16,0},{1,17},{17,1},{2,18},{18,2},{3,19},{19,3},{4,20},{20... | collective-permute-start | bytes 73736 | tf_op jit(solution)/shard_map/ppermute | solution.py:373
  3.4 12.1 %copy-start.3 = (s32[4]{0:T(128)S(1)}, s32[4]{0:T(128)}, u32[]{:S(2)}) copy-start(s32[4]{0:T(128)} %pad_add_fusion.me) | copy-start | bytes 52
  7.7 21.9 %all-to-all-start = ((bf16[16,2,48,256]{3,2,1,0:T(8,128)(2,1)}), bf16[16,2,48,256]{3,2,1,0:T(8,128)(2,1)S(1)}, u32[]{:S(2)}, u32[]{:S(2)}) async-start(bf16[16,2,48,256]{3,2,1,0:T(8,128)(2,1)} %spread.1), calls=%async_computation | async-start | bytes 1572864 | tf_op jit(solution)/shard_map/all_to_all | solution.py:399
  15.4 19.6 %copy-start.12 = (s32[12]{0:T(128)S(1)}, s32[12]{0:T(128)}, u32[]{:S(2)}) copy-start(s32[12]{0:T(128)} %param.12) | copy-start | bytes 148
  18.7 16.1 %copy-start.11 = (s32[512]{0:T(512)S(1)}, s32[512]{0:T(512)}, u32[]{:S(2)}) copy-start(s32[512]{0:T(512)} %param.10) | copy-start | bytes 6148
  18.7 16.3 %copy-start.10 = (s32[12,160]{1,0:T(8,128)S(1)}, s32[12,160]{1,0:T(8,128)}, u32[]{:S(2)}) copy-start(s32[12,160]{1,0:T(8,128)} %param.11) | copy-start | bytes 23044
  29.7 8.3 %collective-permute-start.3 = (bf16[16,48,256]{2,1,0:T(8,128)(2,1)S(1)}, bf16[16,48,256]{2,1,0:T(8,128)(2,1)S(1)}, u32[]{:S(2)}, u32[]{:S(2)}) collective-permute-start(bf16[16,48,256]{2,1,0:T(8,128)(2,1)S(1)} %get-tuple-element.32.refs_0_.refs_6_), channel_id=1, source_target_pairs={{0,1},{1,2},{2,3},{3,0},{4,5},{5,6},{6,7},{7,4},{8,9},{9,10},{10,1... | collective-permute-start | bytes 1179656 | tf_op jit(solution)/shard_map/ppermute | solution.py:382
  31.1 12.3 %collective-permute-start.4 = (bf16[16,48,256]{2,1,0:T(8,128)(2,1)S(1)}, bf16[16,48,256]{2,1,0:T(8,128)(2,1)S(1)}, u32[]{:S(2)}, u32[]{:S(2)}) collective-permute-start(bf16[16,48,256]{2,1,0:T(8,128)(2,1)S(1)} %get-tuple-element.32.refs_0_.refs_6_), channel_id=1, source_target_pairs={{0,2},{1,3},{2,0},{3,1},{4,6},{5,7},{6,4},{7,5},{8,10},{9,11},{10,... | collective-permute-start | bytes 1179656 | tf_op jit(solution)/shard_map/ppermute | solution.py:382
  33.7 9.7 %collective-permute-start.5 = (bf16[16,48,256]{2,1,0:T(8,128)(2,1)S(1)}, bf16[16,48,256]{2,1,0:T(8,128)(2,1)S(1)}, u32[]{:S(2)}, u32[]{:S(2)}) collective-permute-start(bf16[16,48,256]{2,1,0:T(8,128)(2,1)S(1)} %get-tuple-element.32.refs_0_.refs_6_), channel_id=1, source_target_pairs={{0,3},{1,0},{2,1},{3,2},{4,7},{5,4},{6,5},{7,6},{8,11},{9,8},{10,9... | collective-permute-start | bytes 1179656 | tf_op jit(solution)/shard_map/ppermute | solution.py:382
  35.4 24.2 %collective-permute-start.9 = (bf16[16,48,256]{2,1,0:T(8,128)(2,1)S(1)}, bf16[16,48,256]{2,1,0:T(8,128)(2,1)S(1)}, u32[]{:S(2)}, u32[]{:S(2)}) collective-permute-start(bf16[16,48,256]{2,1,0:T(8,128)(2,1)S(1)} %get-tuple-element.31.refs_0_), channel_id=1, source_target_pairs={{0,1},{1,2},{2,3},{3,0},{4,5},{5,6},{6,7},{7,4},{8,9},{9,10},{10,1... | collective-permute-start | bytes 1179656 | tf_op jit(solution)/shard_map/ppermute | solution.py:382
  35.9 24.9 %collective-permute-start.10 = (bf16[16,48,256]{2,1,0:T(8,128)(2,1)S(1)}, bf16[16,48,256]{2,1,0:T(8,128)(2,1)S(1)}, u32[]{:S(2)}, u32[]{:S(2)}) collective-permute-start(bf16[16,48,256]{2,1,0:T(8,128)(2,1)S(1)} %get-tuple-element.31.refs_0_), channel_id=1, source_target_pairs={{0,2},{1,3},{2,0},{3,1},{4,6},{5,7},{6,4},{7,5},{8,10},{9,11},{10,... | collective-permute-start | bytes 1179656 | tf_op jit(solution)/shard_map/ppermute | solution.py:382
  38.0 22.8 %collective-permute-start.11 = (bf16[16,48,256]{2,1,0:T(8,128)(2,1)S(1)}, bf16[16,48,256]{2,1,0:T(8,128)(2,1)S(1)}, u32[]{:S(2)}, u32[]{:S(2)}) collective-permute-start(bf16[16,48,256]{2,1,0:T(8,128)(2,1)S(1)} %get-tuple-element.31.refs_0_), channel_id=1, source_target_pairs={{0,3},{1,0},{2,1},{3,2},{4,7},{5,4},{6,5},{7,6},{8,11},{9,8},{10,9... | collective-permute-start | bytes 1179656 | tf_op jit(solution)/shard_map/ppermute | solution.py:382
  59.2 17.0 %collective-permute-start.6 = (bf16[16,56,256]{2,1,0:T(8,128)(2,1)S(1)}, bf16[16,56,256]{2,1,0:T(8,128)(2,1)S(1)}, u32[]{:S(2)}, u32[]{:S(2)}) collective-permute-start(bf16[16,56,256]{2,1,0:T(8,128)(2,1)S(1)} %get-tuple-element.22), channel_id=1, source_target_pairs={{0,3},{1,0},{2,1},{3,2},{4,7},{5,4},{6,5},{7,6},{8,11},{9,8},{10,9... | collective-permute-start | bytes 1376264 | tf_op jit(solution)/shard_map/ppermute | solution.py:382
  59.3 17.7 %collective-permute-start.7 = (bf16[16,56,256]{2,1,0:T(8,128)(2,1)S(1)}, bf16[16,56,256]{2,1,0:T(8,128)(2,1)S(1)}, u32[]{:S(2)}, u32[]{:S(2)}) collective-permute-start(bf16[16,56,256]{2,1,0:T(8,128)(2,1)S(1)} %get-tuple-element.23), channel_id=1, source_target_pairs={{0,2},{1,3},{2,0},{3,1},{4,6},{5,7},{6,4},{7,5},{8,10},{9,11},{10,... | collective-permute-start | bytes 1376264 | tf_op jit(solution)/shard_map/ppermute | solution.py:382
  59.6 17.4 %collective-permute-start.8 = (bf16[16,56,256]{2,1,0:T(8,128)(2,1)S(1)}, bf16[16,56,256]{2,1,0:T(8,128)(2,1)S(1)}, u32[]{:S(2)}, u32[]{:S(2)}) collective-permute-start(bf16[16,56,256]{2,1,0:T(8,128)(2,1)S(1)} %get-tuple-element.24), channel_id=1, source_target_pairs={{0,1},{1,2},{2,3},{3,0},{4,5},{5,6},{6,7},{7,4},{8,9},{9,10},{10,1... | collective-permute-start | bytes 1376264 | tf_op jit(solution)/shard_map/ppermute | solution.py:382
  74.6 10.5 %collective-permute-start.12 = (bf16[16,56,256]{2,1,0:T(8,128)(2,1)}, bf16[16,56,256]{2,1,0:T(8,128)(2,1)S(1)}, u32[]{:S(2)}, u32[]{:S(2)}) collective-permute-start(bf16[16,56,256]{2,1,0:T(8,128)(2,1)} %get-tuple-element.26), channel_id=1, source_target_pairs={{0,3},{1,0},{2,1},{3,2},{4,7},{5,4},{6,5},{7,6},{8,11},{9,8},{10,9... | collective-permute-start | bytes 1376264 | tf_op jit(solution)/shard_map/ppermute | solution.py:382
  74.7 10.4 %collective-permute-start.13 = (bf16[16,56,256]{2,1,0:T(8,128)(2,1)}, bf16[16,56,256]{2,1,0:T(8,128)(2,1)S(1)}, u32[]{:S(2)}, u32[]{:S(2)}) collective-permute-start(bf16[16,56,256]{2,1,0:T(8,128)(2,1)} %get-tuple-element.27), channel_id=1, source_target_pairs={{0,2},{1,3},{2,0},{3,1},{4,6},{5,7},{6,4},{7,5},{8,10},{9,11},{10,... | collective-permute-start | bytes 1376264 | tf_op jit(solution)/shard_map/ppermute | solution.py:382
  76.2 12.9 %collective-permute-start.14 = (bf16[16,56,256]{2,1,0:T(8,128)(2,1)}, bf16[16,56,256]{2,1,0:T(8,128)(2,1)}, u32[]{:S(2)}, u32[]{:S(2)}) collective-permute-start(bf16[16,56,256]{2,1,0:T(8,128)(2,1)} %get-tuple-element.28), channel_id=1, source_target_pairs={{0,1},{1,2},{2,3},{3,0},{4,5},{5,6},{6,7},{7,4},{8,9},{9,10},{10,1... | collective-permute-start | bytes 1376264 | tf_op jit(solution)/shard_map/ppermute | solution.py:382
  78.9 17.7 %all-to-all-start.1 = ((bf16[16,56,256]{2,1,0:T(8,128)(2,1)}), bf16[16,56,256]{2,1,0:T(8,128)(2,1)}, u32[]{:S(2)}, u32[]{:S(2)}) async-start(bf16[16,56,256]{2,1,0:T(8,128)(2,1)} %merge.2), calls=%async_computation.1 | async-start | bytes 917504 | tf_op jit(solution)/shard_map/all_to_all | solution.py:399
  96.6 13.5 %all-to-all-start.2 = ((bf16[16,56,256]{2,1,0:T(8,128)(2,1)}), bf16[16,56,256]{2,1,0:T(8,128)(2,1)S(1)}, u32[]{:S(2)}, u32[]{:S(2)}) async-start(bf16[16,56,256]{2,1,0:T(8,128)(2,1)} %merge.3), calls=%async_computation.2 | async-start | bytes 917504 | tf_op jit(solution)/shard_map/all_to_all | solution.py:399
  113.0 7.4 %collective-permute-start.15 = (bf16[24,512]{1,0:T(8,128)(2,1)}, bf16[24,512]{1,0:T(8,128)(2,1)S(1)}, u32[]{:S(2)}, u32[]{:S(2)}) collective-permute-start(bf16[24,512]{1,0:T(8,128)(2,1)} %get-tuple-element.30), channel_id=1, source_target_pairs={{0,16},{16,0},{1,17},{17,1},{2,18},{18,2},{3,19},{19,3},{4,20},{20... | collective-permute-start | bytes 73736 | tf_op jit(solution)/shard_map/ppermute | solution.py:373
  (8 other events, 10.4 us)
